TPU v7x, 32 devices: a whole 2x2x4 slice. The times are simulated.
32 devices in a mesh: dom: 16 (over z, x, core), sub: 2 (over y).
Axes of the slice: x: 2, y: 2, z: 4, core: 2. Of those that a mesh axis runs over, the one named last changes fastest.
Arguments:
- entity_table: float32 [16384, 256], P(('dom', 'sub')), may hold values from -3 to 3
- entity_state: float32 [16384], P(('dom', 'sub')), may hold values from 0.1 to 1
- relations: float32 [400, 256], replicated, may hold values from -4 to 4
- relation_state: float32 [400], replicated, may hold values from 0.1 to 1
- head_rows: int32 [16, 2, 8192], P('dom', 'sub'), may hold values from 0 to 1023
- tail_rows: int32 [16, 2, 8192], P('dom', 'sub'), may hold values from 0 to 1023
- relation_ids: int32 [16, 2, 8192], P('dom', 'sub'), may hold values from 0 to 399
- negative_rows: int32 [16, 2, 512], P('dom', 'sub'), may hold values from 0 to 1023
- edge_counts: int32 [16, 2], P('dom', 'sub'), may hold values from 1 to 8192, as said below
Outputs:
- new_table: float32 [16384, 256], P(('dom', 'sub'))
- new_state: float32 [16384], P(('dom', 'sub'))
- new_relations: float32 [400, 256], replicated
Inputs may be any that keep to these rules, and one draw needn't show every extreme that they name: `edge_counts`: at least one device has all 8192 slots live.
All inputs are finite; a program needn't handle non-finite values.
Results may differ from a plain program's by a relative error of at most 0.0003.
The roundings to bfloat16 on the way count: a program that leaves them out, or rounds other values in their place, can miss the bound.
Values may be sent and summed in bfloat16 or wider, within the bound.
No kernel may reach another device: no remote copies, remote signals or barrier semaphores. Data moves between devices by JAX's collectives and lax.ppermute only.
A program may use at most 128 MiB of HBM per device.

v0:
```python
import jax
import jax.numpy as jnp
from jax import lax
from jax.sharding import PartitionSpec as P

learn_rate = 0.1
block_count = 4


def partner(x, axis, stride):
    return lax.ppermute(x, axis, [(i, i ^ 1 << stride) for i in range(lax.axis_size(axis))])


def on_device(
    entity_table,
    entity_state,
    relations,
    relation_state,
    head_rows,
    tail_rows,
    relation_ids,
    negative_rows,
    edge_counts,
):
    local_rows = entity_table.astype(jnp.bfloat16)
    pair_bit = lax.axis_size("dom").bit_length() - 2
    own_slab = lax.all_gather(local_rows, "sub", axis=0, tiled=True)
    far_slab = partner(own_slab, "dom", pair_bit)
    slots = head_rows.shape[2]
    heads = head_rows.reshape(slots)
    tails = tail_rows.reshape(slots)
    kinds = relation_ids.reshape(slots)
    negatives = negative_rows.reshape(negative_rows.shape[2])
    negative_table = far_slab[negatives]
    count_here = edge_counts[0, 0]
    valid = (jnp.arange(slots, dtype=jnp.int32) < count_here).astype(jnp.float32)
    width = slots // block_count

    def one_block(carried, inputs):
        head_ids, tail_ids, kind_ids, live = inputs
        head = own_slab[head_ids].astype(jnp.float32)
        tail = far_slab[tail_ids].astype(jnp.float32)
        operator = relations[kind_ids]
        query = head * operator
        query_b = query.astype(jnp.bfloat16)
        positive = jnp.sum(query * tail, axis=-1)
        negative_scores = jnp.dot(query_b, negative_table.T, preferred_element_type=jnp.float32)
        pos_coef = -jax.nn.sigmoid(-positive) * live
        neg_coef = (jax.nn.sigmoid(negative_scores) * (live[:, None] / negatives.shape[0])).astype(
            jnp.bfloat16
        )
        query_grad = pos_coef[:, None] * tail + jnp.dot(
            neg_coef, negative_table, preferred_element_type=jnp.float32
        )
        carried = carried + jnp.dot(neg_coef.T, query_b, preferred_element_type=jnp.float32)
        return (carried, (query_grad * operator, query_grad * head, pos_coef[:, None] * query))

    start_value = jnp.zeros(negative_table.shape, jnp.float32)
    blocked = (
        heads.reshape(block_count, width),
        tails.reshape(block_count, width),
        kinds.reshape(block_count, width),
        valid.reshape(block_count, width),
    )
    negative_grad, outputs = lax.scan(one_block, start_value, blocked)
    dims = relations.shape[1]
    head_grad = outputs[0].reshape(slots, dims)
    operator_grad = outputs[1].reshape(slots, dims)
    tail_grad = outputs[2].reshape(slots, dims)
    rows = own_slab.shape[0]
    own_grad = jax.ops.segment_sum(head_grad, heads, num_segments=rows)
    far_grad = jax.ops.segment_sum(tail_grad, tails, num_segments=rows)
    far_grad = far_grad + jax.ops.segment_sum(negative_grad, negatives, num_segments=rows)
    relation_part = jax.ops.segment_sum(operator_grad, kinds, num_segments=relations.shape[0])
    returned = partner(far_grad, "dom", pair_bit)
    grad = lax.psum_scatter(own_grad + returned, "sub", scatter_dimension=0, tiled=True)
    relation_grad = lax.psum(relation_part, ("dom", "sub"))
    new_state = entity_state + jnp.mean(grad * grad, axis=-1)
    new_table = entity_table - learn_rate * grad / jnp.sqrt(new_state)[:, None]
    relation_total = relation_state + jnp.mean(relation_grad * relation_grad, axis=-1)
    new_relations = relations - learn_rate * relation_grad / jnp.sqrt(relation_total)[:, None]
    return (new_table, new_state, new_relations)


def solution(mesh):
    in_specs = (
        P(("dom", "sub"), None),
        P(("dom", "sub")),
        P(),
        P(),
        P("dom", "sub", None),
        P("dom", "sub", None),
        P("dom", "sub", None),
        P("dom", "sub", None),
        P("dom", "sub"),
    )
    out_specs = (P(("dom", "sub"), None), P(("dom", "sub")), P())
    return jax.shard_map(
        on_device, mesh=mesh, in_specs=in_specs, out_specs=out_specs, check_vma=False
    )
```

profile of v0, /device:TPU:0, one launch (start us, length us, event | category | flops | bytes accessed | tf_op | source)
XLA Modules:
  0.0 455.2 jit_solution(15044035921723715461)
XLA Ops:
  8.1 1.1 convert_element_type.27
  9.2 9.9 %all_gather.3 = bf16[1024,256]{1,0:T(8,128)(2,1)S(1)} all-gather(bf16[512,256]{1,0:T(8,128)(2,1)S(1)} %convert_element_type.27), channel_id=1, replica_groups=mesh['dom'=16,'sub'=2] {'sub'}, dimensions={0}, use_global_device_ids=true | all-gather | bytes 786432 | tf_op jit(solution)/shard_map/all_gather | solution.py:27
  19.1 2.8 collective-permute-start
  22.4 1.5 reduce.10
  24.5 1.5 reduce.11
  26.6 1.5 reduce.9
  30.7 13.6 %collective-permute-done = bf16[1024,256]{1,0:T(8,128)(2,1)S(1)} collective-permute-done((bf16[1024,256]{1,0:T(8,128)(2,1)S(1)}, bf16[1024,256]{1,0:T(8,128)(2,1)S(1)}, u32[]{:S(2)}, u32[]{:S(2)}) %collective-permute-start) | collective-permute-done | bytes 524320 | tf_op jit(solution)/shard_map/ppermute | solution.py:11
  44.3 2.6 gather_fusion.3
  46.9 171.7 %while.17 = (s32[]{:T(128)}, f32[512,256]{1,0:T(8,128)}, f32[4,2048,256]{2,1,0:T(8,128)}, f32[4,2048,256]{2,1,0:T(8,128)}, f32[4,2048,256]{2,1,0:T(8,128)}, /*in...) while((s32[]{:T(128)}, f32[512,256]{1,0:T(8,128)}, ...), condition=%wide.region_2.3_spmd.clone, body=%wide.region_0.2_spmd.clone.sunk | while | flops 1626112000 | bytes 55255824 | solution.py:65
  46.9 1.4 compare_select_fusion.6
  48.9 7.6 %gather_fusion.1 = f32[2048,256]{1,0:T(8,128)S(1)} fusion(f32[400,256]{1,0:T(8,128)S(1)} %get-tuple-element.285, s32[2048]{0:T(1024)} %broadcast_clamp_fusion.7), kind=kCustom, calls=%fused_computation.1.clone.clone.1 | custom fusion | bytes 4202496 | tf_op jit(solution)/shard_map/while/body/eval_jaxpr/gather | solution.py:43
  56.5 1.3 broadcast_clamp_fusion.6
  57.8 9.7 %gather_fusion = bf16[2048,256]{1,0:T(8,128)(2,1)} fusion(bf16[1024,256]{1,0:T(8,128)(2,1)S(1)} %get-tuple-element.289, s32[2048]{0:T(1024)} %broadcast_clamp_fusion.6), kind=kCustom, calls=%fused_computation.2.clone.clone.1 | custom fusion | bytes 2105344 | tf_op jit(solution)/shard_map/while/body/eval_jaxpr/gather | solution.py:42
  67.6 0.8 compare_select_fusion.7
  68.9 9.7 %gather_fusion.2 = bf16[2048,256]{1,0:T(8,128)(2,1)} fusion(bf16[1024,256]{1,0:T(8,128)(2,1)S(1)} %get-tuple-element.283, s32[2048]{0:T(1024)} %broadcast_clamp_fusion.8), kind=kCustom, calls=%fused_computation.clone.clone.1 | custom fusion | bytes 2105344 | tf_op jit(solution)/shard_map/while/body/eval_jaxpr/gather | solution.py:41
  78.7 2.1 fusion.33
  80.7 0.8 constant_dynamic-slice_fusion.2
  81.5 1.6 multiply_convert_fusion.2
  83.1 3.2 fusion.34
  86.4 3.4 convolution_add_fusion.3
  89.7 1.4 compare_select_fusion.6
  91.7 7.6 %gather_fusion.1 = f32[2048,256]{1,0:T(8,128)S(1)} fusion(f32[400,256]{1,0:T(8,128)S(1)} %get-tuple-element.285, s32[2048]{0:T(1024)} %broadcast_clamp_fusion.7), kind=kCustom, calls=%fused_computation.1.clone.clone.1 | custom fusion | bytes 4202496 | tf_op jit(solution)/shard_map/while/body/eval_jaxpr/gather | solution.py:43
  99.4 1.3 broadcast_clamp_fusion.6
  100.6 9.7 %gather_fusion = bf16[2048,256]{1,0:T(8,128)(2,1)} fusion(bf16[1024,256]{1,0:T(8,128)(2,1)S(1)} %get-tuple-element.289, s32[2048]{0:T(1024)} %broadcast_clamp_fusion.6), kind=kCustom, calls=%fused_computation.2.clone.clone.1 | custom fusion | bytes 2105344 | tf_op jit(solution)/shard_map/while/body/eval_jaxpr/gather | solution.py:42
  110.4 0.8 compare_select_fusion.7
  111.8 9.7 %gather_fusion.2 = bf16[2048,256]{1,0:T(8,128)(2,1)} fusion(bf16[1024,256]{1,0:T(8,128)(2,1)S(1)} %get-tuple-element.283, s32[2048]{0:T(1024)} %broadcast_clamp_fusion.8), kind=kCustom, calls=%fused_computation.clone.clone.1 | custom fusion | bytes 2105344 | tf_op jit(solution)/shard_map/while/body/eval_jaxpr/gather | solution.py:41
  121.5 2.1 fusion.33
  123.5 0.8 constant_dynamic-slice_fusion.2
  124.3 1.6 multiply_convert_fusion.2
  125.9 3.3 fusion.34
  129.2 3.5 convolution_add_fusion.3
  132.8 1.4 compare_select_fusion.6
  134.7 7.6 %gather_fusion.1 = f32[2048,256]{1,0:T(8,128)S(1)} fusion(f32[400,256]{1,0:T(8,128)S(1)} %get-tuple-element.285, s32[2048]{0:T(1024)} %broadcast_clamp_fusion.7), kind=kCustom, calls=%fused_computation.1.clone.clone.1 | custom fusion | bytes 4202496 | tf_op jit(solution)/shard_map/while/body/eval_jaxpr/gather | solution.py:43
  142.4 1.3 broadcast_clamp_fusion.6
  143.7 9.7 %gather_fusion = bf16[2048,256]{1,0:T(8,128)(2,1)} fusion(bf16[1024,256]{1,0:T(8,128)(2,1)S(1)} %get-tuple-element.289, s32[2048]{0:T(1024)} %broadcast_clamp_fusion.6), kind=kCustom, calls=%fused_computation.2.clone.clone.1 | custom fusion | bytes 2105344 | tf_op jit(solution)/shard_map/while/body/eval_jaxpr/gather | solution.py:42
  153.4 0.8 compare_select_fusion.7
  154.8 9.7 %gather_fusion.2 = bf16[2048,256]{1,0:T(8,128)(2,1)} fusion(bf16[1024,256]{1,0:T(8,128)(2,1)S(1)} %get-tuple-element.283, s32[2048]{0:T(1024)} %broadcast_clamp_fusion.8), kind=kCustom, calls=%fused_computation.clone.clone.1 | custom fusion | bytes 2105344 | tf_op jit(solution)/shard_map/while/body/eval_jaxpr/gather | solution.py:41
  164.5 2.1 fusion.33
  166.5 0.8 constant_dynamic-slice_fusion.2
  167.4 1.5 multiply_convert_fusion.2
  168.9 3.3 fusion.34
  172.2 3.5 convolution_add_fusion.3
  175.7 1.4 compare_select_fusion.6
  177.7 7.6 %gather_fusion.1 = f32[2048,256]{1,0:T(8,128)S(1)} fusion(f32[400,256]{1,0:T(8,128)S(1)} %get-tuple-element.285, s32[2048]{0:T(1024)} %broadcast_clamp_fusion.7), kind=kCustom, calls=%fused_computation.1.clone.clone.1 | custom fusion | bytes 4202496 | tf_op jit(solution)/shard_map/while/body/eval_jaxpr/gather | solution.py:43
  185.3 1.3 broadcast_clamp_fusion.6
  186.6 9.7 %gather_fusion = bf16[2048,256]{1,0:T(8,128)(2,1)} fusion(bf16[1024,256]{1,0:T(8,128)(2,1)S(1)} %get-tuple-element.289, s32[2048]{0:T(1024)} %broadcast_clamp_fusion.6), kind=kCustom, calls=%fused_computation.2.clone.clone.1 | custom fusion | bytes 2105344 | tf_op jit(solution)/shard_map/while/body/eval_jaxpr/gather | solution.py:42
  196.4 0.8 compare_select_fusion.7
  197.7 9.7 %gather_fusion.2 = bf16[2048,256]{1,0:T(8,128)(2,1)} fusion(bf16[1024,256]{1,0:T(8,128)(2,1)S(1)} %get-tuple-element.283, s32[2048]{0:T(1024)} %broadcast_clamp_fusion.8), kind=kCustom, calls=%fused_computation.clone.clone.1 | custom fusion | bytes 2105344 | tf_op jit(solution)/shard_map/while/body/eval_jaxpr/gather | solution.py:41
  207.5 2.1 fusion.33
  209.5 0.8 constant_dynamic-slice_fusion.2
  210.3 1.6 multiply_convert_fusion.2
  211.9 3.2 fusion.34
  215.1 3.5 convolution_add_fusion.3
  218.7 44.9 %scatter_custom_fusion = f32[1024,256]{1,0:T(8,128)S(1)} fusion(s32[8192]{0:T(1024)} %bitcast.64, f32[8192,256]{1,0:T(8,128)} %bitcast.69, f32[]{:T(128)} %constant.22.clone.1), kind=kCustom, calls=%fused_computation.35 | custom fusion | flops 2097152 | bytes 1049088 | tf_op jit(solution)/shard_map/scatter-add | solution.py:72
  263.5 4.2 scatter_custom_fusion.1
  268.0 45.3 %scatter_custom_fusion.3 = f32[400,256]{1,0:T(8,128)} fusion(s32[8192]{0:T(1024)} %bitcast.65, f32[8192,256]{1,0:T(8,128)} %bitcast.68, f32[]{:T(128)} %constant.22.clone.1), kind=kCustom, calls=%fused_computation.39 | custom fusion | flops 2097152 | bytes 410112 | tf_op jit(solution)/shard_map/scatter-add | solution.py:74
  313.4 2.0 collective-permute-done.1
  315.4 45.0 %scatter_fusion = f32[1024,256]{1,0:T(8,128)S(1)} fusion(f32[1024,256]{1,0:T(8,128)S(1)} %collective-permute-done.1, s32[8192]{0:T(1024)} %bitcast.63, f32[8192,256]{1,0:T(8,128)} %bitcast.58), kind=kCustom, calls=%fused_computation.6 | custom fusion | flops 2097152 | bytes 25198592 | tf_op jit(solution)/shard_map/scatter-add | solution.py:71
  360.5 1.0 copy-done.1
  361.5 79.5 %all-reduce.2.cloned.1.call-done = f32[400,256]{1,0:T(8,128)} async-done(((f32[400,256]{1,0:T(8,128)}), f32[400,256]{1,0:T(8,128)}) %all-reduce.2.cloned.1.call-update) | async-done | bytes 409616 | tf_op jit(solution)/shard_map/psum | solution.py:77
  440.9 1.1 multiply_reduce_fusion.1
  442.1 1.9 divide_subtract_fusion.1
  444.0 1.2 multiply_reduce_fusion
  445.8 2.0 divide_subtract_fusion
  (73 shorter events, 9.5 us)
Async XLA Ops:
  8.0 38.9 %copy-start = (f32[400,256]{1,0:T(8,128)S(1)}, f32[400,256]{1,0:T(8,128)}, u32[]{:S(2)}) copy-start(f32[400,256]{1,0:T(8,128)} %param.13) | copy-start | bytes 1228804
  8.0 432.9 %all-reduce.2.cloned.1.call-start = ((), (), s32[]{:S(2)}) async-start(), calls=%async_computation.2 | async-start | bytes 819200 | tf_op jit(solution)/shard_map/psum | solution.py:77
  19.1 25.2 %collective-permute-start = (bf16[1024,256]{1,0:T(8,128)(2,1)S(1)}, bf16[1024,256]{1,0:T(8,128)(2,1)S(1)}, u32[]{:S(2)}, u32[]{:S(2)}) collective-permute-start(bf16[1024,256]{1,0:T(8,128)(2,1)S(1)} %all_gather.3), channel_id=1, source_target_pairs={{0,16},{2,18},{4,20},{6,22},{8,24},{10,26},{12,28},{14,30},{16,0},... | collective-permute-start | bytes 1572872 | tf_op jit(solution)/shard_map/ppermute | solution.py:11
  78.6 2.9 copy-start.2
  78.6 2.9 copy-start.5
  81.5 1.6 copy-start.3
  83.1 3.3 copy-start.4
  121.5 2.9 copy-start.2
  121.5 2.9 copy-start.5
  124.3 1.6 copy-start.3
  125.9 3.3 copy-start.4
  164.5 2.9 copy-start.2
  164.5 2.9 copy-start.5
  167.3 1.6 copy-start.3
  168.9 3.3 copy-start.4
  207.4 2.9 copy-start.2
  207.4 2.9 copy-start.5
  210.3 1.6 copy-start.3
  211.9 3.2 copy-start.4
  267.9 47.5 %collective-permute-start.1 = (f32[1024,256]{1,0:T(8,128)S(1)}, f32[1024,256]{1,0:T(8,128)S(1)}, u32[]{:S(2)}, u32[]{:S(2)}) collective-permute-start(f32[1024,256]{1,0:T(8,128)S(1)} %add.88), channel_id=1, source_target_pairs={{0,16},{2,18},{4,20},{6,22},{8,24},{10,26},{12,28},{14,30},{16,0},... | collective-permute-start | bytes 3145736 | tf_op jit(solution)/shard_map/ppermute | solution.py:11
  313.3 130.6 %reduce-scatter.2.cloned.1.call-start = ((), (), s32[]{:S(2)}) async-start(), calls=%async_computation.1 | async-start | bytes 1572864 | tf_op jit(solution)/shard_map/reduce_scatter | solution.py:76
  315.4 126.6 %copy-start.7 = (f32[400]{0:T(512)S(1)}, f32[400]{0:T(512)}, u32[]{:S(2)}) copy-start(f32[400]{0:T(512)} %param.14) | copy-start | bytes 4804
  315.4 129.7 %copy-start.8 = (f32[512]{0:T(512)S(1)}, f32[512]{0:T(512)}, u32[]{:S(2)}) copy-start(f32[512]{0:T(512)} %param.12) | copy-start | bytes 6148
  315.4 130.3 %copy-start.6 = (f32[512,256]{1,0:T(8,128)S(1)}, f32[512,256]{1,0:T(8,128)}, u32[]{:S(2)}) copy-start(f32[512,256]{1,0:T(8,128)} %param.11) | copy-start | bytes 1572868
  360.4 1.0 copy-start.1
Sparse Core Ops, SparseCore 0:
  313.5 127.4 all-reduce.1
Sparse Core Ops, SparseCore 1:
  361.5 19.9 reduce-scatter.1
where the time goes:
time: 459 us; the launch traced here: 455 us
  other arithmetic  180 us (39%)
  local copies, waits for them, and re-layouts  117 us (25%)
  waiting for transfers between devices  95.2 us (21%)
  matrix products  33.2 us (7%)
  between operations  16.2 us (4%)
  blocking collectives  9.94 us (2%)
    psum x1, waiting for transfers between devices, on_device(): relation_grad = lax.psum(relation_part, ('dom', 'sub'))  79.5 us
    scatter-add x1, other arithmetic, on_device(): jax.ops.segment_sum(operator_grad, kinds, num_segments=relations.shape[0])  45.3 us
    scatter-add x1, other arithmetic, on_device(): own_grad = jax.ops.segment_sum(head_grad, heads, num_segments=rows)  45 us
    scatter-add x1, other arithmetic, on_device(): far_grad = jax.ops.segment_sum(tail_grad, tails, num_segments=rows)  44.9 us
    gather x4, local copies, waits for them, and re-layouts, one_block(): tail = far_slab[tail_ids].astype(jnp.float32)  38.9 us
    gather x4, local copies, waits for them, and re-layouts, one_block(): head = own_slab[head_ids].astype(jnp.float32)  38.8 us
    gather x4, local copies, waits for them, and re-layouts, one_block(): operator = relations[kind_ids]  30.4 us
    ppermute x2, waiting for transfers between devices, partner(): lax.ppermute(x, axis, [(i, i ^ 1 << stride) for i in range(lax.axis_size(...  15.7 us
  transfers between devices with their start and end apart: 4, of which 3 were waited for; matrix products, arithmetic and copies ran while one was open for 22% of the time, Pallas kernels for 0%

commit v1 on v0

v1 whole, which is shorter than its diff:
```python
import functools

import jax
import jax.numpy as jnp
from jax import lax
from jax.experimental import pallas as pl
from jax.experimental.pallas import tpu as pltpu
from jax.sharding import PartitionSpec as P

learn_rate = 0.1
block = 512
bf16 = jnp.bfloat16
f32 = jnp.float32
vmem_bytes = 56 * 2**20


def dot(a, b):
    return jnp.dot(a, b, preferred_element_type=f32)


def dot_nt(a, b):
    return lax.dot_general(a, b, (((1,), (1,)), ((), ())), preferred_element_type=f32)


def one_hot(ids, rows):
    places = lax.broadcasted_iota(jnp.int16, (rows, ids.shape[1]), 0)
    return jnp.where(places == ids.astype(jnp.int16), jnp.ones((), bf16), jnp.zeros((), bf16))


def split(x):
    high = x.astype(bf16)
    return high, (x - high.astype(f32)).astype(bf16)


def gather_t(pieces, hot):
    rows = pieces[0].shape[1]
    total = dot(pieces[0][...], hot[:rows])
    for k in range(1, len(pieces)):
        total = total + dot(pieces[k][...], hot[k * rows : (k + 1) * rows])
    return total


def scatter_add(pieces, hot, values):
    rows = pieces[0].shape[0]
    for k, piece in enumerate(pieces):
        part = hot[k * rows : (k + 1) * rows]
        total = dot_nt(part, values[0])
        for value in values[1:]:
            total = total + dot_nt(part, value)
        piece[...] += total


def query_kernel(n, rel_rows, source, place, live, codes, ids, relations, *refs):
    slab, (head_out, operator_out), (rel_full, rel_split) = refs[:n], refs[n : n + 2], refs[n + 2 :]
    dims = relations.shape[1]

    @pl.when(pl.program_id(0) == 0)
    def _():
        rel_full[...] = jnp.zeros_like(rel_full)
        rel_full[: relations.shape[0], :] = relations[...]
        high, low = split(rel_full[...].T)
        rel_split[:dims, :] = high
        rel_split[dims:, :] = low

    @pl.when(pl.program_id(0) < codes[2])
    def _():
        rows = slab[0].shape[1]
        head = gather_t(slab, one_hot(ids[0, 0:1, :] ^ codes[0], n * rows))
        both = dot(rel_split[...], one_hot(ids[0, 2:3, :], rel_rows))
        head_out[0] = head.astype(bf16)
        operator_out[0] = both[:dims] + both[dims:]


def score_kernel(n, source, place, live, codes, ids, negatives, head_in, operator_in, *refs):
    slab, (head_grad, operator_grad), far = refs[:n], refs[n : n + 2], refs[n + 2 : 2 * n + 2]
    table, table_t, negative_grad = refs[2 * n + 2 :]
    step = pl.program_id(0)
    steps = codes[2]
    rows = slab[0].shape[1]
    here = source[step]
    count = table.shape[0]

    @pl.when(step == 0)
    def _():
        for piece in far:
            piece[...] = jnp.zeros_like(piece)

    @pl.when(pl.program_id(0) < codes[2])
    def _():
        @pl.when((step == 0) | (source[jnp.maximum(step - 1, 0)] != here))
        def _():
            found = gather_t(slab, one_hot(negatives[here] ^ codes[0], n * rows))
            table_t[...] = found.astype(bf16)
            table[...] = found.T.astype(bf16)
            negative_grad[...] = jnp.zeros_like(negative_grad)

        width = ids.shape[2]
        alive = (lax.broadcasted_iota(jnp.int32, (1, width), 1) < live[step]).astype(f32)
        hot = one_hot(ids[0, 1:2, :] ^ codes[0], n * rows)
        tail = gather_t(slab, hot)
        head = head_in[0].astype(f32)
        operator = operator_in[0]
        query = head * operator
        query_b = query.astype(bf16)
        positive = jnp.sum(query * tail, axis=0, keepdims=True)
        scores = dot(table[...], query_b)
        pos_coef = -jax.nn.sigmoid(-positive) * alive
        neg_coef = (jax.nn.sigmoid(scores) * (alive * (1.0 / count))).astype(bf16)
        query_grad = pos_coef * tail + dot(table_t[...], neg_coef)
        negative_grad[...] += dot_nt(neg_coef, query_b)
        head_grad[0, 0], head_grad[0, 1] = split(query_grad * operator)
        operator_grad[0, 0], operator_grad[0, 1] = split(query_grad * head)
        scatter_add(far, hot, split(pos_coef * query))

        @pl.when((step == steps - 1) | (source[jnp.minimum(step + 1, source.shape[0] - 1)] != here))
        def _():
            chosen = one_hot(negatives[here] ^ codes[0], n * rows)
            high, low = split(negative_grad[...])
            for k, piece in enumerate(far):
                part = chosen[k * rows : (k + 1) * rows]
                piece[...] += dot(part, high) + dot(part, low)


def scatter_kernel(n, source, place, live, codes, ids, head_grad, operator_grad, *refs):
    own, relation = refs[:n], refs[n:]
    rows = own[0].shape[0]

    @pl.when(pl.program_id(0) == 0)
    def _():
        for piece in refs:
            piece[...] = jnp.zeros_like(piece)

    @pl.when(pl.program_id(0) < codes[2])
    def _():
        hot = one_hot(ids[0, 0:1, :] ^ codes[0], n * rows)
        scatter_add(own, hot, (head_grad[0, 0], head_grad[0, 1]))
        rel_rows = len(relation) * relation[0].shape[0]
        hot = one_hot(ids[0, 2:3, :] ^ codes[1], rel_rows)
        scatter_add(relation, hot, (operator_grad[0, 0], operator_grad[0, 1]))


def relation_kernel(code, relations, state, *refs):
    pieces, out, grad = refs[:-2], refs[-2], refs[-1]
    rows = pieces[0].shape[0]
    for k, piece in enumerate(pieces):
        grad[pl.ds(pl.multiple_of((code[0] ^ k) * rows, rows), rows), :] = piece[...]
    g = grad[: relations.shape[0], :]
    total = state[...] + jnp.mean(g * g, axis=-1, keepdims=True)
    out[...] = relations[...] - learn_rate * g / jnp.sqrt(total)


def exchange(x, axis, mask):
    return lax.ppermute(x, axis, [(i, i ^ mask) for i in range(lax.axis_size(axis))])


def on_device(
    entity_table,
    entity_state,
    relations,
    relation_state,
    head_rows,
    tail_rows,
    relation_ids,
    negative_rows,
    edge_counts,
):
    n = lax.axis_size("sub")
    n_dom = lax.axis_size("dom")
    me_sub = lax.axis_index("sub")
    me_dom = lax.axis_index("dom")
    pair = n_dom // 2
    rows, dims = entity_table.shape
    slots = head_rows.shape[2]
    count = negative_rows.shape[2]
    per_source = slots // block
    rel_rows = -(-relations.shape[0] // 256) * 256
    near = min(4, n_dom)
    plane = near * n
    chunk = rel_rows // plane

    local = entity_table.T.astype(bf16)
    own_slab = [local] + [exchange(local, "sub", k) for k in range(1, n)]
    far_first = exchange(local, "dom", pair)
    far_slab = [far_first] + [exchange(far_first, "sub", k) for k in range(1, n)]
    ids = jnp.stack(
        [x.reshape(per_source, block) for x in (head_rows, tail_rows, relation_ids)], axis=1
    )
    small = jnp.concatenate([negative_rows.reshape(1, count), jnp.broadcast_to(edge_counts, (1, 128))], axis=1)
    all_ids = jnp.concatenate([ids] + [exchange(ids, "sub", k) for k in range(1, n)], axis=0)
    all_small = jnp.stack([small] + [exchange(small, "sub", k) for k in range(1, n)], axis=0)
    negatives = all_small[:, :, :count]
    counts = all_small[:, 0, count]

    spots = jnp.arange(n, dtype=jnp.int32)
    blocks = (counts + (block - 1)) // block
    before = jnp.sum(
        jnp.where((spots[None, :] ^ me_sub) < (spots[:, None] ^ me_sub), blocks[None, :], 0), axis=1
    )
    total = jnp.sum(blocks)
    low = me_sub * total // n
    high = (me_sub + 1) * total // n
    line = jnp.minimum(low + jnp.arange(per_source, dtype=jnp.int32), high - 1)
    inside = (line[:, None] >= before[None, :]) & (line[:, None] < (before + blocks)[None, :])
    source = jnp.sum(jnp.where(inside, spots[None, :], 0), axis=1)
    nth = jnp.sum(jnp.where(inside, line[:, None] - before[None, :], 0), axis=1)
    live = jnp.clip(
        jnp.sum(jnp.where(inside, counts[None, :], 0), axis=1) - nth * block, 0, block
    )
    steps = high - low
    place = source * per_source + nth
    near_code = (me_dom % near) * n + me_sub
    codes = jnp.stack([me_sub * rows, near_code * chunk, steps]).astype(jnp.int32)
    tables = (source, place, live, codes)

    params = pltpu.CompilerParams(vmem_limit_bytes=vmem_bytes)
    id_spec = pl.BlockSpec((1, 3, block), lambda i, s, p, l, c: (p[i], 0, 0))

    def whole(shape):
        return pl.BlockSpec(shape, lambda i, s, p, l, c: (0,) * len(shape))

    def stepped(*shape):
        return pl.BlockSpec((1, *shape), lambda i, s, p, l, c: (jnp.minimum(i, c[2] - 1),) + (0,) * len(shape))

    slab_specs = [whole((dims, rows))] * n
    sums = [jax.ShapeDtypeStruct((rows, dims), f32)] * n
    edge_work = per_source * block * dims
    head, operator = pl.pallas_call(
        functools.partial(query_kernel, n, rel_rows),
        grid_spec=pltpu.PrefetchScalarGridSpec(
            num_scalar_prefetch=4,
            grid=(per_source,),
            in_specs=[id_spec, whole(relations.shape), *slab_specs],
            out_specs=[stepped(dims, block), stepped(dims, block)],
            scratch_shapes=[pltpu.VMEM((rel_rows, dims), f32), pltpu.VMEM((2 * dims, rel_rows), bf16)],
        ),
        out_shape=[
            jax.ShapeDtypeStruct((per_source, dims, block), bf16),
            jax.ShapeDtypeStruct((per_source, dims, block), f32),
        ],
        compiler_params=params,
        cost_estimate=pl.CostEstimate(
            flops=2 * edge_work * (n * rows + 2 * rel_rows), bytes_accessed=6 * edge_work, transcendentals=0
        ),
        name="query_kernel",
    )(*tables, all_ids, relations, *own_slab)

    head_grad, operator_grad, *far_sum = pl.pallas_call(
        functools.partial(score_kernel, n),
        grid_spec=pltpu.PrefetchScalarGridSpec(
            num_scalar_prefetch=4,
            grid=(per_source,),
            in_specs=[
                id_spec,
                whole(negatives.shape),
                stepped(dims, block),
                stepped(dims, block),
                *slab_specs,
            ],
            out_specs=[stepped(2, dims, block), stepped(2, dims, block)] + [whole((rows, dims))] * n,
            scratch_shapes=[
                pltpu.VMEM((count, dims), bf16),
                pltpu.VMEM((dims, count), bf16),
                pltpu.VMEM((count, dims), f32),
            ],
        ),
        out_shape=[jax.ShapeDtypeStruct((per_source, 2, dims, block), bf16)] * 2 + sums,
        compiler_params=params,
        cost_estimate=pl.CostEstimate(
            flops=2 * edge_work * 3 * (n * rows + count), bytes_accessed=14 * edge_work, transcendentals=0
        ),
        name="score_kernel",
    )(*tables, all_ids, negatives, head, operator, *far_slab)

    far_total = far_sum[0]
    for k in range(1, n):
        far_total = far_total + exchange(far_sum[k], "sub", k)
    returned = exchange(far_total, "dom", pair)

    scattered = pl.pallas_call(
        functools.partial(scatter_kernel, n),
        grid_spec=pltpu.PrefetchScalarGridSpec(
            num_scalar_prefetch=4,
            grid=(per_source,),
            in_specs=[id_spec, stepped(2, dims, block), stepped(2, dims, block)],
            out_specs=[whole((rows, dims))] * n + [whole((chunk, dims))] * plane,
        ),
        out_shape=sums + [jax.ShapeDtypeStruct((chunk, dims), f32)] * plane,
        compiler_params=params,
        cost_estimate=pl.CostEstimate(
            flops=4 * edge_work * (n * rows + rel_rows), bytes_accessed=8 * edge_work, transcendentals=0
        ),
        name="scatter_kernel",
    )(*tables, all_ids, head_grad, operator_grad)
    own_sum, relation_sum = scattered[:n], scattered[n:]

    own_total = own_sum[0]
    for k in range(1, n):
        own_total = own_total + exchange(own_sum[k], "sub", k)

    def to_plane(x, mask):
        pairs = []
        for d in range(n_dom):
            for s in range(n):
                pairs.append((d * n + s, (d ^ (mask // n)) * n + (s ^ (mask % n))))
        return lax.ppermute(x, ("dom", "sub"), pairs)

    chunk_total = relation_sum[0]
    for k in range(1, plane):
        chunk_total = chunk_total + to_plane(relation_sum[k], k)
    mask = near
    while mask < n_dom:
        chunk_total = chunk_total + exchange(chunk_total, "dom", mask)
        mask *= 2
    chunks = [chunk_total] + [to_plane(chunk_total, k) for k in range(1, plane)]
    new_relations = pl.pallas_call(
        relation_kernel,
        in_specs=[pl.BlockSpec(memory_space=pltpu.SMEM)] + [pl.BlockSpec(memory_space=pltpu.VMEM)] * (2 + plane),
        out_shape=jax.ShapeDtypeStruct(relations.shape, f32),
        scratch_shapes=[pltpu.VMEM((rel_rows, dims), f32)],
        compiler_params=params,
        name="relation_kernel",
    )(near_code.reshape(1).astype(jnp.int32), relations, relation_state.reshape(-1, 1), *chunks)

    grad = own_total + returned
    new_state = entity_state + jnp.mean(grad * grad, axis=-1)
    new_table = entity_table - learn_rate * grad / jnp.sqrt(new_state)[:, None]
    return (new_table, new_state, new_relations)


def solution(mesh):
    in_specs = (
        P(("dom", "sub"), None),
        P(("dom", "sub")),
        P(),
        P(),
        P("dom", "sub", None),
        P("dom", "sub", None),
        P("dom", "sub", None),
        P("dom", "sub", None),
        P("dom", "sub"),
    )
    out_specs = (P(("dom", "sub"), None), P(("dom", "sub")), P())
    return jax.shard_map(
        on_device, mesh=mesh, in_specs=in_specs, out_specs=out_specs, check_vma=False
    )
```

time: 459 us -> 135 us (0.29); the launches traced: 455 us -> 136 us
  other arithmetic: 180 us -> 10.1 us
  local copies, waits for them, and re-layouts: 117 us -> 4.71 us
  waiting for transfers between devices: 95.2 us -> 16.1 us
  starting transfers between devices: 2.98 us -> 68.6 us
  Pallas kernels: 0 us -> 34.2 us
  matrix products: 33.2 us -> 0 us
  between operations: 16.2 us -> 2.79 us
  blocking collectives: 9.94 us -> 0 us
    scatter-add x4 -> x0, other arithmetic: 139 us -> none  [the longest x1 45.3 us: on_device(): jax.ops.segment_sum(operator_grad, kinds, num_segments=relations.shape[0])]
    gather x13 -> x0, local copies, waits for them, and re-layouts: 111 us -> none  [the longest x4 38.9 us: one_block(): tail = far_slab[tail_ids].astype(jnp.float32)]
    psum x1 -> x0, waiting for transfers between devices: 79.5 us -> none  [on_device(): relation_grad = lax.psum(relation_part, ('dom', 'sub'))]
    ppermute x2 -> x24, starting transfers between devices: 2.89 us -> 68.6 us  [the longest x10 56.6 us: exchange(): lax.ppermute(x, axis, [(i, i ^ mask) for i in range(lax.axis_size(axis))])]
    pallas_call x0 -> x4, Pallas kernels: none -> 34.2 us  [the longest x1 12.9 us: on_device(): pl.pallas_call(functools.partial(score_kernel, n), grid_spec=pltpu.Prefet...]
    dot_general x12 -> x0, matrix products: 33.2 us -> none  [the longest x4 14 us: one_block(): jnp.dot(neg_coef.T, query_b, preferred_element_type=jnp.float32)]
    gather x13 -> x0, other arithmetic: 9.95 us -> none  [the longest x4 5.17 us: one_block(): tail = far_slab[tail_ids].astype(jnp.float32)]
    all_gather x1 -> x0, blocking collectives: 9.94 us -> none  [on_device(): own_slab = lax.all_gather(local_rows, 'sub', axis=0, tiled=True)]
  transfers between devices with their start and end apart: 4 -> 24, of which waited for: 3 -> 11; matrix products, arithmetic and copies ran while one was open for 22% -> 6% of each run, Pallas kernels for 0% -> 16%
where the time goes in v1:
time: 135 us; the launch traced here: 136 us
  starting transfers between devices  68.6 us (51%)
  Pallas kernels  34.2 us (25%)
  waiting for transfers between devices  16.1 us (12%)
  other arithmetic  10.1 us (7%)
  local copies, waits for them, and re-layouts  4.71 us (3%)
  between operations  2.79 us (2%)
    ppermute x10, starting transfers between devices, exchange(): lax.ppermute(x, axis, [(i, i ^ mask) for i in range(lax.axis_size(axis))])  56.6 us
    pallas_call x1, Pallas kernels, on_device(): pl.pallas_call(functools.partial(score_kernel, n), grid_spec=pltpu.Prefet...  12.9 us
    pallas_call x1, Pallas kernels, on_device(): pl.pallas_call(functools.partial(scatter_kernel, n), grid_spec=pltpu.Pref...  12.1 us
    ppermute x14, starting transfers between devices, to_plane(): return lax.ppermute(x, ('dom', 'sub'), pairs)  11.9 us
    ppermute x14, waiting for transfers between devices, to_plane(): return lax.ppermute(x, ('dom', 'sub'), pairs)  9.51 us
    pallas_call x1, Pallas kernels, on_device(): pl.pallas_call(functools.partial(query_kernel, n, rel_rows), grid_spec=pl...  6.92 us
    ppermute x10, waiting for transfers between devices, exchange(): lax.ppermute(x, axis, [(i, i ^ mask) for i in range(lax.axis_size(axis))])  6.59 us
    unnamed x35, local copies, waits for them, and re-layouts  3.2 us
  transfers between devices with their start and end apart: 24, of which 11 were waited for; matrix products, arithmetic and copies ran while one was open for 6% of the time, Pallas kernels for 16%

profile of v1, /device:TPU:0, one launch (start us, length us, event | category | flops | bytes accessed | tf_op | source)
XLA Modules:
  0.0 136.5 jit_solution(16453424669846557054)
XLA Ops:
  0.6 1.2 copy.15
  1.8 0.0 copy-start.2
  1.8 3.0 %collective-permute-start.2 = (bf16[256,512]{1,0:T(8,128)(2,1)S(1)}, bf16[256,512]{1,0:T(8,128)(2,1)S(1)}, u32[]{:S(2)}, u32[]{:S(2)}) collective-permute-start(bf16[256,512]{1,0:T(8,128)(2,1)S(1)} %bitcast.17), channel_id=1, source_target_pairs={{0,1},{1,0},{2,3},{3,2},{4,5},{5,4},{6,7},{7,6},{8,9},{9,8},{10,11... | collective-permute-start | bytes 786440 | tf_op jit(solution)/shard_map/ppermute | solution.py:153
  4.9 2.6 %collective-permute-start.3 = (bf16[256,512]{1,0:T(8,128)(2,1)S(1)}, bf16[256,512]{1,0:T(8,128)(2,1)S(1)}, u32[]{:S(2)}, u32[]{:S(2)}) collective-permute-start(bf16[256,512]{1,0:T(8,128)(2,1)S(1)} %bitcast.18), channel_id=1, source_target_pairs={{0,16},{2,18},{4,20},{6,22},{8,24},{10,26},{12,28},{14,30},{16,0},... | collective-permute-start | bytes 786440 | tf_op jit(solution)/shard_map/ppermute | solution.py:153
  8.1 0.7 pad_bitcast_fusion
  8.8 0.5 collective-permute-start
  9.3 0.9 pad_add_fusion.1
  10.2 1.6 %collective-permute-start.1 = (s32[16,3,512]{2,1,0:T(4,128)S(1)}, s32[16,3,512]{2,1,0:T(4,128)S(1)}, u32[]{:S(2)}, u32[]{:S(2)}) collective-permute-start(s32[16,3,512]{2,1,0:T(4,128)S(1)} %pad_add_fusion.1), channel_id=1, source_target_pairs={{0,1},{1,0},{2,3},{3,2},{4,5},{5,4},{6,7},{7,6},{8,9},{9,8},{10,11... | collective-permute-start | bytes 294920 | tf_op jit(solution)/shard_map/ppermute | solution.py:153
  11.8 0.6 collective-permute-done
  12.4 0.1 add_reduce_fusion
  12.5 0.7 fusion.2
  14.5 0.2 fusion
  14.7 0.1 select_reduce_fusion
  14.8 0.6 subtract_clamp_fusion
  15.4 0.6 pad_add_fusion.2.negatives
  16.0 0.6 pad_add_fusion.3.codes
  16.6 0.0 collective-permute-done.1
  16.6 1.6 %pad_add_fusion.ids = s32[32,3,512]{2,1,0:T(4,128)} fusion(s32[16,3,512]{2,1,0:T(4,128)S(1)} %collective-permute-done.1, s32[16,1,512]{2,1,0:T(1,128)} %bitcast.21, s32[16,1,512]{2,1,0:T(1,128)} %bitcast.23, s32[16,1,512]{2,1,0:T(1,128)} %bitcast.25), kind=kLoop, calls=%fused_computation.3 | loop fusion | flops 147456 | bytes 393216 | tf_op jit(solution)/shard_map/concatenate | solution.py:189
  18.2 0.9 collective-permute-done.3.refs_0_
  19.1 0.5 collective-permute-start.4
  19.6 0.0 collective-permute-done.2.refs_1_
  19.6 0.7 copy-done.15
  20.3 6.9 %query_kernel.1 = (bf16[16,256,512]{2,1,0:T(8,128)(2,1)}, f32[16,256,512]{2,1,0:T(8,128)}) custom-call(s32[16]{0:T(128)} %copy-done.12, s32[16]{0:T(128)} %get-tuple-element.45.place, s32[16]{0:T(128)} %get-tuple-element.44.live, s32[3]{0:T(128)} %pad_add_fusion.3.codes, s32[32,3,512]{2,1,0:T(4,128)} %pad_add_fusion.ids, f32[400,256]{1,0:T(8,128)} %relations.3, ...), custom_call_target="tpu_custom_call" | custom-call | flops 8589934592 | bytes 12582912 | tf_op jit(solution)/shard_map/query_kernel/pallas_call | solution.py:227
  27.2 0.0 collective-permute-done.4.refs_1_
  27.3 0.7 copy-done.16
  27.9 12.9 %score_kernel.1 = (bf16[16,2,256,512]{3,2,1,0:T(8,128)(2,1)}, bf16[16,2,256,512]{3,2,1,0:T(8,128)(2,1)}, f32[512,256]{1,0:T(8,128)}, f32[512,256]{1,0:T(8,128)}) custom-call(s32[16]{0:T(128)} %copy-done.12, s32[16]{0:T(128)} %get-tuple-element.45.place, s32[16]{0:T(128)} %get-tuple-element.44.live, s32[3]{0:T(128)} %pad_add_fusion.3.codes, ...), custom_call_target="tpu_custom_call" | custom-call | flops 19327352832 | bytes 29360128 | tf_op jit(solution)/shard_map/score_kernel/pallas_call | solution.py:247
  40.8 5.3 %collective-permute-start.6 = (f32[512,256]{1,0:T(8,128)}, f32[512,256]{1,0:T(8,128)S(1)}, u32[]{:S(2)}, u32[]{:S(2)}) collective-permute-start(f32[512,256]{1,0:T(8,128)} %get-tuple-element.26), channel_id=1, source_target_pairs={{0,1},{1,0},{2,3},{3,2},{4,5},{5,4},{6,7},{7,6},{8,9},{9,8},{10,11... | collective-permute-start | bytes 1572872 | tf_op jit(solution)/shard_map/ppermute | solution.py:153
  46.1 12.1 %scatter_kernel.1 = (f32[512,256]{1,0:T(8,128)}, f32[512,256]{1,0:T(8,128)}, f32[64,256]{1,0:T(8,128)}, f32[64,256]{1,0:T(8,128)}, f32[64,256]{1,0:T(8,128)}, /*...) custom-call(s32[16]{0:T(128)} %copy-done.12, ...), custom_call_target="tpu_custom_call" | custom-call | flops 12884901888 | bytes 16777216 | tf_op jit(solution)/shard_map/scatter_kernel/pallas_call | solution.py:279
  58.3 3.3 %collective-permute-start.10 = (f32[64,256]{1,0:T(8,128)}, f32[64,256]{1,0:T(8,128)S(1)}, u32[]{:S(2)}, u32[]{:S(2)}) collective-permute-start(f32[64,256]{1,0:T(8,128)} %get-tuple-element.30), channel_id=1, source_target_pairs={{0,3},{1,2},{2,1},{3,0},{4,7},{5,6},{6,5},{7,4},{8,11},{9,10},{10,... | collective-permute-start | bytes 196616 | tf_op jit(solution)/shard_map/ppermute | solution.py:305
  61.6 0.0 collective-permute-start.11
  61.6 1.2 collective-permute-start.12
  62.8 0.1 collective-permute-start.13
  62.9 1.4 %collective-permute-done.10 = f32[64,256]{1,0:T(8,128)S(1)} collective-permute-done((f32[64,256]{1,0:T(8,128)}, f32[64,256]{1,0:T(8,128)S(1)}, u32[]{:S(2)}, u32[]{:S(2)}) %collective-permute-start.10) | collective-permute-done | bytes 65568 | tf_op jit(solution)/shard_map/ppermute | solution.py:305
  64.4 1.9 %collective-permute-start.14 = (f32[64,256]{1,0:T(8,128)}, f32[64,256]{1,0:T(8,128)S(1)}, u32[]{:S(2)}, u32[]{:S(2)}) collective-permute-start(f32[64,256]{1,0:T(8,128)} %get-tuple-element.34), channel_id=1, source_target_pairs={{0,7},{1,6},{2,5},{3,4},{4,3},{5,2},{6,1},{7,0},{8,15},{9,14},{10,... | collective-permute-start | bytes 196616 | tf_op jit(solution)/shard_map/ppermute | solution.py:305
  66.3 0.3 collective-permute-start.8
  66.6 0.0 collective-permute-done.6
  66.6 0.0 collective-permute-start.9
  66.6 0.1 add.101
  66.6 0.5 collective-permute-done.12
  67.1 1.8 %collective-permute-start.5 = (f32[512,256]{1,0:T(8,128)}, f32[512,256]{1,0:T(8,128)S(1)}, u32[]{:S(2)}, u32[]{:S(2)}) collective-permute-start(f32[512,256]{1,0:T(8,128)} %get-tuple-element.24), channel_id=1, source_target_pairs={{0,1},{1,0},{2,3},{3,2},{4,5},{5,4},{6,7},{7,6},{8,9},{9,8},{10,11... | collective-permute-start | bytes 1572872 | tf_op jit(solution)/shard_map/ppermute | solution.py:153
  68.9 0.0 collective-permute-done.13
  68.9 5.4 %collective-permute-start.7 = (f32[512,256]{1,0:T(8,128)S(1)}, f32[512,256]{1,0:T(8,128)S(1)}, u32[]{:S(2)}, u32[]{:S(2)}) collective-permute-start(f32[512,256]{1,0:T(8,128)S(1)} %add.101), channel_id=1, source_target_pairs={{0,16},{2,18},{4,20},{6,22},{8,24},{10,26},{12,28},{14,30},{16,0},... | collective-permute-start | bytes 1572872 | tf_op jit(solution)/shard_map/ppermute | solution.py:153
  74.3 0.0 collective-permute-done.8
  74.3 0.9 add_add_fusion.1
  75.2 25.7 %collective-permute-start.15 = (f32[64,256]{1,0:T(8,128)S(1)}, f32[64,256]{1,0:T(8,128)S(1)}, u32[]{:S(2)}, u32[]{:S(2)}) collective-permute-start(f32[64,256]{1,0:T(8,128)S(1)} %add_add_fusion.1), channel_id=1, source_target_pairs={{0,8},{2,10},{4,12},{6,14},{8,0},{10,2},{12,4},{14,6},{16,24},{18,... | collective-permute-start | bytes 196616 | tf_op jit(solution)/shard_map/ppermute | solution.py:153
  100.9 2.2 %collective-permute-done.15 = f32[64,256]{1,0:T(8,128)S(1)} collective-permute-done((f32[64,256]{1,0:T(8,128)S(1)}, f32[64,256]{1,0:T(8,128)S(1)}, u32[]{:S(2)}, u32[]{:S(2)}) %collective-permute-start.15) | collective-permute-done | bytes 65568 | tf_op jit(solution)/shard_map/ppermute | solution.py:153
  103.2 10.2 %collective-permute-start.16 = (f32[64,256]{1,0:T(8,128)S(1)}, f32[64,256]{1,0:T(8,128)S(1)}, u32[]{:S(2)}, u32[]{:S(2)}) collective-permute-start(f32[64,256]{1,0:T(8,128)S(1)} %add.111), channel_id=1, source_target_pairs={{0,16},{2,18},{4,20},{6,22},{8,24},{10,26},{12,28},{14,30},{16,0},... | collective-permute-start | bytes 196616 | tf_op jit(solution)/shard_map/ppermute | solution.py:153
  113.4 2.8 %collective-permute-done.16 = f32[64,256]{1,0:T(8,128)S(1)} collective-permute-done((f32[64,256]{1,0:T(8,128)S(1)}, f32[64,256]{1,0:T(8,128)S(1)}, u32[]{:S(2)}, u32[]{:S(2)}) %collective-permute-start.16) | collective-permute-done | bytes 65568 | tf_op jit(solution)/shard_map/ppermute | solution.py:153
  116.2 1.1 collective-permute-start.17
  117.3 1.1 collective-permute-start.19
  118.4 2.5 %collective-permute-done.17.refs_1_ = f32[64,256]{1,0:T(8,128)S(1)} collective-permute-done((f32[64,256]{1,0:T(8,128)S(1)}, f32[64,256]{1,0:T(8,128)S(1)}, u32[]{:S(2)}, u32[]{:S(2)}) %collective-permute-start.17) | collective-permute-done | bytes 65568 | tf_op jit(solution)/shard_map/ppermute | solution.py:305
  120.9 0.7 collective-permute-start.20
  121.6 1.7 %collective-permute-start.21 = (f32[64,256]{1,0:T(8,128)S(1)}, f32[64,256]{1,0:T(8,128)S(1)}, u32[]{:S(2)}, u32[]{:S(2)}) collective-permute-start(f32[64,256]{1,0:T(8,128)S(1)} %add.112.refs_0_), channel_id=1, source_target_pairs={{0,5},{1,4},{2,7},{3,6},{4,1},{5,0},{6,3},{7,2},{8,13},{9,12},{10,... | collective-permute-start | bytes 196616 | tf_op jit(solution)/shard_map/ppermute | solution.py:305
  123.4 1.8 %collective-permute-done.20.refs_4_ = f32[64,256]{1,0:T(8,128)S(1)} collective-permute-done((f32[64,256]{1,0:T(8,128)S(1)}, f32[64,256]{1,0:T(8,128)S(1)}, u32[]{:S(2)}, u32[]{:S(2)}) %collective-permute-start.20) | collective-permute-done | bytes 65568 | tf_op jit(solution)/shard_map/ppermute | solution.py:305
  125.2 0.4 collective-permute-start.23
  125.6 0.8 copy.16.state
  126.4 0.4 collective-permute-done.21.refs_5_
  126.8 0.4 collective-permute-done.22.refs_6_
  127.3 2.5 %collective-permute-done.23.refs_7_ = f32[64,256]{1,0:T(8,128)S(1)} collective-permute-done((f32[64,256]{1,0:T(8,128)S(1)}, f32[64,256]{1,0:T(8,128)S(1)}, u32[]{:S(2)}, u32[]{:S(2)}) %collective-permute-start.23) | collective-permute-done | bytes 65568 | tf_op jit(solution)/shard_map/ppermute | solution.py:305
  129.8 0.6 copy-done.10
  130.4 2.3 %relation_kernel.1 = f32[400,256]{1,0:T(8,128)} custom-call(s32[1]{0:T(128)} %bitcast.11.code, f32[400,256]{1,0:T(8,128)} %relations.3, f32[400,1]{1,0:T(8,128)} %copy.16.state, f32[64,256]{1,0:T(8,128)} %copy-done.3, f32[64,256]{1,0:T(8,128)} %copy-done.4, f32[64,256]{1,0:T(8,128)} %copy-done.5, f32[64,256]{1,0:T(8,128)} %copy-done.6, f32[64,256]{1,0:T(8,128)} %copy-done.7, ...), custom_call_target="tpu_custom_call" | custom-call | tf_op jit(solution)/shard_map/relation_kernel/pallas_call | solution.py:315
  132.7 1.2 multiply_reduce_fusion
  133.9 0.6 fusion.1
  134.5 2.0 %divide_subtract_fusion = f32[512,256]{1,0:T(8,128)} fusion(f32[512,256]{1,0:T(8,128)S(1)} %copy-done, f32[512]{0:T(512)S(1)} %get-tuple-element.38, f32[512,256]{1,0:T(8,128)S(1)} %collective-permute-done.7, f32[512,256]{1,0:T(8,128)} %get-tuple-element.23, f32[512,256]{1,0:T(8,128)S(1)} %collective-permute-done.5), kind=kLoop, calls=%fused_computation | loop fusion | flops 655360 | bytes 2623488 | tf_op jit(solution)/shard_map/sub | solution.py:326
  (44 shorter events, 0.1 us)
Async XLA Ops:
  1.8 17.8 %copy-start.2 = (bf16[512,256]{0,1:T(8,128)(2,1)}, bf16[512,256]{0,1:T(8,128)(2,1)S(1)}, u32[]{:S(2)}) copy-start(bf16[512,256]{0,1:T(8,128)(2,1)S(1)} %copy.15) | copy-start | bytes 786436
  1.8 17.8 %collective-permute-start.2 = (bf16[256,512]{1,0:T(8,128)(2,1)S(1)}, bf16[256,512]{1,0:T(8,128)(2,1)S(1)}, u32[]{:S(2)}, u32[]{:S(2)}) collective-permute-start(bf16[256,512]{1,0:T(8,128)(2,1)S(1)} %bitcast.17), channel_id=1, source_target_pairs={{0,1},{1,0},{2,3},{3,2},{4,5},{5,4},{6,7},{7,6},{8,9},{9,8},{10,11... | collective-permute-start | bytes 786440 | tf_op jit(solution)/shard_map/ppermute | solution.py:153
  4.9 14.3 %collective-permute-start.3 = (bf16[256,512]{1,0:T(8,128)(2,1)S(1)}, bf16[256,512]{1,0:T(8,128)(2,1)S(1)}, u32[]{:S(2)}, u32[]{:S(2)}) collective-permute-start(bf16[256,512]{1,0:T(8,128)(2,1)S(1)} %bitcast.18), channel_id=1, source_target_pairs={{0,16},{2,18},{4,20},{6,22},{8,24},{10,26},{12,28},{14,30},{16,0},... | collective-permute-start | bytes 786440 | tf_op jit(solution)/shard_map/ppermute | solution.py:153
  8.8 3.6 %collective-permute-start = (s32[1,640]{1,0:T(1,128)S(1)}, s32[1,640]{1,0:T(1,128)S(1)}, u32[]{:S(2)}, u32[]{:S(2)}) collective-permute-start(s32[1,640]{1,0:T(1,128)S(1)} %get-tuple-element.43), channel_id=1, source_target_pairs={{0,1},{1,0},{2,3},{3,2},{4,5},{5,4},{6,7},{7,6},{8,9},{9,8},{10,11... | collective-permute-start | bytes 7688 | tf_op jit(solution)/shard_map/ppermute | solution.py:153
  10.2 6.4 %collective-permute-start.1 = (s32[16,3,512]{2,1,0:T(4,128)S(1)}, s32[16,3,512]{2,1,0:T(4,128)S(1)}, u32[]{:S(2)}, u32[]{:S(2)}) collective-permute-start(s32[16,3,512]{2,1,0:T(4,128)S(1)} %pad_add_fusion.1), channel_id=1, source_target_pairs={{0,1},{1,0},{2,3},{3,2},{4,5},{5,4},{6,7},{7,6},{8,9},{9,8},{10,11... | collective-permute-start | bytes 294920 | tf_op jit(solution)/shard_map/ppermute | solution.py:153
  14.8 4.8 %copy-start.12 = (s32[16]{0:T(128)}, s32[16]{0:T(128)S(1)}, u32[]{:S(2)}) copy-start(s32[16]{0:T(128)S(1)} %get-tuple-element.37.source) | copy-start | bytes 196
  19.1 8.1 %copy-start.14 = (bf16[256,512]{1,0:T(8,128)(2,1)}, bf16[256,512]{1,0:T(8,128)(2,1)S(1)}, u32[]{:S(2)}) copy-start(bf16[256,512]{1,0:T(8,128)(2,1)S(1)} %collective-permute-done.3.refs_0_) | copy-start | bytes 786436
  19.1 8.1 %collective-permute-start.4 = (bf16[256,512]{1,0:T(8,128)(2,1)S(1)}, bf16[256,512]{1,0:T(8,128)(2,1)S(1)}, u32[]{:S(2)}, u32[]{:S(2)}) collective-permute-start(bf16[256,512]{1,0:T(8,128)(2,1)S(1)} %collective-permute-done.3.refs_0_), channel_id=1, source_target_pairs={{0,1},{1,0},{2,3},{3,2},{4,5},{5,4},{6,7},{7,6},{8,9},{9,8},{10,11... | collective-permute-start | bytes 786440 | tf_op jit(solution)/shard_map/ppermute | solution.py:153
  19.6 0.7 copy-start.15
  27.2 0.7 copy-start.16
  40.8 25.8 %collective-permute-start.6 = (f32[512,256]{1,0:T(8,128)}, f32[512,256]{1,0:T(8,128)S(1)}, u32[]{:S(2)}, u32[]{:S(2)}) collective-permute-start(f32[512,256]{1,0:T(8,128)} %get-tuple-element.26), channel_id=1, source_target_pairs={{0,1},{1,0},{2,3},{3,2},{4,5},{5,4},{6,7},{7,6},{8,9},{9,8},{10,11... | collective-permute-start | bytes 1572872 | tf_op jit(solution)/shard_map/ppermute | solution.py:153
  46.1 20.4 %copy-start.1 = (f32[512,256]{1,0:T(8,128)S(1)}, f32[512,256]{1,0:T(8,128)}, u32[]{:S(2)}) copy-start(f32[512,256]{1,0:T(8,128)} %get-tuple-element.25) | copy-start | bytes 1572868
  46.1 79.5 %copy-start.11 = (f32[400]{0:T(512)S(1)}, f32[400]{0:T(512)}, u32[]{:S(2)}) copy-start(f32[400]{0:T(512)} %param.12) | copy-start | bytes 4804
  46.1 87.8 %copy-start.13 = (f32[512]{0:T(512)S(1)}, f32[512]{0:T(512)}, u32[]{:S(2)}) copy-start(f32[512]{0:T(512)} %param.10) | copy-start | bytes 6148
  46.1 88.3 %copy-start = (f32[512,256]{1,0:T(8,128)S(1)}, f32[512,256]{1,0:T(8,128)}, u32[]{:S(2)}) copy-start(f32[512,256]{1,0:T(8,128)} %param.9) | copy-start | bytes 1572868
  58.3 6.1 %collective-permute-start.10 = (f32[64,256]{1,0:T(8,128)}, f32[64,256]{1,0:T(8,128)S(1)}, u32[]{:S(2)}, u32[]{:S(2)}) collective-permute-start(f32[64,256]{1,0:T(8,128)} %get-tuple-element.30), channel_id=1, source_target_pairs={{0,3},{1,2},{2,1},{3,0},{4,7},{5,6},{6,5},{7,4},{8,11},{9,10},{10,... | collective-permute-start | bytes 196616 | tf_op jit(solution)/shard_map/ppermute | solution.py:305
  61.6 4.7 %collective-permute-start.11 = (f32[64,256]{1,0:T(8,128)}, f32[64,256]{1,0:T(8,128)S(1)}, u32[]{:S(2)}, u32[]{:S(2)}) collective-permute-start(f32[64,256]{1,0:T(8,128)} %get-tuple-element.31), channel_id=1, source_target_pairs={{0,4},{1,5},{2,6},{3,7},{4,0},{5,1},{6,2},{7,3},{8,12},{9,13},{10,... | collective-permute-start | bytes 196616 | tf_op jit(solution)/shard_map/ppermute | solution.py:305
  61.6 5.5 %collective-permute-start.12 = (f32[64,256]{1,0:T(8,128)}, f32[64,256]{1,0:T(8,128)S(1)}, u32[]{:S(2)}, u32[]{:S(2)}) collective-permute-start(f32[64,256]{1,0:T(8,128)} %get-tuple-element.32), channel_id=1, source_target_pairs={{0,5},{1,4},{2,7},{3,6},{4,1},{5,0},{6,3},{7,2},{8,13},{9,12},{10,... | collective-permute-start | bytes 196616 | tf_op jit(solution)/shard_map/ppermute | solution.py:305
  62.8 6.1 %collective-permute-start.13 = (f32[64,256]{1,0:T(8,128)}, f32[64,256]{1,0:T(8,128)S(1)}, u32[]{:S(2)}, u32[]{:S(2)}) collective-permute-start(f32[64,256]{1,0:T(8,128)} %get-tuple-element.33), channel_id=1, source_target_pairs={{0,6},{1,7},{2,4},{3,5},{4,2},{5,3},{6,0},{7,1},{8,14},{9,15},{10,... | collective-permute-start | bytes 196616 | tf_op jit(solution)/shard_map/ppermute | solution.py:305
  64.4 9.9 %collective-permute-start.14 = (f32[64,256]{1,0:T(8,128)}, f32[64,256]{1,0:T(8,128)S(1)}, u32[]{:S(2)}, u32[]{:S(2)}) collective-permute-start(f32[64,256]{1,0:T(8,128)} %get-tuple-element.34), channel_id=1, source_target_pairs={{0,7},{1,6},{2,5},{3,4},{4,3},{5,2},{6,1},{7,0},{8,15},{9,14},{10,... | collective-permute-start | bytes 196616 | tf_op jit(solution)/shard_map/ppermute | solution.py:305
  66.3 8.0 %collective-permute-start.8 = (f32[64,256]{1,0:T(8,128)}, f32[64,256]{1,0:T(8,128)S(1)}, u32[]{:S(2)}, u32[]{:S(2)}) collective-permute-start(f32[64,256]{1,0:T(8,128)} %get-tuple-element.28), channel_id=1, source_target_pairs={{0,1},{1,0},{2,3},{3,2},{4,5},{5,4},{6,7},{7,6},{8,9},{9,8},{10,11... | collective-permute-start | bytes 196616 | tf_op jit(solution)/shard_map/ppermute | solution.py:305
  66.6 7.8 %collective-permute-start.9 = (f32[64,256]{1,0:T(8,128)}, f32[64,256]{1,0:T(8,128)S(1)}, u32[]{:S(2)}, u32[]{:S(2)}) collective-permute-start(f32[64,256]{1,0:T(8,128)} %get-tuple-element.29), channel_id=1, source_target_pairs={{0,2},{1,3},{2,0},{3,1},{4,6},{5,7},{6,4},{7,5},{8,10},{9,11},{10,... | collective-permute-start | bytes 196616 | tf_op jit(solution)/shard_map/ppermute | solution.py:305
  67.1 65.6 %collective-permute-start.5 = (f32[512,256]{1,0:T(8,128)}, f32[512,256]{1,0:T(8,128)S(1)}, u32[]{:S(2)}, u32[]{:S(2)}) collective-permute-start(f32[512,256]{1,0:T(8,128)} %get-tuple-element.24), channel_id=1, source_target_pairs={{0,1},{1,0},{2,3},{3,2},{4,5},{5,4},{6,7},{7,6},{8,9},{9,8},{10,11... | collective-permute-start | bytes 1572872 | tf_op jit(solution)/shard_map/ppermute | solution.py:153
  68.9 63.7 %collective-permute-start.7 = (f32[512,256]{1,0:T(8,128)S(1)}, f32[512,256]{1,0:T(8,128)S(1)}, u32[]{:S(2)}, u32[]{:S(2)}) collective-permute-start(f32[512,256]{1,0:T(8,128)S(1)} %add.101), channel_id=1, source_target_pairs={{0,16},{2,18},{4,20},{6,22},{8,24},{10,26},{12,28},{14,30},{16,0},... | collective-permute-start | bytes 1572872 | tf_op jit(solution)/shard_map/ppermute | solution.py:153
  75.2 28.0 %collective-permute-start.15 = (f32[64,256]{1,0:T(8,128)S(1)}, f32[64,256]{1,0:T(8,128)S(1)}, u32[]{:S(2)}, u32[]{:S(2)}) collective-permute-start(f32[64,256]{1,0:T(8,128)S(1)} %add_add_fusion.1), channel_id=1, source_target_pairs={{0,8},{2,10},{4,12},{6,14},{8,0},{10,2},{12,4},{14,6},{16,24},{18,... | collective-permute-start | bytes 196616 | tf_op jit(solution)/shard_map/ppermute | solution.py:153
  103.2 13.0 %collective-permute-start.16 = (f32[64,256]{1,0:T(8,128)S(1)}, f32[64,256]{1,0:T(8,128)S(1)}, u32[]{:S(2)}, u32[]{:S(2)}) collective-permute-start(f32[64,256]{1,0:T(8,128)S(1)} %add.111), channel_id=1, source_target_pairs={{0,16},{2,18},{4,20},{6,22},{8,24},{10,26},{12,28},{14,30},{16,0},... | collective-permute-start | bytes 196616 | tf_op jit(solution)/shard_map/ppermute | solution.py:153
  116.2 13.5 %copy-start.3 = (f32[64,256]{1,0:T(8,128)}, f32[64,256]{1,0:T(8,128)S(1)}, u32[]{:S(2)}) copy-start(f32[64,256]{1,0:T(8,128)S(1)} %add.112.refs_0_) | copy-start | bytes 196612
  116.2 4.7 %collective-permute-start.17 = (f32[64,256]{1,0:T(8,128)S(1)}, f32[64,256]{1,0:T(8,128)S(1)}, u32[]{:S(2)}, u32[]{:S(2)}) collective-permute-start(f32[64,256]{1,0:T(8,128)S(1)} %add.112.refs_0_), channel_id=1, source_target_pairs={{0,1},{1,0},{2,3},{3,2},{4,5},{5,4},{6,7},{7,6},{8,9},{9,8},{10,11... | collective-permute-start | bytes 196616 | tf_op jit(solution)/shard_map/ppermute | solution.py:305
  117.3 4.3 %collective-permute-start.18 = (f32[64,256]{1,0:T(8,128)S(1)}, f32[64,256]{1,0:T(8,128)S(1)}, u32[]{:S(2)}, u32[]{:S(2)}) collective-permute-start(f32[64,256]{1,0:T(8,128)S(1)} %add.112.refs_0_), channel_id=1, source_target_pairs={{0,2},{1,3},{2,0},{3,1},{4,6},{5,7},{6,4},{7,5},{8,10},{9,11},{10,... | collective-permute-start | bytes 196616 | tf_op jit(solution)/shard_map/ppermute | solution.py:305
  117.3 6.1 %collective-permute-start.19 = (f32[64,256]{1,0:T(8,128)S(1)}, f32[64,256]{1,0:T(8,128)S(1)}, u32[]{:S(2)}, u32[]{:S(2)}) collective-permute-start(f32[64,256]{1,0:T(8,128)S(1)} %add.112.refs_0_), channel_id=1, source_target_pairs={{0,3},{1,2},{2,1},{3,0},{4,7},{5,6},{6,5},{7,4},{8,11},{9,10},{10,... | collective-permute-start | bytes 196616 | tf_op jit(solution)/shard_map/ppermute | solution.py:305
  120.9 8.9 %copy-start.4 = (f32[64,256]{1,0:T(8,128)}, f32[64,256]{1,0:T(8,128)S(1)}, u32[]{:S(2)}) copy-start(f32[64,256]{1,0:T(8,128)S(1)} %collective-permute-done.17.refs_1_) | copy-start | bytes 196612
  120.9 4.3 %collective-permute-start.20 = (f32[64,256]{1,0:T(8,128)S(1)}, f32[64,256]{1,0:T(8,128)S(1)}, u32[]{:S(2)}, u32[]{:S(2)}) collective-permute-start(f32[64,256]{1,0:T(8,128)S(1)} %add.112.refs_0_), channel_id=1, source_target_pairs={{0,4},{1,5},{2,6},{3,7},{4,0},{5,1},{6,2},{7,3},{8,12},{9,13},{10,... | collective-permute-start | bytes 196616 | tf_op jit(solution)/shard_map/ppermute | solution.py:305
  121.6 8.1 %copy-start.5 = (f32[64,256]{1,0:T(8,128)}, f32[64,256]{1,0:T(8,128)S(1)}, u32[]{:S(2)}) copy-start(f32[64,256]{1,0:T(8,128)S(1)} %collective-permute-done.18.refs_2_) | copy-start | bytes 196612
  121.6 5.2 %collective-permute-start.21 = (f32[64,256]{1,0:T(8,128)S(1)}, f32[64,256]{1,0:T(8,128)S(1)}, u32[]{:S(2)}, u32[]{:S(2)}) collective-permute-start(f32[64,256]{1,0:T(8,128)S(1)} %add.112.refs_0_), channel_id=1, source_target_pairs={{0,5},{1,4},{2,7},{3,6},{4,1},{5,0},{6,3},{7,2},{8,13},{9,12},{10,... | collective-permute-start | bytes 196616 | tf_op jit(solution)/shard_map/ppermute | solution.py:305
  123.4 6.4 %copy-start.6 = (f32[64,256]{1,0:T(8,128)}, f32[64,256]{1,0:T(8,128)S(1)}, u32[]{:S(2)}) copy-start(f32[64,256]{1,0:T(8,128)S(1)} %collective-permute-done.19.refs_3_) | copy-start | bytes 196612
  123.4 3.9 %collective-permute-start.22 = (f32[64,256]{1,0:T(8,128)S(1)}, f32[64,256]{1,0:T(8,128)S(1)}, u32[]{:S(2)}, u32[]{:S(2)}) collective-permute-start(f32[64,256]{1,0:T(8,128)S(1)} %add.112.refs_0_), channel_id=1, source_target_pairs={{0,6},{1,7},{2,4},{3,5},{4,2},{5,3},{6,0},{7,1},{8,14},{9,15},{10,... | collective-permute-start | bytes 196616 | tf_op jit(solution)/shard_map/ppermute | solution.py:305
  125.2 4.6 %copy-start.7 = (f32[64,256]{1,0:T(8,128)}, f32[64,256]{1,0:T(8,128)S(1)}, u32[]{:S(2)}) copy-start(f32[64,256]{1,0:T(8,128)S(1)} %collective-permute-done.20.refs_4_) | copy-start | bytes 196612
  125.2 4.6 %collective-permute-start.23 = (f32[64,256]{1,0:T(8,128)S(1)}, f32[64,256]{1,0:T(8,128)S(1)}, u32[]{:S(2)}, u32[]{:S(2)}) collective-permute-start(f32[64,256]{1,0:T(8,128)S(1)} %add.112.refs_0_), channel_id=1, source_target_pairs={{0,7},{1,6},{2,5},{3,4},{4,3},{5,2},{6,1},{7,0},{8,15},{9,14},{10,... | collective-permute-start | bytes 196616 | tf_op jit(solution)/shard_map/ppermute | solution.py:305
  126.8 3.0 %copy-start.8 = (f32[64,256]{1,0:T(8,128)}, f32[64,256]{1,0:T(8,128)S(1)}, u32[]{:S(2)}) copy-start(f32[64,256]{1,0:T(8,128)S(1)} %collective-permute-done.21.refs_5_) | copy-start | bytes 196612
  127.3 2.5 %copy-start.9 = (f32[64,256]{1,0:T(8,128)}, f32[64,256]{1,0:T(8,128)S(1)}, u32[]{:S(2)}) copy-start(f32[64,256]{1,0:T(8,128)S(1)} %collective-permute-done.22.refs_6_) | copy-start | bytes 196612
  129.8 0.6 copy-start.10

commit v2 on v1

v2 whole, which is shorter than its diff:
```python
import functools

import jax
import jax.numpy as jnp
from jax import lax
from jax.experimental import pallas as pl
from jax.experimental.pallas import tpu as pltpu
from jax.sharding import PartitionSpec as P

learn_rate = 0.1
block = 512
bf16 = jnp.bfloat16
f32 = jnp.float32
vmem_bytes = 56 * 2**20


def dot(a, b):
    return jnp.dot(a, b, preferred_element_type=f32)


def dot_nt(a, b):
    return lax.dot_general(a, b, (((1,), (1,)), ((), ())), preferred_element_type=f32)


def one_hot(ids, rows):
    places = lax.broadcasted_iota(jnp.int16, (rows, ids.shape[1]), 0)
    return jnp.where(places == ids.astype(jnp.int16), jnp.ones((), bf16), jnp.zeros((), bf16))


def split(x):
    high = x.astype(bf16)
    return high, (x - high.astype(f32)).astype(bf16)


def gather_t(pieces, hot):
    rows = pieces[0].shape[1]
    total = dot(pieces[0][...], hot[:rows])
    for k in range(1, len(pieces)):
        total = total + dot(pieces[k][...], hot[k * rows : (k + 1) * rows])
    return total


def scatter_add(pieces, hot, values):
    start = 0
    for piece in pieces:
        part = hot[start : start + piece.shape[0]]
        start += piece.shape[0]
        total = dot_nt(part, values[0])
        for value in values[1:]:
            total = total + dot_nt(part, value)
        piece[...] += total


def edge_kernel(n, source, place, live, codes, ids, negatives, relations, *refs):
    near, away = refs[:n], refs[n : 2 * n]
    grad_out, near_sum, away_sum = refs[2 * n], refs[2 * n + 1 : 3 * n + 1], refs[3 * n + 1 : 4 * n + 1]
    relation_sum = refs[4 * n + 1 : -5]
    rel_full, rel_split, table, table_t, negative_grad = refs[-5:]
    step = pl.program_id(0)
    steps = codes[2]
    rows = near[0].shape[1]
    dims = relations.shape[1]
    rel_rows = rel_full.shape[0]
    here = source[step]
    swapped = here >= n
    count = table.shape[0]

    @pl.when(step == 0)
    def _():
        for piece in (*near_sum, *away_sum, *relation_sum):
            piece[...] = jnp.zeros_like(piece)
        rel_full[...] = jnp.zeros_like(rel_full)
        rel_full[: relations.shape[0], :] = relations[...]
        high, low = split(rel_full[...].T)
        rel_split[:dims, :] = high
        rel_split[dims:, :] = low

    def take_table(slab):
        found = gather_t(slab, one_hot(negatives[here] ^ codes[0], n * rows))
        table_t[...] = found.astype(bf16)
        table[...] = found.T.astype(bf16)
        negative_grad[...] = jnp.zeros_like(negative_grad)

    fresh = (step < steps) & ((step == 0) | (source[jnp.maximum(step - 1, 0)] != here))
    pl.when(fresh & ~swapped)(lambda: take_table(away))
    pl.when(fresh & swapped)(lambda: take_table(near))

    @pl.when(step < steps)
    def _():
        width = ids.shape[2]
        entries = ids[0].astype(jnp.int32)
        heads, tails, kinds = entries[0:1], entries[1:2], entries[2:3]
        alive = (lax.broadcasted_iota(jnp.int32, (1, width), 1) < live[step]).astype(f32)
        near_ids = jnp.where(swapped, tails, heads) ^ codes[0]
        away_hot = one_hot(jnp.where(swapped, heads, tails) ^ codes[0], n * rows)
        near_rows = gather_t(near, one_hot(near_ids, n * rows))
        away_rows = gather_t(away, away_hot)
        head = jnp.where(swapped, away_rows, near_rows)
        tail = jnp.where(swapped, near_rows, away_rows)
        both = dot(rel_split[...], one_hot(kinds, rel_rows))
        operator = both[:dims] + both[dims:]
        query = head * operator
        query_b = query.astype(bf16)
        positive = jnp.sum(query * tail, axis=0, keepdims=True)
        scores = dot(table[...], query_b)
        pos_coef = -jax.nn.sigmoid(-positive) * alive
        neg_coef = (jax.nn.sigmoid(scores) * (alive * (1.0 / count))).astype(bf16)
        query_grad = pos_coef * tail + dot(table_t[...], neg_coef)
        negative_grad[...] += dot_nt(neg_coef, query_b)
        head_grad = query_grad * operator
        tail_grad = pos_coef * query
        grad_out[0, 0], grad_out[0, 1] = split(jnp.where(swapped, tail_grad, head_grad))
        scatter_add(away_sum, away_hot, split(jnp.where(swapped, head_grad, tail_grad)))
        scatter_add(relation_sum, one_hot(kinds ^ codes[1], rel_rows), split(query_grad * head))

    def add_negatives(sums):
        chosen = one_hot(negatives[here] ^ codes[0], n * rows)
        high, low = split(negative_grad[...])
        for k, piece in enumerate(sums):
            part = chosen[k * rows : (k + 1) * rows]
            piece[...] += dot(part, high) + dot(part, low)

    final = (step == steps - 1) | ((step < steps) & (source[jnp.minimum(step + 1, steps - 1)] != here))
    pl.when(final & ~swapped)(lambda: add_negatives(away_sum))
    pl.when(final & swapped)(lambda: add_negatives(near_sum))


def near_kernel(n, source, place, live, codes, ids, grads, *refs):
    base, sums = refs[:n], refs[n:]
    rows = sums[0].shape[0]
    step = pl.program_id(0)

    @pl.when(step == 0)
    def _():
        for start, piece in zip(base, sums, strict=True):
            piece[...] = start[...]

    @pl.when(step < codes[2])
    def _():
        entries = ids[0].astype(jnp.int32)
        near_ids = jnp.where(source[step] >= n, entries[1:2], entries[0:1]) ^ codes[0]
        scatter_add(sums, one_hot(near_ids, n * rows), (grads[0, 0], grads[0, 1]))


def entity_kernel(n, table, state, returned, *refs):
    parts, (new_table, new_state) = refs[:n], refs[n:]
    grad = returned[...]
    for part in parts:
        grad = grad + part[...]
    lanes = 128
    before = jnp.broadcast_to(state[...], (lanes, table.shape[0])).T[:, :1]
    after = before + jnp.mean(grad * grad, axis=-1, keepdims=True)
    new_table[...] = table[...] - learn_rate * grad / jnp.sqrt(after)
    new_state[...] = jnp.broadcast_to(after, (table.shape[0], lanes)).T[:1]


def relation_kernel(chunk, code, relations, state, mine, theirs, out, grad):
    chunks = mine.shape[0] // chunk
    for k in range(2 * chunks):
        part = (mine, theirs)[k // chunks]
        start = (k % chunks) * chunk
        grad[pl.ds(pl.multiple_of((code[0] ^ k) * chunk, chunk), chunk), :] = part[start : start + chunk, :]
    g = grad[: relations.shape[0], :]
    total = state[...] + jnp.mean(g * g, axis=-1, keepdims=True)
    out[...] = relations[...] - learn_rate * g / jnp.sqrt(total)


def exchange(x, axis, mask):
    return lax.ppermute(x, axis, [(i, i ^ mask) for i in range(lax.axis_size(axis))])


def on_device(
    entity_table,
    entity_state,
    relations,
    relation_state,
    head_rows,
    tail_rows,
    relation_ids,
    negative_rows,
    edge_counts,
):
    n = lax.axis_size("sub")
    n_dom = lax.axis_size("dom")
    me_sub = lax.axis_index("sub")
    me_dom = lax.axis_index("dom")
    pair = n_dom // 2
    rows, dims = entity_table.shape
    slots = head_rows.shape[2]
    count = negative_rows.shape[2]
    per_source = slots // block
    rel_rows = -(-relations.shape[0] // 256) * 256
    chips = 2 * n
    chunk = rel_rows // (2 * chips)

    local = entity_table.T.astype(bf16)
    away_first = exchange(local, "dom", pair)
    near_slab = [local] + [exchange(local, "sub", k) for k in range(1, n)]
    away_slab = [away_first] + [exchange(away_first, "sub", k) for k in range(1, n)]

    def from_pair(x):
        across = exchange(x, "dom", pair)
        return [x, *(exchange(x, "sub", k) for k in range(1, n)), across, *(exchange(across, "sub", k) for k in range(1, n))]

    ids = jnp.stack(
        [x.reshape(per_source, block) for x in (head_rows, tail_rows, relation_ids)], axis=1
    ).astype(jnp.int16)
    small = jnp.concatenate([negative_rows.reshape(1, count), jnp.broadcast_to(edge_counts, (1, 128))], axis=1)
    all_ids = jnp.concatenate(from_pair(ids), axis=0)
    all_small = jnp.stack(from_pair(small), axis=0)
    negatives = all_small[:, :, :count]
    counts = all_small[:, 0, count]

    team = 2 * n
    me = (me_dom // pair) * n + me_sub
    spots = jnp.arange(team, dtype=jnp.int32)
    blocks = (counts + (block - 1)) // block
    before = jnp.sum(jnp.where((spots[None, :] ^ me) < (spots[:, None] ^ me), blocks[None, :], 0), axis=1)
    total = jnp.sum(blocks)
    low = me * total // team
    high = (me + 1) * total // team
    line = jnp.minimum(low + jnp.arange(per_source, dtype=jnp.int32), high - 1)
    inside = (line[:, None] >= before[None, :]) & (line[:, None] < (before + blocks)[None, :])
    source = jnp.sum(jnp.where(inside, spots[None, :], 0), axis=1)
    nth = jnp.sum(jnp.where(inside, line[:, None] - before[None, :], 0), axis=1)
    live = jnp.clip(
        jnp.sum(jnp.where(inside, counts[None, :], 0), axis=1) - nth * block, 0, block
    )
    place = source * per_source + nth
    chunk_code = (me_dom % 2) * chips + (me_dom // 2 % 2) * n + me_sub
    codes = jnp.stack([me_sub * rows, chunk_code * chunk, high - low]).astype(jnp.int32)
    tables = (source, place, live, codes)

    params = pltpu.CompilerParams(vmem_limit_bytes=vmem_bytes)
    id_spec = pl.BlockSpec((1, 3, block), lambda i, s, p, l, c: (p[i], 0, 0))

    def whole(shape):
        return pl.BlockSpec(shape, lambda i, s, p, l, c: (0,) * len(shape))

    grad_spec = pl.BlockSpec((1, 2, dims, block), lambda i, s, p, l, c: (jnp.minimum(i, c[2] - 1), 0, 0, 0))
    sums = [jax.ShapeDtypeStruct((rows, dims), f32)] * n
    edge_work = per_source * block * dims
    pieces = [(chunk, dims)] * chips + [(chips * chunk, dims)]
    grads, *found = pl.pallas_call(
        functools.partial(edge_kernel, n),
        grid_spec=pltpu.PrefetchScalarGridSpec(
            num_scalar_prefetch=4,
            grid=(per_source,),
            in_specs=[id_spec, whole(negatives.shape), whole(relations.shape)] + [whole((dims, rows))] * team,
            out_specs=[grad_spec] + [whole((rows, dims))] * team + [whole(x) for x in pieces],
            scratch_shapes=[
                pltpu.VMEM((rel_rows, dims), f32),
                pltpu.VMEM((2 * dims, rel_rows), bf16),
                pltpu.VMEM((count, dims), bf16),
                pltpu.VMEM((dims, count), bf16),
                pltpu.VMEM((count, dims), f32),
            ],
        ),
        out_shape=[jax.ShapeDtypeStruct((per_source, 2, dims, block), bf16)]
        + sums * 2
        + [jax.ShapeDtypeStruct(x, f32) for x in pieces],
        compiler_params=params,
        cost_estimate=pl.CostEstimate(
            flops=2 * edge_work * (4 * n * rows + 3 * count + 4 * rel_rows), bytes_accessed=8 * edge_work, transcendentals=0
        ),
        name="edge_kernel",
    )(*tables, all_ids, negatives, relations, *near_slab, *away_slab)
    near_base, away_sum, relation_keep, relation_send = found[:n], found[n:team], found[team:-1], found[-1]

    away_total = away_sum[0]
    for k in range(1, n):
        away_total = away_total + exchange(away_sum[k], "sub", k)
    returned = exchange(away_total, "dom", pair)

    def to_chip(x, mask):
        pairs = []
        for d in range(n_dom):
            for s in range(n):
                pairs.append((d * n + s, (d ^ (mask // n * 2)) * n + (s ^ (mask % n))))
        return lax.ppermute(x, ("dom", "sub"), pairs)

    other_core = exchange(relation_send, "dom", 1)
    parts = [relation_keep[k] + other_core[k * chunk : (k + 1) * chunk] for k in range(chips)]
    chunk_total = parts[0]
    for k in range(1, chips):
        chunk_total = chunk_total + to_chip(parts[k], k)
    mask = 4
    while mask < n_dom:
        chunk_total = chunk_total + exchange(chunk_total, "dom", mask)
        mask *= 2
    mine = jnp.concatenate([chunk_total] + [to_chip(chunk_total, k) for k in range(1, chips)], axis=0)
    theirs = exchange(mine, "dom", 1)

    near_sum = pl.pallas_call(
        functools.partial(near_kernel, n),
        grid_spec=pltpu.PrefetchScalarGridSpec(
            num_scalar_prefetch=4,
            grid=(per_source,),
            in_specs=[id_spec, grad_spec] + [whole((rows, dims))] * n,
            out_specs=[whole((rows, dims))] * n,
        ),
        out_shape=sums,
        compiler_params=params,
        cost_estimate=pl.CostEstimate(
            flops=2 * edge_work * n * rows, bytes_accessed=4 * edge_work, transcendentals=0
        ),
        name="near_kernel",
    )(*tables, all_ids, grads, *near_base)

    in_vmem = pl.BlockSpec(memory_space=pltpu.VMEM)
    new_table, new_state = pl.pallas_call(
        functools.partial(entity_kernel, n),
        in_specs=[in_vmem] * (3 + n),
        out_specs=[in_vmem] * 2,
        out_shape=[jax.ShapeDtypeStruct((rows, dims), f32), jax.ShapeDtypeStruct((1, rows), f32)],
        compiler_params=params,
        name="entity_kernel",
    )(
        entity_table,
        entity_state.reshape(1, rows),
        returned,
        near_sum[0],
        *(exchange(near_sum[k], "sub", k) for k in range(1, n)),
    )
    theirs, new_table, new_state = lax.optimization_barrier((theirs, new_table, new_state))
    new_relations = pl.pallas_call(
        functools.partial(relation_kernel, chunk),
        in_specs=[pl.BlockSpec(memory_space=pltpu.SMEM)] + [in_vmem] * 4,
        out_specs=in_vmem,
        out_shape=jax.ShapeDtypeStruct(relations.shape, f32),
        scratch_shapes=[pltpu.VMEM((rel_rows, dims), f32)],
        compiler_params=params,
        name="relation_kernel",
    )(chunk_code.reshape(1).astype(jnp.int32), relations, relation_state.reshape(-1, 1), mine, theirs)
    return (new_table, new_state.reshape(rows), new_relations)


def solution(mesh):
    in_specs = (
        P(("dom", "sub"), None),
        P(("dom", "sub")),
        P(),
        P(),
        P("dom", "sub", None),
        P("dom", "sub", None),
        P("dom", "sub", None),
        P("dom", "sub", None),
        P("dom", "sub"),
    )
    out_specs = (P(("dom", "sub"), None), P(("dom", "sub")), P())
    return jax.shard_map(
        on_device, mesh=mesh, in_specs=in_specs, out_specs=out_specs, check_vma=False
    )
```

time: 135 us -> 134 us (level); the launches traced: 136 us -> 134 us
  starting transfers between devices: 68.6 us -> 29.2 us
  waiting for transfers between devices: 16.1 us -> 44.5 us
  Pallas kernels: 34.2 us -> 43.8 us
  other arithmetic: 10.1 us -> 8.15 us
    ppermute x10 -> x16, starting transfers between devices: 56.6 us -> 22.1 us  [exchange(): lax.ppermute(x, axis, [(i, i ^ mask) for i in range(lax.axis_size(axis))])]
    ppermute x10 -> x16, waiting for transfers between devices: 6.59 us -> 39.1 us  [exchange(): lax.ppermute(x, axis, [(i, i ^ mask) for i in range(lax.axis_size(axis))])]
    pallas_call x4, Pallas kernels: 34.2 us -> 43.8 us  [the longest x1 29 us: on_device(): pl.pallas_call(functools.partial(edge_kernel, n), grid_spec=pltpu.Prefetc...]
    ppermute x14 -> x6, starting transfers between devices: 11.9 us -> 7.12 us  [to_chip(): return lax.ppermute(x, ('dom', 'sub'), pairs)]
    ppermute x14 -> x6, waiting for transfers between devices: 9.51 us -> 5.34 us  [to_chip(): return lax.ppermute(x, ('dom', 'sub'), pairs)]
    another operation x2 -> x5, other arithmetic: 1.21 us -> 3.5 us  [the longest x1 0.61 us: on_device(): jnp.stack([me_sub * rows, near_code * chunk, steps]).astype(jnp.int32)]
    sub x1 -> x0, other arithmetic: 1.99 us -> none  [on_device(): new_table = entity_table - learn_rate * grad / jnp.sqrt(new_state)[:, None]]
    unnamed x35 -> x23, local copies, waits for them, and re-layouts: 3.2 us -> 3.62 us
  transfers between devices with their start and end apart: 24 -> 22, of which waited for: 11 -> 10; matrix products, arithmetic and copies ran while one was open for 6% -> 7% of each run, Pallas kernels for 16% -> 9%
where the time goes in v2:
time: 134 us
  waiting for transfers between devices  44.5 us (33%)
  Pallas kernels  43.8 us (33%)
  starting transfers between devices  29.2 us (22%)
  other arithmetic  8.15 us (6%)
  local copies, waits for them, and re-layouts  5.14 us (4%)
  between operations  2.81 us (2%)
    ppermute x16, waiting for transfers between devices, exchange(): lax.ppermute(x, axis, [(i, i ^ mask) for i in range(lax.axis_size(axis))])  39.1 us
    pallas_call x1, Pallas kernels, on_device(): pl.pallas_call(functools.partial(edge_kernel, n), grid_spec=pltpu.Prefetc...  29 us
    ppermute x16, starting transfers between devices, exchange(): lax.ppermute(x, axis, [(i, i ^ mask) for i in range(lax.axis_size(axis))])  22.1 us
    pallas_call x1, Pallas kernels, on_device(): pl.pallas_call(functools.partial(near_kernel, n), grid_spec=pltpu.Prefetc...  9.88 us
    ppermute x6, starting transfers between devices, to_chip(): return lax.ppermute(x, ('dom', 'sub'), pairs)  7.12 us
    ppermute x6, waiting for transfers between devices, to_chip(): return lax.ppermute(x, ('dom', 'sub'), pairs)  5.34 us
    unnamed x23, local copies, waits for them, and re-layouts  3.62 us
    pallas_call x1, Pallas kernels, on_device(): pl.pallas_call(functools.partial(entity_kernel, n), in_specs=[in_vmem] *...  2.69 us
  transfers between devices with their start and end apart: 22, of which 10 were waited for; matrix products, arithmetic and copies ran while one was open for 7% of the time, Pallas kernels for 9%

profile of v2, /device:TPU:0, one launch (start us, length us, event | category | flops | bytes accessed | tf_op | source)
XLA Modules:
  0.0 133.6 jit_solution(13746256875555253947)
XLA Ops:
  1.3 0.7 pad_bitcast_fusion
  2.0 4.0 %collective-permute-start.1 = (s32[1,640]{1,0:T(1,128)S(1)}, s32[1,640]{1,0:T(1,128)S(1)}, u32[]{:S(2)}, u32[]{:S(2)}) collective-permute-start(s32[1,640]{1,0:T(1,128)S(1)} %get-tuple-element.46), channel_id=1, source_target_pairs={{0,16},{2,18},{4,20},{6,22},{8,24},{10,26},{12,28},{14,30},{16,0},... | collective-permute-start | bytes 7688 | tf_op jit(solution)/shard_map/ppermute | solution.py:169
  6.0 1.5 %collective-permute-start = (s32[1,640]{1,0:T(1,128)S(1)}, s32[1,640]{1,0:T(1,128)S(1)}, u32[]{:S(2)}, u32[]{:S(2)}) collective-permute-start(s32[1,640]{1,0:T(1,128)S(1)} %get-tuple-element.46), channel_id=1, source_target_pairs={{0,1},{1,0},{2,3},{3,2},{4,5},{5,4},{6,7},{7,6},{8,9},{9,8},{10,11... | collective-permute-start | bytes 7688 | tf_op jit(solution)/shard_map/ppermute | solution.py:169
  7.5 0.8 convert.13
  8.3 0.8 convert.14
  9.1 0.8 convert.12
  9.9 0.1 pad_add_fusion.1
  10.0 0.4 collective-permute-start.4
  10.4 0.2 collective-permute-start.3
  10.7 1.2 copy.15
  11.9 2.9 %collective-permute-start.7 = (bf16[256,512]{1,0:T(8,128)(2,1)S(1)}, bf16[256,512]{1,0:T(8,128)(2,1)S(1)}, u32[]{:S(2)}, u32[]{:S(2)}) collective-permute-start(bf16[256,512]{1,0:T(8,128)(2,1)S(1)} %bitcast.27), channel_id=1, source_target_pairs={{0,16},{2,18},{4,20},{6,22},{8,24},{10,26},{12,28},{14,30},{16,0},... | collective-permute-start | bytes 786440 | tf_op jit(solution)/shard_map/ppermute | solution.py:169
  14.8 0.0 collective-permute-done.1
  14.8 1.5 %collective-permute-start.2 = (s32[1,640]{1,0:T(1,128)S(1)}, s32[1,640]{1,0:T(1,128)S(1)}, u32[]{:S(2)}, u32[]{:S(2)}) collective-permute-start(s32[1,640]{1,0:T(1,128)S(1)} %collective-permute-done.1), channel_id=1, source_target_pairs={{0,1},{1,0},{2,3},{3,2},{4,5},{5,4},{6,7},{7,6},{8,9},{9,8},{10,11... | collective-permute-start | bytes 7688 | tf_op jit(solution)/shard_map/ppermute | solution.py:169
  16.3 0.0 collective-permute-done
  16.3 0.5 collective-permute-start.6
  16.8 1.6 %collective-permute-done.2 = s32[1,640]{1,0:T(1,128)S(1)} collective-permute-done((s32[1,640]{1,0:T(1,128)S(1)}, s32[1,640]{1,0:T(1,128)S(1)}, u32[]{:S(2)}, u32[]{:S(2)}) %collective-permute-start.2) | collective-permute-done | bytes 2592 | tf_op jit(solution)/shard_map/ppermute | solution.py:169
  18.4 0.2 add_reduce_fusion
  18.6 0.7 fusion.3
  20.6 0.2 select_reduce_fusion.3
  20.8 0.1 select_reduce_fusion
  20.9 0.6 subtract_clamp_fusion
  21.5 5.7 %collective-permute-done.7.refs_2_ = bf16[256,512]{1,0:T(8,128)(2,1)S(1)} collective-permute-done((bf16[256,512]{1,0:T(8,128)(2,1)S(1)}, bf16[256,512]{1,0:T(8,128)(2,1)S(1)}, u32[]{:S(2)}, u32[]{:S(2)}) %collective-permute-start.7) | collective-permute-done | bytes 262176 | tf_op jit(solution)/shard_map/ppermute | solution.py:169
  27.2 0.7 collective-permute-start.8
  27.9 0.6 pad_add_fusion.2.negatives
  28.5 0.0 collective-permute-done.4
  28.5 1.4 %collective-permute-start.5 = (s16[16,3,512]{2,1,0:T(4,128)(2,1)S(1)}, s16[16,3,512]{2,1,0:T(4,128)(2,1)S(1)}, u32[]{:S(2)}, u32[]{:S(2)}) collective-permute-start(s16[16,3,512]{2,1,0:T(4,128)(2,1)S(1)} %collective-permute-done.4), channel_id=1, source_target_pairs={{0,1},{1,0},{2,3},{3,2},{4,5},{5,4},{6,7},{7,6},{8,9},{9,8},{10,11... | collective-permute-start | bytes 147464 | tf_op jit(solution)/shard_map/ppermute | solution.py:169
  29.8 0.6 pad_add_fusion.5.codes
  30.4 5.8 %collective-permute-done.5 = s16[16,3,512]{2,1,0:T(4,128)(2,1)S(1)} collective-permute-done((s16[16,3,512]{2,1,0:T(4,128)(2,1)S(1)}, s16[16,3,512]{2,1,0:T(4,128)(2,1)S(1)}, u32[]{:S(2)}, u32[]{:S(2)}) %collective-permute-start.5) | collective-permute-done | bytes 49184 | tf_op jit(solution)/shard_map/ppermute | solution.py:169
  36.2 0.9 pad_add_fusion.ids
  37.1 0.0 collective-permute-done.6.refs_1_
  37.1 0.0 collective-permute-done.8.refs_3_
  37.2 0.7 copy-done.9
  37.8 0.1 copy-done.10
  37.9 29.0 %edge_kernel.1 = (bf16[16,2,256,512]{3,2,1,0:T(8,128)(2,1)}, f32[512,256]{1,0:T(8,128)}, f32[512,256]{1,0:T(8,128)}, f32[512,256]{1,0:T(8,128)}, f32[512,256]{1,...) custom-call(s32[16]{0:T(128)} %copy-done.7, ...), custom_call_target="tpu_custom_call" | custom-call | flops 32212254720 | bytes 16777216 | tf_op jit(solution)/shard_map/edge_kernel/pallas_call | solution.py:244
  66.9 2.9 %collective-permute-start.9 = (f32[256,256]{1,0:T(8,128)}, f32[256,256]{1,0:T(8,128)S(1)}, u32[]{:S(2)}, u32[]{:S(2)}) collective-permute-start(f32[256,256]{1,0:T(8,128)} %get-tuple-element.21), channel_id=1, source_target_pairs={{0,2},{2,0},{4,6},{6,4},{8,10},{10,8},{12,14},{14,12},{16,18},{18,... | collective-permute-start | bytes 786440 | tf_op jit(solution)/shard_map/ppermute | solution.py:169
  69.7 1.4 %collective-permute-done.9 = f32[256,256]{1,0:T(8,128)S(1)} collective-permute-done((f32[256,256]{1,0:T(8,128)}, f32[256,256]{1,0:T(8,128)S(1)}, u32[]{:S(2)}, u32[]{:S(2)}) %collective-permute-start.9) | collective-permute-done | bytes 262176 | tf_op jit(solution)/shard_map/ppermute | solution.py:169
  71.1 1.0 slice_add_fusion.2
  72.1 1.6 %collective-permute-start.10 = (f32[64,256]{1,0:T(8,128)S(1)}, f32[64,256]{1,0:T(8,128)S(1)}, u32[]{:S(2)}, u32[]{:S(2)}) collective-permute-start(f32[64,256]{1,0:T(8,128)S(1)} %get-tuple-element.42), channel_id=1, source_target_pairs={{0,1},{1,0},{2,3},{3,2},{4,5},{5,4},{6,7},{7,6},{8,9},{9,8},{10,11... | collective-permute-start | bytes 196616 | tf_op jit(solution)/shard_map/ppermute | solution.py:280
  73.7 2.0 %collective-permute-start.12 = (f32[64,256]{1,0:T(8,128)S(1)}, f32[64,256]{1,0:T(8,128)S(1)}, u32[]{:S(2)}, u32[]{:S(2)}) collective-permute-start(f32[64,256]{1,0:T(8,128)S(1)} %get-tuple-element.43), channel_id=1, source_target_pairs={{0,5},{1,4},{2,7},{3,6},{4,1},{5,0},{6,3},{7,2},{8,13},{9,12},{10,... | collective-permute-start | bytes 196616 | tf_op jit(solution)/shard_map/ppermute | solution.py:280
  75.7 1.5 %collective-permute-start.19 = (f32[512,256]{1,0:T(8,128)}, f32[512,256]{1,0:T(8,128)S(1)}, u32[]{:S(2)}, u32[]{:S(2)}) collective-permute-start(f32[512,256]{1,0:T(8,128)} %get-tuple-element.26), channel_id=1, source_target_pairs={{0,1},{1,0},{2,3},{3,2},{4,5},{5,4},{6,7},{7,6},{8,9},{9,8},{10,11... | collective-permute-start | bytes 1572872 | tf_op jit(solution)/shard_map/ppermute | solution.py:169
  77.2 1.3 collective-permute-done.11
  78.5 0.9 collective-permute-done.12
  79.4 0.9 fusion.2
  80.3 0.1 collective-permute-start.13
  80.4 0.0 copy-start.6
  80.4 9.9 %near_kernel.1 = (f32[512,256]{1,0:T(8,128)}, f32[512,256]{1,0:T(8,128)}) custom-call(s32[16]{0:T(128)} %copy-done.7, s32[16]{0:T(128)} %get-tuple-element.48.place, s32[16]{0:T(128)} %get-tuple-element.47.live, s32[3]{0:T(128)} %pad_add_fusion.5.codes, s16[64,3,512]{2,1,0:T(4,128)(2,1)} %pad_add_fusion.ids, ...), custom_call_target="tpu_custom_call" | custom-call | flops 4294967296 | bytes 8388608 | tf_op jit(solution)/shard_map/near_kernel/pallas_call | solution.py:294
  90.2 1.3 %collective-permute-start.21 = (f32[512,256]{1,0:T(8,128)}, f32[512,256]{1,0:T(8,128)S(1)}, u32[]{:S(2)}, u32[]{:S(2)}) collective-permute-start(f32[512,256]{1,0:T(8,128)} %get-tuple-element.31), channel_id=1, source_target_pairs={{0,1},{1,0},{2,3},{3,2},{4,5},{5,4},{6,7},{7,6},{8,9},{9,8},{10,11... | collective-permute-start | bytes 1572872 | tf_op jit(solution)/shard_map/ppermute | solution.py:169
  91.6 0.1 add.114
  91.7 1.5 %collective-permute-start.20 = (f32[512,256]{1,0:T(8,128)S(1)}, f32[512,256]{1,0:T(8,128)S(1)}, u32[]{:S(2)}, u32[]{:S(2)}) collective-permute-start(f32[512,256]{1,0:T(8,128)S(1)} %add.114), channel_id=1, source_target_pairs={{0,16},{2,18},{4,20},{6,22},{8,24},{10,26},{12,28},{14,30},{16,0},... | collective-permute-start | bytes 1572872 | tf_op jit(solution)/shard_map/ppermute | solution.py:169
  93.2 1.5 %collective-permute-start.14 = (f32[64,256]{1,0:T(8,128)S(1)}, f32[64,256]{1,0:T(8,128)S(1)}, u32[]{:S(2)}, u32[]{:S(2)}) collective-permute-start(f32[64,256]{1,0:T(8,128)S(1)} %add.112), channel_id=1, source_target_pairs={{0,16},{2,18},{4,20},{6,22},{8,24},{10,26},{12,28},{14,30},{16,0},... | collective-permute-start | bytes 196616 | tf_op jit(solution)/shard_map/ppermute | solution.py:169
  94.7 24.6 %collective-permute-done.14 = f32[64,256]{1,0:T(8,128)S(1)} collective-permute-done((f32[64,256]{1,0:T(8,128)S(1)}, f32[64,256]{1,0:T(8,128)S(1)}, u32[]{:S(2)}, u32[]{:S(2)}) %collective-permute-start.14) | collective-permute-done | bytes 65568 | tf_op jit(solution)/shard_map/ppermute | solution.py:169
  119.3 0.5 collective-permute-start.15
  119.8 0.1 collective-permute-start.16
  119.9 3.0 %collective-permute-start.17 = (f32[64,256]{1,0:T(8,128)S(1)}, f32[64,256]{1,0:T(8,128)S(1)}, u32[]{:S(2)}, u32[]{:S(2)}) collective-permute-start(f32[64,256]{1,0:T(8,128)S(1)} %add.113), channel_id=1, source_target_pairs={{0,5},{1,4},{2,7},{3,6},{4,1},{5,0},{6,3},{7,2},{8,13},{9,12},{10,... | collective-permute-start | bytes 196616 | tf_op jit(solution)/shard_map/ppermute | solution.py:280
  122.9 0.8 collective-permute-done.15
  123.6 0.9 collective-permute-done.16
  124.6 1.4 %collective-permute-done.17 = f32[64,256]{1,0:T(8,128)S(1)} collective-permute-done((f32[64,256]{1,0:T(8,128)S(1)}, f32[64,256]{1,0:T(8,128)S(1)}, u32[]{:S(2)}, u32[]{:S(2)}) %collective-permute-start.17) | collective-permute-done | bytes 65568 | tf_op jit(solution)/shard_map/ppermute | solution.py:280
  126.0 0.1 collective-permute-start.18
  126.1 0.8 copy.16.state
  127.0 0.8 copy-done.2
  127.7 0.2 copy-done.3
  127.9 2.7 %entity_kernel.1 = (f32[512,256]{1,0:T(8,128)}, f32[1,512]{1,0:T(1,128)}) custom-call(f32[512,256]{1,0:T(8,128)} %table.1, f32[1,512]{1,0:T(1,128)} %bitcast.37, f32[512,256]{1,0:T(8,128)} %copy-done.3, f32[512,256]{1,0:T(8,128)} %get-tuple-element.30.refs_0_, f32[512,256]{1,0:T(8,128)} %copy-done.2), custom_call_target="tpu_custom_call" | custom-call | tf_op jit(solution)/shard_map/entity_kernel/pallas_call | solution.py:311
  130.6 0.7 copy-done.5
  131.3 2.3 %relation_kernel.1 = f32[400,256]{1,0:T(8,128)} custom-call(s32[1]{0:T(128)} %bitcast.15.code, f32[400,256]{1,0:T(8,128)} %relations.3, f32[400,1]{1,0:T(8,128)} %copy.16.state, f32[256,256]{1,0:T(8,128)} %copy-done, f32[256,256]{1,0:T(8,128)} %copy-done.5), custom_call_target="tpu_custom_call" | custom-call | tf_op jit(solution)/shard_map/relation_kernel/pallas_call | solution.py:326
  (30 shorter events, 0.1 us)
Async XLA Ops:
  2.0 12.8 %collective-permute-start.1 = (s32[1,640]{1,0:T(1,128)S(1)}, s32[1,640]{1,0:T(1,128)S(1)}, u32[]{:S(2)}, u32[]{:S(2)}) collective-permute-start(s32[1,640]{1,0:T(1,128)S(1)} %get-tuple-element.46), channel_id=1, source_target_pairs={{0,16},{2,18},{4,20},{6,22},{8,24},{10,26},{12,28},{14,30},{16,0},... | collective-permute-start | bytes 7688 | tf_op jit(solution)/shard_map/ppermute | solution.py:169
  6.0 10.3 %collective-permute-start = (s32[1,640]{1,0:T(1,128)S(1)}, s32[1,640]{1,0:T(1,128)S(1)}, u32[]{:S(2)}, u32[]{:S(2)}) collective-permute-start(s32[1,640]{1,0:T(1,128)S(1)} %get-tuple-element.46), channel_id=1, source_target_pairs={{0,1},{1,0},{2,3},{3,2},{4,5},{5,4},{6,7},{7,6},{8,9},{9,8},{10,11... | collective-permute-start | bytes 7688 | tf_op jit(solution)/shard_map/ppermute | solution.py:169
  10.0 18.5 %collective-permute-start.4 = (s16[16,3,512]{2,1,0:T(4,128)(2,1)S(1)}, s16[16,3,512]{2,1,0:T(4,128)(2,1)S(1)}, u32[]{:S(2)}, u32[]{:S(2)}) collective-permute-start(s16[16,3,512]{2,1,0:T(4,128)(2,1)S(1)} %pad_add_fusion.1), channel_id=1, source_target_pairs={{0,16},{2,18},{4,20},{6,22},{8,24},{10,26},{12,28},{14,30},{16,0},... | collective-permute-start | bytes 147464 | tf_op jit(solution)/shard_map/ppermute | solution.py:169
  10.4 20.0 %collective-permute-start.3 = (s16[16,3,512]{2,1,0:T(4,128)(2,1)S(1)}, s16[16,3,512]{2,1,0:T(4,128)(2,1)S(1)}, u32[]{:S(2)}, u32[]{:S(2)}) collective-permute-start(s16[16,3,512]{2,1,0:T(4,128)(2,1)S(1)} %pad_add_fusion.1), channel_id=1, source_target_pairs={{0,1},{1,0},{2,3},{3,2},{4,5},{5,4},{6,7},{7,6},{8,9},{9,8},{10,11... | collective-permute-start | bytes 147464 | tf_op jit(solution)/shard_map/ppermute | solution.py:169
  11.8 25.3 %copy-start.4 = (bf16[512,256]{0,1:T(8,128)(2,1)}, bf16[512,256]{0,1:T(8,128)(2,1)S(1)}, u32[]{:S(2)}) copy-start(bf16[512,256]{0,1:T(8,128)(2,1)S(1)} %copy.15) | copy-start | bytes 786436
  11.9 15.3 %collective-permute-start.7 = (bf16[256,512]{1,0:T(8,128)(2,1)S(1)}, bf16[256,512]{1,0:T(8,128)(2,1)S(1)}, u32[]{:S(2)}, u32[]{:S(2)}) collective-permute-start(bf16[256,512]{1,0:T(8,128)(2,1)S(1)} %bitcast.27), channel_id=1, source_target_pairs={{0,16},{2,18},{4,20},{6,22},{8,24},{10,26},{12,28},{14,30},{16,0},... | collective-permute-start | bytes 786440 | tf_op jit(solution)/shard_map/ppermute | solution.py:169
  14.8 3.7 %collective-permute-start.2 = (s32[1,640]{1,0:T(1,128)S(1)}, s32[1,640]{1,0:T(1,128)S(1)}, u32[]{:S(2)}, u32[]{:S(2)}) collective-permute-start(s32[1,640]{1,0:T(1,128)S(1)} %collective-permute-done.1), channel_id=1, source_target_pairs={{0,1},{1,0},{2,3},{3,2},{4,5},{5,4},{6,7},{7,6},{8,9},{9,8},{10,11... | collective-permute-start | bytes 7688 | tf_op jit(solution)/shard_map/ppermute | solution.py:169
  16.3 20.8 %collective-permute-start.6 = (bf16[256,512]{1,0:T(8,128)(2,1)S(1)}, bf16[256,512]{1,0:T(8,128)(2,1)S(1)}, u32[]{:S(2)}, u32[]{:S(2)}) collective-permute-start(bf16[256,512]{1,0:T(8,128)(2,1)S(1)} %bitcast.28), channel_id=1, source_target_pairs={{0,1},{1,0},{2,3},{3,2},{4,5},{5,4},{6,7},{7,6},{8,9},{9,8},{10,11... | collective-permute-start | bytes 786440 | tf_op jit(solution)/shard_map/ppermute | solution.py:169
  20.9 16.3 %copy-start.7 = (s32[16]{0:T(128)}, s32[16]{0:T(128)S(1)}, u32[]{:S(2)}) copy-start(s32[16]{0:T(128)S(1)} %get-tuple-element.39.source) | copy-start | bytes 196
  27.2 10.0 %copy-start.8 = (bf16[256,512]{1,0:T(8,128)(2,1)}, bf16[256,512]{1,0:T(8,128)(2,1)S(1)}, u32[]{:S(2)}) copy-start(bf16[256,512]{1,0:T(8,128)(2,1)S(1)} %collective-permute-done.7.refs_2_) | copy-start | bytes 786436
  27.2 9.9 %collective-permute-start.8 = (bf16[256,512]{1,0:T(8,128)(2,1)S(1)}, bf16[256,512]{1,0:T(8,128)(2,1)S(1)}, u32[]{:S(2)}, u32[]{:S(2)}) collective-permute-start(bf16[256,512]{1,0:T(8,128)(2,1)S(1)} %collective-permute-done.7.refs_2_), channel_id=1, source_target_pairs={{0,1},{1,0},{2,3},{3,2},{4,5},{5,4},{6,7},{7,6},{8,9},{9,8},{10,11... | collective-permute-start | bytes 786440 | tf_op jit(solution)/shard_map/ppermute | solution.py:169
  28.5 7.8 %collective-permute-start.5 = (s16[16,3,512]{2,1,0:T(4,128)(2,1)S(1)}, s16[16,3,512]{2,1,0:T(4,128)(2,1)S(1)}, u32[]{:S(2)}, u32[]{:S(2)}) collective-permute-start(s16[16,3,512]{2,1,0:T(4,128)(2,1)S(1)} %collective-permute-done.4), channel_id=1, source_target_pairs={{0,1},{1,0},{2,3},{3,2},{4,5},{5,4},{6,7},{7,6},{8,9},{9,8},{10,11... | collective-permute-start | bytes 147464 | tf_op jit(solution)/shard_map/ppermute | solution.py:169
  37.1 0.7 copy-start.9
  37.1 0.8 copy-start.10
  66.9 4.2 %collective-permute-start.9 = (f32[256,256]{1,0:T(8,128)}, f32[256,256]{1,0:T(8,128)S(1)}, u32[]{:S(2)}, u32[]{:S(2)}) collective-permute-start(f32[256,256]{1,0:T(8,128)} %get-tuple-element.21), channel_id=1, source_target_pairs={{0,2},{2,0},{4,6},{6,4},{8,10},{10,8},{12,14},{14,12},{16,18},{18,... | collective-permute-start | bytes 786440 | tf_op jit(solution)/shard_map/ppermute | solution.py:169
  71.1 20.5 %copy-start.1 = (f32[512,256]{1,0:T(8,128)S(1)}, f32[512,256]{1,0:T(8,128)}, u32[]{:S(2)}) copy-start(f32[512,256]{1,0:T(8,128)} %get-tuple-element.25) | copy-start | bytes 1572868
  72.1 5.1 %collective-permute-start.10 = (f32[64,256]{1,0:T(8,128)S(1)}, f32[64,256]{1,0:T(8,128)S(1)}, u32[]{:S(2)}, u32[]{:S(2)}) collective-permute-start(f32[64,256]{1,0:T(8,128)S(1)} %get-tuple-element.42), channel_id=1, source_target_pairs={{0,1},{1,0},{2,3},{3,2},{4,5},{5,4},{6,7},{7,6},{8,9},{9,8},{10,11... | collective-permute-start | bytes 196616 | tf_op jit(solution)/shard_map/ppermute | solution.py:280
  73.7 4.8 %collective-permute-start.11 = (f32[64,256]{1,0:T(8,128)S(1)}, f32[64,256]{1,0:T(8,128)S(1)}, u32[]{:S(2)}, u32[]{:S(2)}) collective-permute-start(f32[64,256]{1,0:T(8,128)S(1)} %get-tuple-element.44), channel_id=1, source_target_pairs={{0,4},{1,5},{2,6},{3,7},{4,0},{5,1},{6,2},{7,3},{8,12},{9,13},{10,... | collective-permute-start | bytes 196616 | tf_op jit(solution)/shard_map/ppermute | solution.py:280
  73.7 5.7 %collective-permute-start.12 = (f32[64,256]{1,0:T(8,128)S(1)}, f32[64,256]{1,0:T(8,128)S(1)}, u32[]{:S(2)}, u32[]{:S(2)}) collective-permute-start(f32[64,256]{1,0:T(8,128)S(1)} %get-tuple-element.43), channel_id=1, source_target_pairs={{0,5},{1,4},{2,7},{3,6},{4,1},{5,0},{6,3},{7,2},{8,13},{9,12},{10,... | collective-permute-start | bytes 196616 | tf_op jit(solution)/shard_map/ppermute | solution.py:280
  75.7 15.9 %collective-permute-start.19 = (f32[512,256]{1,0:T(8,128)}, f32[512,256]{1,0:T(8,128)S(1)}, u32[]{:S(2)}, u32[]{:S(2)}) collective-permute-start(f32[512,256]{1,0:T(8,128)} %get-tuple-element.26), channel_id=1, source_target_pairs={{0,1},{1,0},{2,3},{3,2},{4,5},{5,4},{6,7},{7,6},{8,9},{9,8},{10,11... | collective-permute-start | bytes 1572872 | tf_op jit(solution)/shard_map/ppermute | solution.py:169
  80.3 12.9 %collective-permute-start.13 = (f32[64,256]{1,0:T(8,128)S(1)}, f32[64,256]{1,0:T(8,128)S(1)}, u32[]{:S(2)}, u32[]{:S(2)}) collective-permute-start(f32[64,256]{1,0:T(8,128)S(1)} %fusion.2), channel_id=1, source_target_pairs={{0,8},{2,10},{4,12},{6,14},{8,0},{10,2},{12,4},{14,6},{16,24},{18,... | collective-permute-start | bytes 196616 | tf_op jit(solution)/shard_map/ppermute | solution.py:169
  80.4 45.7 %copy-start.6 = (f32[400]{0:T(512)S(1)}, f32[400]{0:T(512)}, u32[]{:S(2)}) copy-start(f32[400]{0:T(512)} %param.12) | copy-start | bytes 4804
  90.2 36.7 %collective-permute-start.21 = (f32[512,256]{1,0:T(8,128)}, f32[512,256]{1,0:T(8,128)S(1)}, u32[]{:S(2)}, u32[]{:S(2)}) collective-permute-start(f32[512,256]{1,0:T(8,128)} %get-tuple-element.31), channel_id=1, source_target_pairs={{0,1},{1,0},{2,3},{3,2},{4,5},{5,4},{6,7},{7,6},{8,9},{9,8},{10,11... | collective-permute-start | bytes 1572872 | tf_op jit(solution)/shard_map/ppermute | solution.py:169
  91.7 35.3 %collective-permute-start.20 = (f32[512,256]{1,0:T(8,128)S(1)}, f32[512,256]{1,0:T(8,128)S(1)}, u32[]{:S(2)}, u32[]{:S(2)}) collective-permute-start(f32[512,256]{1,0:T(8,128)S(1)} %add.114), channel_id=1, source_target_pairs={{0,16},{2,18},{4,20},{6,22},{8,24},{10,26},{12,28},{14,30},{16,0},... | collective-permute-start | bytes 1572872 | tf_op jit(solution)/shard_map/ppermute | solution.py:169
  93.2 26.1 %collective-permute-start.14 = (f32[64,256]{1,0:T(8,128)S(1)}, f32[64,256]{1,0:T(8,128)S(1)}, u32[]{:S(2)}, u32[]{:S(2)}) collective-permute-start(f32[64,256]{1,0:T(8,128)S(1)} %add.112), channel_id=1, source_target_pairs={{0,16},{2,18},{4,20},{6,22},{8,24},{10,26},{12,28},{14,30},{16,0},... | collective-permute-start | bytes 196616 | tf_op jit(solution)/shard_map/ppermute | solution.py:169
  119.3 4.3 %collective-permute-start.15 = (f32[64,256]{1,0:T(8,128)S(1)}, f32[64,256]{1,0:T(8,128)S(1)}, u32[]{:S(2)}, u32[]{:S(2)}) collective-permute-start(f32[64,256]{1,0:T(8,128)S(1)} %add.113), channel_id=1, source_target_pairs={{0,1},{1,0},{2,3},{3,2},{4,5},{5,4},{6,7},{7,6},{8,9},{9,8},{10,11... | collective-permute-start | bytes 196616 | tf_op jit(solution)/shard_map/ppermute | solution.py:280
  119.8 4.8 %collective-permute-start.16 = (f32[64,256]{1,0:T(8,128)S(1)}, f32[64,256]{1,0:T(8,128)S(1)}, u32[]{:S(2)}, u32[]{:S(2)}) collective-permute-start(f32[64,256]{1,0:T(8,128)S(1)} %add.113), channel_id=1, source_target_pairs={{0,4},{1,5},{2,6},{3,7},{4,0},{5,1},{6,2},{7,3},{8,12},{9,13},{10,... | collective-permute-start | bytes 196616 | tf_op jit(solution)/shard_map/ppermute | solution.py:280
  119.9 6.1 %collective-permute-start.17 = (f32[64,256]{1,0:T(8,128)S(1)}, f32[64,256]{1,0:T(8,128)S(1)}, u32[]{:S(2)}, u32[]{:S(2)}) collective-permute-start(f32[64,256]{1,0:T(8,128)S(1)} %add.113), channel_id=1, source_target_pairs={{0,5},{1,4},{2,7},{3,6},{4,1},{5,0},{6,3},{7,2},{8,13},{9,12},{10,... | collective-permute-start | bytes 196616 | tf_op jit(solution)/shard_map/ppermute | solution.py:280
  126.0 4.6 %copy-start = (f32[256,256]{1,0:T(8,128)}, f32[256,256]{1,0:T(8,128)S(1)}, u32[]{:S(2)}) copy-start(f32[256,256]{1,0:T(8,128)S(1)} %pad_maximum_fusion.mine) | copy-start | bytes 786436
  126.0 4.6 %collective-permute-start.18 = (f32[256,256]{1,0:T(8,128)S(1)}, f32[256,256]{1,0:T(8,128)S(1)}, u32[]{:S(2)}, u32[]{:S(2)}) collective-permute-start(f32[256,256]{1,0:T(8,128)S(1)} %pad_maximum_fusion.mine), channel_id=1, source_target_pairs={{0,2},{2,0},{4,6},{6,4},{8,10},{10,8},{12,14},{14,12},{16,18},{18,... | collective-permute-start | bytes 786440 | tf_op jit(solution)/shard_map/ppermute | solution.py:169
  126.9 0.8 copy-start.2
  126.9 1.0 copy-start.3
  130.6 0.7 copy-start.5

commit v3 on v2

v3 whole, which is shorter than its diff:
```python
import functools

import jax
import jax.numpy as jnp
from jax import lax
from jax.experimental import pallas as pl
from jax.experimental.pallas import tpu as pltpu
from jax.sharding import PartitionSpec as P

learn_rate = 0.1
bf16 = jnp.bfloat16
f32 = jnp.float32
i32 = jnp.int32
params = pltpu.CompilerParams(vmem_limit_bytes=56 * 2**20)


def dot(a, b):
    return jnp.dot(a, b, preferred_element_type=f32)


def dot_nt(a, b):
    return lax.dot_general(a, b, (((1,), (1,)), ((), ())), preferred_element_type=f32)


def one_hot(ids, rows):
    places = lax.broadcasted_iota(jnp.int16, (rows, ids.shape[1]), 0)
    return jnp.where(places == ids.astype(jnp.int16), jnp.ones((), bf16), jnp.zeros((), bf16))


def split(x):
    high = x.astype(bf16)
    return jnp.concatenate([high, (x - high.astype(f32)).astype(bf16)], axis=1)


def gather(pieces, ids):
    rows = pieces[0].shape[1]
    hot = one_hot(ids, len(pieces) * rows)
    total = dot(pieces[0][...], hot[:rows])
    for k in range(1, len(pieces)):
        total = total + dot(pieces[k][...], hot[k * rows : (k + 1) * rows])
    return total


def scatter_add(pieces, ids, pair):
    hot = one_hot(ids, sum(piece.shape[0] for piece in pieces))
    hot = jnp.concatenate([hot, hot], axis=1)
    start = 0
    for piece in pieces:
        piece[...] += dot_nt(hot[start : start + piece.shape[0]], pair)
        start += piece.shape[0]


def prep_kernel(count, table, heads, tails, kinds, negatives, rows_out, ids_out):
    rows_out[...] = table[...].T.astype(bf16)
    blocks, _, width = ids_out.shape
    for j in range(blocks - 1):
        at = slice(j * width, (j + 1) * width)
        block = jnp.concatenate([heads[:, at], tails[:, at], kinds[:, at]], axis=0)
        ids_out[j] = block.astype(jnp.int16)
    last = jnp.concatenate([negatives[...], jnp.full((2, width), count[0, 0], i32)], axis=0)
    ids_out[blocks - 1] = last.astype(jnp.int16)


def plan_kernel(n, codes, *refs):
    sources, (plan, step_ids, negative_ids) = refs[:-3], refs[-3:]
    team = len(sources)
    most, _, width = step_ids.shape
    me = codes[0]
    counts, blocks = [], []
    for k, ids in enumerate(sources):
        last = ids[most].astype(i32)
        counts.append(jnp.max(last[1:2]))
        blocks.append(lax.div(counts[k] + (width - 1), i32(width)))
        negative_ids[k] = last[0:1] ^ codes[1]
    total = sum(blocks)
    low = lax.div(me * total, i32(team))
    high = lax.div((me + 1) * total, i32(team))
    plan[2 * most] = high - low
    before = []
    for k in range(team):
        ahead = [jnp.where((me ^ j) < (me ^ k), blocks[j], 0) for j in range(team) if j != k]
        before.append(sum(ahead))
        seen = (before[k] < high) & (before[k] + blocks[k] > low)
        plan[2 * most + 1 + k] = seen.astype(i32)

    def one_step(i, carry):
        line = jnp.minimum(low + i, high - 1)
        for k, ids in enumerate(sources):

            @pl.when((line >= before[k]) & (line < before[k] + blocks[k]))
            def _(k=k, ids=ids):
                nth = line - before[k]
                plan[i] = k
                plan[most + i] = jnp.clip(counts[k] - nth * width, 0, width)
                entries = ids[nth].astype(i32)
                near, away = (0, 1) if k < n else (1, 0)
                step_ids[i, 0:1] = entries[near : near + 1] ^ codes[1]
                step_ids[i, 1:2] = entries[away : away + 1] ^ codes[1]
                step_ids[i, 2:3] = entries[2:3]
                step_ids[i, 3:4] = entries[2:3] ^ codes[2]

        return carry

    lax.fori_loop(0, most, one_step, 0)


def near_kernel(plan, ids, relations, *refs):
    slab, (rows_out, operator_out, rel_full, rel_split) = refs[:-4], refs[-4:]
    dims = relations.shape[1]

    @pl.when(pl.program_id(0) == 0)
    def _():
        rel_full[...] = jnp.zeros_like(rel_full)
        rel_full[: relations.shape[0], :] = relations[...]
        full = rel_full[...].T
        high = full.astype(bf16)
        rel_split[:dims, :] = high
        rel_split[dims:, :] = (full - high.astype(f32)).astype(bf16)

    @pl.when(pl.program_id(0) < plan[2 * pl.num_programs(0)])
    def _():
        rows_out[0] = gather(slab, ids[0, 0:1, :]).astype(bf16)
        both = dot(rel_split[...], one_hot(ids[0, 2:3, :], rel_full.shape[0]))
        operator_out[0] = both[:dims] + both[dims:]


def edge_kernel(n, plan, ids, negative_ids, near_in, operator_in, *refs):
    near, away = refs[:n], refs[n : 2 * n]
    near_grad, away_grad, negative_out = refs[2 * n : 2 * n + 3]
    relation_sum, (table, table_t, negative_grad) = refs[2 * n + 3 : -3], refs[-3:]
    step = pl.program_id(0)
    most = pl.num_programs(0)
    steps = plan[2 * most]
    here = plan[step]
    swapped = here >= n
    count = table.shape[0]

    @pl.when(step == 0)
    def _():
        for piece in relation_sum:
            piece[...] = jnp.zeros_like(piece)

    def take_table(slab):
        found = gather(slab, negative_ids[here])
        table_t[...] = found.astype(bf16)
        table[...] = found.T.astype(bf16)
        negative_grad[...] = jnp.zeros_like(negative_grad)

    fresh = (step < steps) & ((step == 0) | (plan[jnp.maximum(step - 1, 0)] != here))
    pl.when(fresh & ~swapped)(lambda: take_table(away))
    pl.when(fresh & swapped)(lambda: take_table(near))

    @pl.when(step < steps)
    def _():
        width = ids.shape[2]
        alive = (lax.broadcasted_iota(i32, (1, width), 1) < plan[most + step]).astype(f32)
        near_rows = near_in[0].astype(f32)
        away_rows = gather(away, ids[0, 1:2, :])
        head = jnp.where(swapped, away_rows, near_rows)
        tail = jnp.where(swapped, near_rows, away_rows)
        operator = operator_in[0]
        query = head * operator
        query_b = query.astype(bf16)
        positive = jnp.sum(query * tail, axis=0, keepdims=True)
        scores = dot(table[...], query_b)
        pos_coef = -jax.nn.sigmoid(-positive) * alive
        neg_coef = (jax.nn.sigmoid(scores) * (alive * (1.0 / count))).astype(bf16)
        query_grad = pos_coef * tail + dot(table_t[...], neg_coef)
        negative_grad[...] += dot_nt(query_b, neg_coef)
        head_grad = query_grad * operator
        tail_grad = pos_coef * query
        near_grad[0] = split(jnp.where(swapped, tail_grad, head_grad))
        away_grad[0] = split(jnp.where(swapped, head_grad, tail_grad))
        scatter_add(relation_sum, ids[0, 3:4, :], split(query_grad * head))

    @pl.when((step == steps - 1) | ((step < steps) & (plan[jnp.minimum(step + 1, steps - 1)] != here)))
    def _():
        negative_out[0] = split(negative_grad[...])


def scatter_kernel(most, row, start, first, plan, ids, negative_ids, grads, negative_grads, *sums):
    step = pl.program_id(0)

    @pl.when(step == 0)
    def _():
        for piece in sums:
            piece[...] = jnp.zeros_like(piece)

    @pl.when(step < plan[2 * most])
    def _():
        scatter_add(sums, ids[0, row : row + 1, :] - start, grads[0])

    @pl.when((step >= most) & (plan[2 * most + 1 + first + jnp.maximum(step - most, 0)] != 0))
    def _():
        scatter_add(sums, negative_ids[0] - start, negative_grads[0])


def entity_kernel(n, table, state, returned, *refs):
    parts, (new_table, new_state) = refs[:n], refs[n:]
    grad = returned[...]
    for part in parts:
        grad = grad + part[...]
    lanes = 128
    before = jnp.broadcast_to(state[...], (lanes, table.shape[0])).T[:, :1]
    after = before + jnp.mean(grad * grad, axis=-1, keepdims=True)
    new_table[...] = table[...] - learn_rate * grad / jnp.sqrt(after)
    new_state[...] = jnp.broadcast_to(after, (table.shape[0], lanes)).T[:1]


def relation_kernel(chunk, codes, relations, state, mine, theirs, out, grad):
    chunks = mine.shape[0] // chunk
    for k in range(2 * chunks):
        part = (mine, theirs)[k // chunks]
        start = (k % chunks) * chunk
        grad[pl.ds(pl.multiple_of(codes[2] ^ (k * chunk), chunk), chunk), :] = part[start : start + chunk, :]
    g = grad[: relations.shape[0], :]
    total = state[...] + jnp.mean(g * g, axis=-1, keepdims=True)
    out[...] = relations[...] - learn_rate * g / jnp.sqrt(total)


def exchange(x, axis, mask):
    return lax.ppermute(x, axis, [(i, i ^ mask) for i in range(lax.axis_size(axis))])


def on_device(
    entity_table,
    entity_state,
    relations,
    relation_state,
    head_rows,
    tail_rows,
    relation_ids,
    negative_rows,
    edge_counts,
):
    n = lax.axis_size("sub")
    n_dom = lax.axis_size("dom")
    me_sub = lax.axis_index("sub")
    me_dom = lax.axis_index("dom")
    pair = n_dom // 2
    team = 2 * n
    rows, dims = entity_table.shape
    slots = head_rows.shape[2]
    count = negative_rows.shape[2]
    width = count
    most = slots // width
    rel_rows = -(-relations.shape[0] // 256) * 256
    chips = 2 * n
    chunk = rel_rows // (2 * chips)
    shape = jax.ShapeDtypeStruct
    in_vmem = pl.BlockSpec(memory_space=pltpu.VMEM)
    in_smem = pl.BlockSpec(memory_space=pltpu.SMEM)

    me = lax.shift_right_logical(me_dom, pair.bit_length() - 1) * n + me_sub
    chunk_code = (me_dom & 1) * chips + ((me_dom >> 1) & 1) * n + me_sub
    codes = jnp.stack([me, me_sub * rows, chunk_code * chunk]).astype(i32)

    local, ids = pl.pallas_call(
        prep_kernel,
        in_specs=[in_smem] + [in_vmem] * 5,
        out_specs=[in_vmem] * 2,
        out_shape=[shape((dims, rows), bf16), shape((most + 1, 3, width), jnp.int16)],
        compiler_params=params,
        name="prep_kernel",
    )(
        edge_counts,
        entity_table,
        head_rows.reshape(1, slots),
        tail_rows.reshape(1, slots),
        relation_ids.reshape(1, slots),
        negative_rows.reshape(1, count),
    )

    def along_sub(x):
        return [x] + [exchange(x, "sub", k) for k in range(1, n)]

    away_slab = along_sub(exchange(local, "dom", pair))
    all_ids = along_sub(ids) + along_sub(exchange(ids, "dom", pair))
    near_slab = along_sub(local)

    plan, step_ids, negative_ids = pl.pallas_call(
        functools.partial(plan_kernel, n),
        in_specs=[in_smem] + [in_vmem] * team,
        out_specs=[in_smem, in_vmem, in_vmem],
        out_shape=[
            shape((2 * most + 1 + team,), i32),
            shape((most, 4, width), i32),
            shape((team, 1, width), i32),
        ],
        compiler_params=params,
        name="plan_kernel",
    )(codes, *all_ids)

    def whole(*dims):
        return pl.BlockSpec(dims, lambda i, p: (0,) * len(dims))

    def stepped(*dims):
        return pl.BlockSpec((1, *dims), lambda i, p: (jnp.minimum(i, p[2 * most] - 1),) + (0,) * len(dims))

    def call(kernel, name, grid, in_specs, outs, scratch, unit, args):
        return pl.pallas_call(
            kernel,
            grid_spec=pltpu.PrefetchScalarGridSpec(
                num_scalar_prefetch=1,
                grid=(grid,),
                in_specs=in_specs,
                out_specs=[spec for spec, _ in outs],
                scratch_shapes=scratch,
            ),
            out_shape=[x for _, x in outs],
            compiler_params=params,
            cost_estimate=pl.CostEstimate(
                flops=2 * slots * dims * unit, bytes_accessed=4 * slots * dims, transcendentals=0
            ),
            name=name,
        )(plan, *args)

    id_spec = stepped(4, width)
    slab_specs = [whole(dims, rows)] * n
    near_rows, operator = call(
        near_kernel,
        "near_kernel",
        most,
        [id_spec, whole(*relations.shape)] + slab_specs,
        [
            (stepped(dims, width), shape((most, dims, width), bf16)),
            (stepped(dims, width), shape((most, dims, width), f32)),
        ],
        [pltpu.VMEM((rel_rows, dims), f32), pltpu.VMEM((2 * dims, rel_rows), bf16)],
        n * rows + 2 * rel_rows,
        (step_ids, relations, *near_slab),
    )

    grad_out = (stepped(dims, 2 * width), shape((most, dims, 2 * width), bf16))
    pieces = [(chunk, dims)] * chips + [(chips * chunk, dims)]
    near_grad, away_grad, negative_grad, *relation_part = call(
        functools.partial(edge_kernel, n),
        "edge_kernel",
        most,
        [id_spec, whole(team, 1, width), stepped(dims, width), stepped(dims, width)] + slab_specs * 2,
        [
            grad_out,
            grad_out,
            (
                pl.BlockSpec((1, dims, 2 * width), lambda i, p: (p[jnp.minimum(i, p[2 * most] - 1)], 0, 0)),
                shape((team, dims, 2 * width), bf16),
            ),
        ]
        + [(whole(*x), shape(x, f32)) for x in pieces],
        [pltpu.VMEM((count, dims), bf16), pltpu.VMEM((dims, count), bf16), pltpu.VMEM((dims, count), f32)],
        n * rows + 3 * count + 2 * rel_rows,
        (step_ids, negative_ids, near_rows, operator, *near_slab, *away_slab),
    )

    def scatter(name, row, start, parts, first, grads):
        def negative_spec(*dims):
            return pl.BlockSpec((1, *dims), lambda i, p: (first + jnp.maximum(i - most, 0),) + (0,) * len(dims))

        return call(
            functools.partial(scatter_kernel, most, row, start, first),
            name,
            most + n,
            [id_spec, negative_spec(1, width), stepped(dims, 2 * width), negative_spec(dims, 2 * width)],
            [(whole(rows, dims), shape((rows, dims), f32))] * parts,
            [],
            2 * parts * rows,
            (step_ids, negative_ids, grads, negative_grad),
        )

    away_other = scatter("away_other_kernel", 1, rows, n - 1, 0, away_grad)
    away_mine = scatter("away_mine_kernel", 1, 0, 1, 0, away_grad)
    away_total = away_mine[0]
    for k in range(1, n):
        away_total = away_total + exchange(away_other[k - 1], "sub", k)
    returned = exchange(away_total, "dom", pair)

    def to_chip(x, mask):
        pairs = []
        for d in range(n_dom):
            for s in range(n):
                pairs.append((d * n + s, (d ^ (mask // n * 2)) * n + (s ^ (mask % n))))
        return lax.ppermute(x, ("dom", "sub"), pairs)

    other_core = exchange(relation_part[chips], "dom", 1)
    parts = [relation_part[k] + other_core[k * chunk : (k + 1) * chunk] for k in range(chips)]
    chunk_total = parts[0]
    for k in range(1, chips):
        chunk_total = chunk_total + to_chip(parts[k], k)
    mask = 4
    while mask < n_dom:
        chunk_total = chunk_total + exchange(chunk_total, "dom", mask)
        mask *= 2
    mine = jnp.concatenate([chunk_total] + [to_chip(chunk_total, k) for k in range(1, chips)], axis=0)
    theirs = exchange(mine, "dom", 1)

    near_grad, away_total = lax.optimization_barrier((near_grad, away_total))
    near_sum = scatter("own_kernel", 0, 0, n, n, near_grad)

    new_table, new_state = pl.pallas_call(
        functools.partial(entity_kernel, n),
        in_specs=[in_vmem] * (3 + n),
        out_specs=[in_vmem] * 2,
        out_shape=[shape((rows, dims), f32), shape((1, rows), f32)],
        compiler_params=params,
        name="entity_kernel",
    )(
        entity_table,
        entity_state.reshape(1, rows),
        returned,
        near_sum[0],
        *(exchange(near_sum[k], "sub", k) for k in range(1, n)),
    )
    new_relations = pl.pallas_call(
        functools.partial(relation_kernel, chunk),
        in_specs=[in_smem] + [in_vmem] * 4,
        out_specs=in_vmem,
        out_shape=shape(relations.shape, f32),
        scratch_shapes=[pltpu.VMEM((rel_rows, dims), f32)],
        compiler_params=params,
        name="relation_kernel",
    )(codes, relations, relation_state.reshape(-1, 1), mine, theirs)
    return (new_table, new_state.reshape(rows), new_relations)


def solution(mesh):
    in_specs = (
        P(("dom", "sub"), None),
        P(("dom", "sub")),
        P(),
        P(),
        P("dom", "sub", None),
        P("dom", "sub", None),
        P("dom", "sub", None),
        P("dom", "sub", None),
        P("dom", "sub"),
    )
    out_specs = (P(("dom", "sub"), None), P(("dom", "sub")), P())
    return jax.shard_map(
        on_device, mesh=mesh, in_specs=in_specs, out_specs=out_specs, check_vma=False
    )
```

time: 134 us -> 149 us (1.11)
  Pallas kernels: 43.8 us -> 59.8 us
  other arithmetic: 8.15 us -> 1.85 us
  starting transfers between devices: 29.2 us -> 35.2 us
    pallas_call x3 -> x8, Pallas kernels: 41.1 us -> 57.1 us  [the longest x5 50.4 us: call(): pl.pallas_call(kernel, grid_spec=pltpu.PrefetchScalarGridSpec(num_scalar_...]
    ppermute x6, starting transfers between devices: 7.12 us -> 10.3 us  [to_chip(): return lax.ppermute(x, ('dom', 'sub'), pairs)]
    another operation x6 -> x1, other arithmetic: 3.62 us -> 0.65 us  [on_device(): codes = jnp.stack([me, me_sub * rows, chunk_code * chunk]).astype(i32)]
    ppermute x16 -> x13, starting transfers between devices: 22.1 us -> 25 us  [exchange(): lax.ppermute(x, axis, [(i, i ^ mask) for i in range(lax.axis_size(axis))])]
    ppermute x16 -> x13, waiting for transfers between devices: 39.1 us -> 41.2 us  [exchange(): lax.ppermute(x, axis, [(i, i ^ mask) for i in range(lax.axis_size(axis))])]
    ppermute x6, waiting for transfers between devices: 5.34 us -> 3.73 us  [to_chip(): return lax.ppermute(x, ('dom', 'sub'), pairs)]
    unnamed x23 -> x30, local copies, waits for them, and re-layouts: 3.62 us -> 3.73 us
  transfers between devices with their start and end apart: 22 -> 19, of which waited for: 10 -> 8; matrix products, arithmetic and copies ran while one was open for 7% -> 2% of each run, Pallas kernels for 9% -> 26%
where the time goes in v3:
time: 149 us; the launch traced here: 148 us
  Pallas kernels  59.8 us (40%)
  waiting for transfers between devices  44.9 us (30%)
  starting transfers between devices  35.2 us (24%)
  local copies, waits for them, and re-layouts  4.56 us (3%)
  other arithmetic  1.85 us (1%)
    pallas_call x5, Pallas kernels, call(): pl.pallas_call(kernel, grid_spec=pltpu.PrefetchScalarGridSpec(num_scalar_...  50.4 us
    ppermute x13, waiting for transfers between devices, exchange(): lax.ppermute(x, axis, [(i, i ^ mask) for i in range(lax.axis_size(axis))])  41.2 us
    ppermute x13, starting transfers between devices, exchange(): lax.ppermute(x, axis, [(i, i ^ mask) for i in range(lax.axis_size(axis))])  25 us
    ppermute x6, starting transfers between devices, to_chip(): return lax.ppermute(x, ('dom', 'sub'), pairs)  10.3 us
    unnamed x30, local copies, waits for them, and re-layouts  3.73 us
    ppermute x6, waiting for transfers between devices, to_chip(): return lax.ppermute(x, ('dom', 'sub'), pairs)  3.73 us
  transfers between devices with their start and end apart: 19, of which 8 were waited for; matrix products, arithmetic and copies ran while one was open for 2% of the time, Pallas kernels for 26%

profile of v3, /device:TPU:0, one launch (start us, length us, event | category | flops | bytes accessed | tf_op | source)
XLA Modules:
  0.0 147.8 jit_solution(14757577478097671745)
XLA Ops:
  1.3 1.9 %prep_kernel.1 = (bf16[256,512]{1,0:T(8,128)(2,1)}, s16[17,3,512]{2,1,0:T(4,128)(2,1)}) custom-call(s32[1,1]{1,0:T(1,128)S(6)} %copy.13.count, f32[512,256]{1,0:T(8,128)} %table.3, s32[1,8192]{1,0:T(1,128)} %bitcast.10, s32[1,8192]{1,0:T(1,128)} %bitcast.11, s32[1,8192]{1,0:T(1,128)} %bitcast.12, s32[1,512]{1,0:T(1,128)} %bitcast.13), custom_call_target="tpu_custom_call" | custom-call | tf_op jit(solution)/shard_map/prep_kernel/pallas_call | solution.py:258
  3.2 4.0 %collective-permute-start.4 = (bf16[256,512]{1,0:T(8,128)(2,1)}, bf16[256,512]{1,0:T(8,128)(2,1)S(1)}, u32[]{:S(2)}, u32[]{:S(2)}) collective-permute-start(bf16[256,512]{1,0:T(8,128)(2,1)} %get-tuple-element.27.refs_0_), channel_id=1, source_target_pairs={{0,16},{2,18},{4,20},{6,22},{8,24},{10,26},{12,28},{14,30},{16,0},... | collective-permute-start | bytes 786440 | tf_op jit(solution)/shard_map/ppermute | solution.py:222
  7.3 1.5 %collective-permute-start.3 = (bf16[256,512]{1,0:T(8,128)(2,1)}, bf16[256,512]{1,0:T(8,128)(2,1)S(1)}, u32[]{:S(2)}, u32[]{:S(2)}) collective-permute-start(bf16[256,512]{1,0:T(8,128)(2,1)} %get-tuple-element.27.refs_0_), channel_id=1, source_target_pairs={{0,1},{1,0},{2,3},{3,2},{4,5},{5,4},{6,7},{7,6},{8,9},{9,8},{10,11... | collective-permute-start | bytes 786440 | tf_op jit(solution)/shard_map/ppermute | solution.py:222
  8.8 0.3 collective-permute-start.1
  9.1 0.2 collective-permute-start
  9.3 13.1 %collective-permute-done.1.refs_2_ = s16[17,3,512]{2,1,0:T(4,128)(2,1)S(1)} collective-permute-done((s16[17,3,512]{2,1,0:T(4,128)(2,1)}, s16[17,3,512]{2,1,0:T(4,128)(2,1)S(1)}, u32[]{:S(2)}, u32[]{:S(2)}) %collective-permute-start.1) | collective-permute-done | bytes 52256 | tf_op jit(solution)/shard_map/ppermute | solution.py:222
  22.4 1.6 %collective-permute-start.2 = (s16[17,3,512]{2,1,0:T(4,128)(2,1)S(1)}, s16[17,3,512]{2,1,0:T(4,128)(2,1)S(1)}, u32[]{:S(2)}, u32[]{:S(2)}) collective-permute-start(s16[17,3,512]{2,1,0:T(4,128)(2,1)S(1)} %collective-permute-done.1.refs_2_), channel_id=1, source_target_pairs={{0,1},{1,0},{2,3},{3,2},{4,5},{5,4},{6,7},{7,6},{8,9},{9,8},{10,11... | collective-permute-start | bytes 156680 | tf_op jit(solution)/shard_map/ppermute | solution.py:222
  23.9 0.7 pad_add_fusion.codes
  24.6 0.0 collective-permute-done.refs_1_
  24.6 2.1 %collective-permute-done.2.refs_3_ = s16[17,3,512]{2,1,0:T(4,128)(2,1)S(1)} collective-permute-done((s16[17,3,512]{2,1,0:T(4,128)(2,1)S(1)}, s16[17,3,512]{2,1,0:T(4,128)(2,1)S(1)}, u32[]{:S(2)}, u32[]{:S(2)}) %collective-permute-start.2) | collective-permute-done | bytes 52256 | tf_op jit(solution)/shard_map/ppermute | solution.py:222
  26.7 0.0 copy-done.4
  26.7 0.0 copy-done.5
  26.7 0.6 copy-done.6
  27.3 2.5 %plan_kernel.1 = (s32[37]{0:T(128)}, s32[16,4,512]{2,1,0:T(4,128)}, s32[4,1,512]{2,1,0:T(1,128)}) custom-call(s32[3]{0:T(128)} %pad_add_fusion.codes, s16[17,3,512]{2,1,0:T(4,128)(2,1)} %get-tuple-element.23.refs_0_, s16[17,3,512]{2,1,0:T(4,128)(2,1)} %copy-done.5, s16[17,3,512]{2,1,0:T(4,128)(2,1)} %copy-done.4, s16[17,3,512]{2,1,0:T(4,128)(2,1)} %copy-done.6), custom_call_target="tpu_custom_call" | custom-call | tf_op jit(solution)/shard_map/plan_kernel/pallas_call | solution.py:281
  29.8 0.0 collective-permute-done.4.refs_2_
  29.9 0.0 copy-start.12
  29.9 1.6 %collective-permute-start.5 = (bf16[256,512]{1,0:T(8,128)(2,1)S(1)}, bf16[256,512]{1,0:T(8,128)(2,1)S(1)}, u32[]{:S(2)}, u32[]{:S(2)}) collective-permute-start(bf16[256,512]{1,0:T(8,128)(2,1)S(1)} %collective-permute-done.4.refs_2_), channel_id=1, source_target_pairs={{0,1},{1,0},{2,3},{3,2},{4,5},{5,4},{6,7},{7,6},{8,9},{9,8},{10,11... | collective-permute-start | bytes 786440 | tf_op jit(solution)/shard_map/ppermute | solution.py:222
  31.5 0.0 collective-permute-done.3.refs_1_
  31.5 0.7 copy-done.13
  32.2 7.6 %near_kernel.1 = (bf16[16,256,512]{2,1,0:T(8,128)(2,1)}, f32[16,256,512]{2,1,0:T(8,128)}) custom-call(s32[37]{0:T(128)} %get-tuple-element.24.plan, s32[16,4,512]{2,1,0:T(4,128)} %get-tuple-element.25.ids, f32[400,256]{1,0:T(8,128)} %relations.3, bf16[256,512]{1,0:T(8,128)(2,1)} %get-tuple-element.27.refs_0_, bf16[256,512]{1,0:T(8,128)(2,1)} %copy-done.13), custom_call_target="tpu_custom_call" | custom-call | flops 8589934592 | bytes 8388608 | tf_op jit(solution)/shard_map/near_kernel/pallas_call | solution.py:301
  39.8 0.0 collective-permute-done.5.refs_3_
  39.8 0.7 copy-done.14
  40.5 16.9 %edge_kernel.1 = (bf16[16,256,1024]{2,1,0:T(8,128)(2,1)}, bf16[16,256,1024]{2,1,0:T(8,128)(2,1)}, bf16[4,256,1024]{2,1,0:T(8,128)(2,1)}, f32[64,256]{1,0:T(8,128...) custom-call(s32[37]{0:T(128)} %get-tuple-element.24.plan, ...), custom_call_target="tpu_custom_call" | custom-call | flops 15032385536 | bytes 8388608 | tf_op jit(solution)/shard_map/edge_kernel/pallas_call | solution.py:301
  57.4 0.0 copy-start.7
  57.4 0.0 copy-start.8
  57.4 0.0 copy-start.9
  57.4 1.0 collective-permute-start.9
  58.4 8.2 %away_other_kernel.1 = f32[512,256]{1,0:T(8,128)} custom-call(s32[37]{0:T(128)} %get-tuple-element.24.plan, s32[16,4,512]{2,1,0:T(4,128)} %get-tuple-element.25.ids, s32[4,1,512]{2,1,0:T(1,128)} %get-tuple-element.26.negative_ids, bf16[16,256,1024]{2,1,0:T(8,128)(2,1)} %get-tuple-element.30.grads, bf16[4,256,1024]{2,1,0:T(8,128)(2,1)} %get-tuple-element.31.negative_grads), custom_call_target="tpu_custom_call" | custom-call | flops 4294967296 | bytes 8388608 | tf_op jit(solution)/shard_map/away_other_kernel/pallas_call | solution.py:301
  66.6 4.1 %collective-permute-start.6 = (f32[512,256]{1,0:T(8,128)}, f32[512,256]{1,0:T(8,128)S(1)}, u32[]{:S(2)}, u32[]{:S(2)}) collective-permute-start(f32[512,256]{1,0:T(8,128)} %away_other_kernel.1), channel_id=1, source_target_pairs={{0,1},{1,0},{2,3},{3,2},{4,5},{5,4},{6,7},{7,6},{8,9},{9,8},{10,11... | collective-permute-start | bytes 1572872 | tf_op jit(solution)/shard_map/ppermute | solution.py:222
  70.7 0.0 collective-permute-done.9
  70.7 0.0 copy-done.7
  70.8 0.1 collective-permute-start.10
  70.8 5.3 %collective-permute-start.11 = (f32[64,256]{1,0:T(8,128)S(1)}, f32[64,256]{1,0:T(8,128)S(1)}, u32[]{:S(2)}, u32[]{:S(2)}) collective-permute-start(f32[64,256]{1,0:T(8,128)S(1)} %get-tuple-element.45), channel_id=1, source_target_pairs={{0,4},{1,5},{2,6},{3,7},{4,0},{5,1},{6,2},{7,3},{8,12},{9,13},{10,... | collective-permute-start | bytes 196616 | tf_op jit(solution)/shard_map/ppermute | solution.py:382
  76.1 1.4 collective-permute-start.12
  77.5 8.2 %away_mine_kernel.1 = f32[512,256]{1,0:T(8,128)} custom-call(s32[37]{0:T(128)} %get-tuple-element.24.plan, s32[16,4,512]{2,1,0:T(4,128)} %get-tuple-element.25.ids, s32[4,1,512]{2,1,0:T(1,128)} %get-tuple-element.26.negative_ids, bf16[16,256,1024]{2,1,0:T(8,128)(2,1)} %get-tuple-element.30.grads, bf16[4,256,1024]{2,1,0:T(8,128)(2,1)} %get-tuple-element.31.negative_grads), custom_call_target="tpu_custom_call" | custom-call | flops 4294967296 | bytes 8388608 | tf_op jit(solution)/shard_map/away_mine_kernel/pallas_call | solution.py:301
  85.7 0.5 collective-permute-done.10
  86.2 0.0 collective-permute-done.11
  86.2 0.0 collective-permute-done.12
  86.3 3.2 %collective-permute-start.13 = (f32[64,256]{1,0:T(8,128)S(1)}, f32[64,256]{1,0:T(8,128)S(1)}, u32[]{:S(2)}, u32[]{:S(2)}) collective-permute-start(f32[64,256]{1,0:T(8,128)S(1)} %fusion.2), channel_id=1, source_target_pairs={{0,8},{2,10},{4,12},{6,14},{8,0},{10,2},{12,4},{14,6},{16,24},{18,... | collective-permute-start | bytes 196616 | tf_op jit(solution)/shard_map/ppermute | solution.py:222
  89.5 0.0 collective-permute-done.6
  89.5 1.1 add.42
  90.6 0.0 copy-start.11
  90.6 9.4 %own_kernel.1 = (f32[512,256]{1,0:T(8,128)}, f32[512,256]{1,0:T(8,128)}) custom-call(s32[37]{0:T(128)} %get-tuple-element.24.plan, s32[16,4,512]{2,1,0:T(4,128)} %get-tuple-element.25.ids, s32[4,1,512]{2,1,0:T(1,128)} %get-tuple-element.26.negative_ids, bf16[16,256,1024]{2,1,0:T(8,128)(2,1)} %get-tuple-element.33.grads, ...), custom_call_target="tpu_custom_call" | custom-call | flops 8589934592 | bytes 8388608 | tf_op jit(solution)/shard_map/own_kernel/pallas_call | solution.py:301
  100.1 0.5 collective-permute-start.8
  100.6 6.8 %collective-permute-start.7 = (f32[512,256]{1,0:T(8,128)S(1)}, f32[512,256]{1,0:T(8,128)S(1)}, u32[]{:S(2)}, u32[]{:S(2)}) collective-permute-start(f32[512,256]{1,0:T(8,128)S(1)} %add.42), channel_id=1, source_target_pairs={{0,16},{2,18},{4,20},{6,22},{8,24},{10,26},{12,28},{14,30},{16,0},... | collective-permute-start | bytes 1572872 | tf_op jit(solution)/shard_map/ppermute | solution.py:222
  107.4 0.0 collective-permute-done.13
  107.4 0.1 collective-permute-start.14
  107.5 25.3 %collective-permute-done.14 = f32[64,256]{1,0:T(8,128)S(1)} collective-permute-done((f32[64,256]{1,0:T(8,128)S(1)}, f32[64,256]{1,0:T(8,128)S(1)}, u32[]{:S(2)}, u32[]{:S(2)}) %collective-permute-start.14) | collective-permute-done | bytes 65568 | tf_op jit(solution)/shard_map/ppermute | solution.py:222
  132.8 0.1 collective-permute-start.15
  132.8 0.1 collective-permute-start.16
  132.9 3.4 %collective-permute-start.17 = (f32[64,256]{1,0:T(8,128)S(1)}, f32[64,256]{1,0:T(8,128)S(1)}, u32[]{:S(2)}, u32[]{:S(2)}) collective-permute-start(f32[64,256]{1,0:T(8,128)S(1)} %add.51), channel_id=1, source_target_pairs={{0,5},{1,4},{2,7},{3,6},{4,1},{5,0},{6,3},{7,2},{8,13},{9,12},{10,... | collective-permute-start | bytes 196616 | tf_op jit(solution)/shard_map/ppermute | solution.py:382
  136.3 0.8 collective-permute-done.15
  137.1 0.5 collective-permute-done.16
  137.6 1.9 %collective-permute-done.17 = f32[64,256]{1,0:T(8,128)S(1)} collective-permute-done((f32[64,256]{1,0:T(8,128)S(1)}, f32[64,256]{1,0:T(8,128)S(1)}, u32[]{:S(2)}, u32[]{:S(2)}) %collective-permute-start.17) | collective-permute-done | bytes 65568 | tf_op jit(solution)/shard_map/ppermute | solution.py:382
  139.6 0.1 collective-permute-start.18
  139.6 0.8 copy.12.state
  140.5 0.7 collective-permute-done.18.theirs
  141.2 0.7 copy-done.3
  141.9 2.3 %relation_kernel.1 = f32[400,256]{1,0:T(8,128)} custom-call(s32[3]{0:T(128)} %pad_add_fusion.codes, f32[400,256]{1,0:T(8,128)} %relations.3, f32[400,1]{1,0:T(8,128)} %copy.12.state, f32[256,256]{1,0:T(8,128)} %copy-done, f32[256,256]{1,0:T(8,128)} %copy-done.3), custom_call_target="tpu_custom_call" | custom-call | tf_op jit(solution)/shard_map/relation_kernel/pallas_call | solution.py:413
  144.2 0.0 collective-permute-done.8.refs_1_
  144.2 0.0 collective-permute-done.7.returned
  144.2 0.8 copy-done.1
  145.0 0.2 copy-done.2
  145.2 2.7 %entity_kernel.1 = (f32[512,256]{1,0:T(8,128)}, f32[1,512]{1,0:T(1,128)}) custom-call(f32[512,256]{1,0:T(8,128)} %table.3, f32[1,512]{1,0:T(1,128)} %bitcast.15, f32[512,256]{1,0:T(8,128)} %copy-done.2, f32[512,256]{1,0:T(8,128)} %get-tuple-element.34.refs_0_, f32[512,256]{1,0:T(8,128)} %copy-done.1), custom_call_target="tpu_custom_call" | custom-call | tf_op jit(solution)/shard_map/entity_kernel/pallas_call | solution.py:399
  (21 shorter events, 0.1 us)
Async XLA Ops:
  3.2 26.6 %collective-permute-start.4 = (bf16[256,512]{1,0:T(8,128)(2,1)}, bf16[256,512]{1,0:T(8,128)(2,1)S(1)}, u32[]{:S(2)}, u32[]{:S(2)}) collective-permute-start(bf16[256,512]{1,0:T(8,128)(2,1)} %get-tuple-element.27.refs_0_), channel_id=1, source_target_pairs={{0,16},{2,18},{4,20},{6,22},{8,24},{10,26},{12,28},{14,30},{16,0},... | collective-permute-start | bytes 786440 | tf_op jit(solution)/shard_map/ppermute | solution.py:222
  7.3 24.2 %collective-permute-start.3 = (bf16[256,512]{1,0:T(8,128)(2,1)}, bf16[256,512]{1,0:T(8,128)(2,1)S(1)}, u32[]{:S(2)}, u32[]{:S(2)}) collective-permute-start(bf16[256,512]{1,0:T(8,128)(2,1)} %get-tuple-element.27.refs_0_), channel_id=1, source_target_pairs={{0,1},{1,0},{2,3},{3,2},{4,5},{5,4},{6,7},{7,6},{8,9},{9,8},{10,11... | collective-permute-start | bytes 786440 | tf_op jit(solution)/shard_map/ppermute | solution.py:222
  8.8 13.6 %collective-permute-start.1 = (s16[17,3,512]{2,1,0:T(4,128)(2,1)}, s16[17,3,512]{2,1,0:T(4,128)(2,1)S(1)}, u32[]{:S(2)}, u32[]{:S(2)}) collective-permute-start(s16[17,3,512]{2,1,0:T(4,128)(2,1)} %get-tuple-element.23.refs_0_), channel_id=1, source_target_pairs={{0,16},{2,18},{4,20},{6,22},{8,24},{10,26},{12,28},{14,30},{16,0},... | collective-permute-start | bytes 156680 | tf_op jit(solution)/shard_map/ppermute | solution.py:222
  9.1 15.5 %collective-permute-start = (s16[17,3,512]{2,1,0:T(4,128)(2,1)}, s16[17,3,512]{2,1,0:T(4,128)(2,1)S(1)}, u32[]{:S(2)}, u32[]{:S(2)}) collective-permute-start(s16[17,3,512]{2,1,0:T(4,128)(2,1)} %get-tuple-element.23.refs_0_), channel_id=1, source_target_pairs={{0,1},{1,0},{2,3},{3,2},{4,5},{5,4},{6,7},{7,6},{8,9},{9,8},{10,11... | collective-permute-start | bytes 156680 | tf_op jit(solution)/shard_map/ppermute | solution.py:222
  22.4 4.3 %copy-start.4 = (s16[17,3,512]{2,1,0:T(4,128)(2,1)}, s16[17,3,512]{2,1,0:T(4,128)(2,1)S(1)}, u32[]{:S(2)}) copy-start(s16[17,3,512]{2,1,0:T(4,128)(2,1)S(1)} %collective-permute-done.1.refs_2_) | copy-start | bytes 156676
  22.4 4.3 %collective-permute-start.2 = (s16[17,3,512]{2,1,0:T(4,128)(2,1)S(1)}, s16[17,3,512]{2,1,0:T(4,128)(2,1)S(1)}, u32[]{:S(2)}, u32[]{:S(2)}) collective-permute-start(s16[17,3,512]{2,1,0:T(4,128)(2,1)S(1)} %collective-permute-done.1.refs_2_), channel_id=1, source_target_pairs={{0,1},{1,0},{2,3},{3,2},{4,5},{5,4},{6,7},{7,6},{8,9},{9,8},{10,11... | collective-permute-start | bytes 156680 | tf_op jit(solution)/shard_map/ppermute | solution.py:222
  24.6 2.1 %copy-start.5 = (s16[17,3,512]{2,1,0:T(4,128)(2,1)}, s16[17,3,512]{2,1,0:T(4,128)(2,1)S(1)}, u32[]{:S(2)}) copy-start(s16[17,3,512]{2,1,0:T(4,128)(2,1)S(1)} %collective-permute-done.refs_1_) | copy-start | bytes 156676
  26.7 0.6 copy-start.6
  29.9 9.9 %copy-start.12 = (bf16[256,512]{1,0:T(8,128)(2,1)}, bf16[256,512]{1,0:T(8,128)(2,1)S(1)}, u32[]{:S(2)}) copy-start(bf16[256,512]{1,0:T(8,128)(2,1)S(1)} %collective-permute-done.4.refs_2_) | copy-start | bytes 786436
  29.9 9.9 %collective-permute-start.5 = (bf16[256,512]{1,0:T(8,128)(2,1)S(1)}, bf16[256,512]{1,0:T(8,128)(2,1)S(1)}, u32[]{:S(2)}, u32[]{:S(2)}) collective-permute-start(bf16[256,512]{1,0:T(8,128)(2,1)S(1)} %collective-permute-done.4.refs_2_), channel_id=1, source_target_pairs={{0,1},{1,0},{2,3},{3,2},{4,5},{5,4},{6,7},{7,6},{8,9},{9,8},{10,11... | collective-permute-start | bytes 786440 | tf_op jit(solution)/shard_map/ppermute | solution.py:222
  31.5 0.7 copy-start.13
  39.8 0.7 copy-start.14
  57.4 13.3 %copy-start.7 = (f32[64,256]{1,0:T(8,128)S(1)}, f32[64,256]{1,0:T(8,128)}, u32[]{:S(2)}) copy-start(f32[64,256]{1,0:T(8,128)} %get-tuple-element.40) | copy-start | bytes 196612
  57.4 13.3 %copy-start.8 = (f32[64,256]{1,0:T(8,128)S(1)}, f32[64,256]{1,0:T(8,128)}, u32[]{:S(2)}) copy-start(f32[64,256]{1,0:T(8,128)} %get-tuple-element.41) | copy-start | bytes 196612
  57.4 13.3 %copy-start.9 = (f32[64,256]{1,0:T(8,128)S(1)}, f32[64,256]{1,0:T(8,128)}, u32[]{:S(2)}) copy-start(f32[64,256]{1,0:T(8,128)} %get-tuple-element.42) | copy-start | bytes 196612
  57.4 13.3 %collective-permute-start.9 = (f32[256,256]{1,0:T(8,128)}, f32[256,256]{1,0:T(8,128)S(1)}, u32[]{:S(2)}, u32[]{:S(2)}) collective-permute-start(f32[256,256]{1,0:T(8,128)} %get-tuple-element.39), channel_id=1, source_target_pairs={{0,2},{2,0},{4,6},{6,4},{8,10},{10,8},{12,14},{14,12},{16,18},{18,... | collective-permute-start | bytes 786440 | tf_op jit(solution)/shard_map/ppermute | solution.py:222
  66.6 19.6 %copy-start.10 = (f32[64,256]{1,0:T(8,128)S(1)}, f32[64,256]{1,0:T(8,128)}, u32[]{:S(2)}) copy-start(f32[64,256]{1,0:T(8,128)} %get-tuple-element.38) | copy-start | bytes 196612
  66.6 22.9 %collective-permute-start.6 = (f32[512,256]{1,0:T(8,128)}, f32[512,256]{1,0:T(8,128)S(1)}, u32[]{:S(2)}, u32[]{:S(2)}) collective-permute-start(f32[512,256]{1,0:T(8,128)} %away_other_kernel.1), channel_id=1, source_target_pairs={{0,1},{1,0},{2,3},{3,2},{4,5},{5,4},{6,7},{7,6},{8,9},{9,8},{10,11... | collective-permute-start | bytes 1572872 | tf_op jit(solution)/shard_map/ppermute | solution.py:222
  70.8 15.5 %collective-permute-start.10 = (f32[64,256]{1,0:T(8,128)S(1)}, f32[64,256]{1,0:T(8,128)S(1)}, u32[]{:S(2)}, u32[]{:S(2)}) collective-permute-start(f32[64,256]{1,0:T(8,128)S(1)} %get-tuple-element.43), channel_id=1, source_target_pairs={{0,1},{1,0},{2,3},{3,2},{4,5},{5,4},{6,7},{7,6},{8,9},{9,8},{10,11... | collective-permute-start | bytes 196616 | tf_op jit(solution)/shard_map/ppermute | solution.py:382
  70.8 15.4 %collective-permute-start.11 = (f32[64,256]{1,0:T(8,128)S(1)}, f32[64,256]{1,0:T(8,128)S(1)}, u32[]{:S(2)}, u32[]{:S(2)}) collective-permute-start(f32[64,256]{1,0:T(8,128)S(1)} %get-tuple-element.45), channel_id=1, source_target_pairs={{0,4},{1,5},{2,6},{3,7},{4,0},{5,1},{6,2},{7,3},{8,12},{9,13},{10,... | collective-permute-start | bytes 196616 | tf_op jit(solution)/shard_map/ppermute | solution.py:382
  76.1 10.1 %collective-permute-start.12 = (f32[64,256]{1,0:T(8,128)S(1)}, f32[64,256]{1,0:T(8,128)S(1)}, u32[]{:S(2)}, u32[]{:S(2)}) collective-permute-start(f32[64,256]{1,0:T(8,128)S(1)} %get-tuple-element.44), channel_id=1, source_target_pairs={{0,5},{1,4},{2,7},{3,6},{4,1},{5,0},{6,3},{7,2},{8,13},{9,12},{10,... | collective-permute-start | bytes 196616 | tf_op jit(solution)/shard_map/ppermute | solution.py:382
  86.3 21.1 %collective-permute-start.13 = (f32[64,256]{1,0:T(8,128)S(1)}, f32[64,256]{1,0:T(8,128)S(1)}, u32[]{:S(2)}, u32[]{:S(2)}) collective-permute-start(f32[64,256]{1,0:T(8,128)S(1)} %fusion.2), channel_id=1, source_target_pairs={{0,8},{2,10},{4,12},{6,14},{8,0},{10,2},{12,4},{14,6},{16,24},{18,... | collective-permute-start | bytes 196616 | tf_op jit(solution)/shard_map/ppermute | solution.py:222
  90.6 49.0 %copy-start.11 = (f32[400]{0:T(512)S(1)}, f32[400]{0:T(512)}, u32[]{:S(2)}) copy-start(f32[400]{0:T(512)} %param.12) | copy-start | bytes 4804
  100.1 44.1 %collective-permute-start.8 = (f32[512,256]{1,0:T(8,128)}, f32[512,256]{1,0:T(8,128)S(1)}, u32[]{:S(2)}, u32[]{:S(2)}) collective-permute-start(f32[512,256]{1,0:T(8,128)} %get-tuple-element.35), channel_id=1, source_target_pairs={{0,1},{1,0},{2,3},{3,2},{4,5},{5,4},{6,7},{7,6},{8,9},{9,8},{10,11... | collective-permute-start | bytes 1572872 | tf_op jit(solution)/shard_map/ppermute | solution.py:222
  100.6 43.6 %collective-permute-start.7 = (f32[512,256]{1,0:T(8,128)S(1)}, f32[512,256]{1,0:T(8,128)S(1)}, u32[]{:S(2)}, u32[]{:S(2)}) collective-permute-start(f32[512,256]{1,0:T(8,128)S(1)} %add.42), channel_id=1, source_target_pairs={{0,16},{2,18},{4,20},{6,22},{8,24},{10,26},{12,28},{14,30},{16,0},... | collective-permute-start | bytes 1572872 | tf_op jit(solution)/shard_map/ppermute | solution.py:222
  107.4 25.4 %collective-permute-start.14 = (f32[64,256]{1,0:T(8,128)S(1)}, f32[64,256]{1,0:T(8,128)S(1)}, u32[]{:S(2)}, u32[]{:S(2)}) collective-permute-start(f32[64,256]{1,0:T(8,128)S(1)} %add.50), channel_id=1, source_target_pairs={{0,16},{2,18},{4,20},{6,22},{8,24},{10,26},{12,28},{14,30},{16,0},... | collective-permute-start | bytes 196616 | tf_op jit(solution)/shard_map/ppermute | solution.py:222
  132.8 4.3 %collective-permute-start.15 = (f32[64,256]{1,0:T(8,128)S(1)}, f32[64,256]{1,0:T(8,128)S(1)}, u32[]{:S(2)}, u32[]{:S(2)}) collective-permute-start(f32[64,256]{1,0:T(8,128)S(1)} %add.51), channel_id=1, source_target_pairs={{0,1},{1,0},{2,3},{3,2},{4,5},{5,4},{6,7},{7,6},{8,9},{9,8},{10,11... | collective-permute-start | bytes 196616 | tf_op jit(solution)/shard_map/ppermute | solution.py:382
  132.8 4.8 %collective-permute-start.16 = (f32[64,256]{1,0:T(8,128)S(1)}, f32[64,256]{1,0:T(8,128)S(1)}, u32[]{:S(2)}, u32[]{:S(2)}) collective-permute-start(f32[64,256]{1,0:T(8,128)S(1)} %add.51), channel_id=1, source_target_pairs={{0,4},{1,5},{2,6},{3,7},{4,0},{5,1},{6,2},{7,3},{8,12},{9,13},{10,... | collective-permute-start | bytes 196616 | tf_op jit(solution)/shard_map/ppermute | solution.py:382
  132.9 6.6 %collective-permute-start.17 = (f32[64,256]{1,0:T(8,128)S(1)}, f32[64,256]{1,0:T(8,128)S(1)}, u32[]{:S(2)}, u32[]{:S(2)}) collective-permute-start(f32[64,256]{1,0:T(8,128)S(1)} %add.51), channel_id=1, source_target_pairs={{0,5},{1,4},{2,7},{3,6},{4,1},{5,0},{6,3},{7,2},{8,13},{9,12},{10,... | collective-permute-start | bytes 196616 | tf_op jit(solution)/shard_map/ppermute | solution.py:382
  139.5 1.6 %copy-start = (f32[256,256]{1,0:T(8,128)}, f32[256,256]{1,0:T(8,128)S(1)}, u32[]{:S(2)}) copy-start(f32[256,256]{1,0:T(8,128)S(1)} %pad_maximum_fusion.mine) | copy-start | bytes 786436
  139.6 1.6 %collective-permute-start.18 = (f32[256,256]{1,0:T(8,128)S(1)}, f32[256,256]{1,0:T(8,128)S(1)}, u32[]{:S(2)}, u32[]{:S(2)}) collective-permute-start(f32[256,256]{1,0:T(8,128)S(1)} %pad_maximum_fusion.mine), channel_id=1, source_target_pairs={{0,2},{2,0},{4,6},{6,4},{8,10},{10,8},{12,14},{14,12},{16,18},{18,... | collective-permute-start | bytes 786440 | tf_op jit(solution)/shard_map/ppermute | solution.py:222
  141.2 0.7 copy-start.3
  144.2 0.8 copy-start.1
  144.2 1.0 copy-start.2

commit v4 on v3

v4 whole, which is shorter than its diff:
```python
import functools

import jax
import jax.numpy as jnp
from jax import lax
from jax.experimental import pallas as pl
from jax.experimental.pallas import tpu as pltpu
from jax.sharding import PartitionSpec as P

learn_rate = 0.1
bf16 = jnp.bfloat16
f32 = jnp.float32
i32 = jnp.int32
params = pltpu.CompilerParams(vmem_limit_bytes=10 * 2**20)


def dot(a, b):
    return jnp.dot(a, b, preferred_element_type=f32)


def dot_nt(a, b):
    return lax.dot_general(a, b, (((1,), (1,)), ((), ())), preferred_element_type=f32)


def one_hot(ids, rows):
    places = lax.broadcasted_iota(jnp.int16, (rows, ids.shape[1]), 0)
    return jnp.where(places == ids.astype(jnp.int16), jnp.ones((), bf16), jnp.zeros((), bf16))


def split(x):
    high = x.astype(bf16)
    return jnp.concatenate([high, (x - high.astype(f32)).astype(bf16)], axis=0)


def gather(pieces, ids):
    rows = pieces[0].shape[1]
    hot = one_hot(ids, len(pieces) * rows)
    total = dot(pieces[0][...], hot[:rows])
    for k in range(1, len(pieces)):
        total = total + dot(pieces[k][...], hot[k * rows : (k + 1) * rows])
    return total


def scatter_add(pieces, ids, pair):
    dims = pair.shape[0] // 2
    hot = one_hot(ids, sum(piece.shape[0] for piece in pieces))
    start = 0
    for piece in pieces:
        part = hot[start : start + piece.shape[0]]
        piece[...] += dot_nt(part, pair[:dims]) + dot_nt(part, pair[dims:])
        start += piece.shape[0]


def add_negatives(pieces, ids, pair):
    count = pair.shape[0] // 2
    hot = one_hot(ids, sum(piece.shape[0] for piece in pieces))
    start = 0
    for piece in pieces:
        part = hot[start : start + piece.shape[0]]
        piece[...] += dot(part, pair[:count]) + dot(part, pair[count:])
        start += piece.shape[0]


def prep_kernel(count, table, heads, tails, kinds, negatives, *refs):
    rows_out, ids_out = refs[:-1], refs[-1]
    each = rows_out[0].shape[1]
    for k, out in enumerate(rows_out):
        out[...] = table[k * each : (k + 1) * each, :].T.astype(bf16)
    blocks, _, width = ids_out.shape
    for j in range(blocks - 1):
        at = slice(j * width, (j + 1) * width)
        block = jnp.concatenate([heads[:, at], tails[:, at], kinds[:, at]], axis=0)
        ids_out[j] = block.astype(jnp.int16)
    last = jnp.concatenate([negatives[...], jnp.full((2, width), count[0, 0], i32)], axis=0)
    ids_out[blocks - 1] = last.astype(jnp.int16)


def plan_kernel(n, codes, *refs):
    sources, (plan, step_ids, negative_ids) = refs[:-3], refs[-3:]
    team = len(sources)
    most, _, width = step_ids.shape
    me = codes[0]
    counts, blocks = [], []
    for k, ids in enumerate(sources):
        last = ids[most].astype(i32)
        counts.append(jnp.max(last[1:2]))
        blocks.append(lax.div(counts[k] + (width - 1), i32(width)))
        negative_ids[k] = last[0:1] ^ codes[1]
    total = sum(blocks)
    low = lax.div(me * total, i32(team))
    high = lax.div((me + 1) * total, i32(team))
    plan[2 * most] = high - low
    before = []
    for k in range(team):
        ahead = [jnp.where((me ^ j) < (me ^ k), blocks[j], 0) for j in range(team) if j != k]
        before.append(sum(ahead))
        seen = (before[k] < high) & (before[k] + blocks[k] > low)
        plan[2 * most + 1 + k] = seen.astype(i32)

    def one_step(i, carry):
        line = jnp.minimum(low + i, high - 1)
        for k, ids in enumerate(sources):

            @pl.when((line >= before[k]) & (line < before[k] + blocks[k]))
            def _(k=k, ids=ids):
                nth = line - before[k]
                plan[i] = k
                plan[most + i] = jnp.clip(counts[k] - nth * width, 0, width)
                entries = ids[nth].astype(i32)
                near, away = (0, 1) if k < n else (1, 0)
                step_ids[i, 0:1] = entries[near : near + 1] ^ codes[1]
                step_ids[i, 1:2] = entries[away : away + 1] ^ codes[1]
                step_ids[i, 2:3] = entries[2:3]
                step_ids[i, 3:4] = entries[2:3] ^ codes[2]

        return carry

    lax.fori_loop(0, most, one_step, 0)


def near_kernel(plan, ids, relations, *refs):
    slab, (rows_out, operator_out, rel_full, rel_split) = refs[:-4], refs[-4:]
    dims = relations.shape[1]
    rel_full[...] = jnp.zeros_like(rel_full)
    rel_full[: relations.shape[0], :] = relations[...]
    rel_split[...] = split(rel_full[...].T)

    def one_block(i, carry):
        entries = ids[i]
        rows_out[i] = gather(slab, entries[0:1]).astype(bf16)
        both = dot(rel_split[...], one_hot(entries[2:3], rel_full.shape[0]))
        operator_out[i] = both[:dims] + both[dims:]
        return carry

    lax.fori_loop(0, plan[2 * ids.shape[0]], one_block, 0)


def edge_kernel(n, parts, plan, ids, negative_ids, near_in, operator_in, *refs):
    near, away = refs[:parts], refs[parts : 2 * parts]
    near_grad, away_grad, negative_out = refs[2 * parts : 2 * parts + 3]
    away_other = refs[2 * parts + 3 : 2 * parts + 2 + n]
    relation_sum, (table, table_t, negative_grad) = refs[2 * parts + 2 + n : -3], refs[-3:]
    most, _, width = ids.shape
    steps = plan[2 * most]
    count = table.shape[0]
    for piece in (*away_other, *relation_sum):
        piece[...] = jnp.zeros_like(piece)
    rows = sum(piece.shape[1] for piece in away) // n

    def one_block(i, carry):
        here = plan[i]
        swapped = here >= n

        def take_table(slab):
            found = gather(slab, negative_ids[here])
            table_t[...] = found.astype(bf16)
            table[...] = found.T.astype(bf16)
            negative_grad[...] = jnp.zeros_like(negative_grad)

        fresh = (i == 0) | (plan[jnp.maximum(i - 1, 0)] != here)
        pl.when(fresh & ~swapped)(lambda: take_table(away))
        pl.when(fresh & swapped)(lambda: take_table(near))

        entries = ids[i]
        alive = (lax.broadcasted_iota(i32, (1, width), 1) < plan[most + i]).astype(f32)
        near_rows = near_in[i].astype(f32)
        away_rows = gather(away, entries[1:2])
        head = jnp.where(swapped, away_rows, near_rows)
        tail = jnp.where(swapped, near_rows, away_rows)
        operator = operator_in[i]
        query = head * operator
        query_b = query.astype(bf16)
        positive = jnp.sum(query * tail, axis=0, keepdims=True)
        scores = dot(table[...], query_b)
        pos_coef = -jax.nn.sigmoid(-positive) * alive
        neg_coef = (jax.nn.sigmoid(scores) * (alive * (1.0 / count))).astype(bf16)
        query_grad = pos_coef * tail + dot(table_t[...], neg_coef)
        negative_grad[...] += dot_nt(neg_coef, query_b)
        head_grad = query_grad * operator
        tail_grad = pos_coef * query
        near_grad[i] = split(jnp.where(swapped, tail_grad, head_grad))
        away_pair = split(jnp.where(swapped, head_grad, tail_grad))
        away_grad[i] = away_pair
        scatter_add(away_other, entries[1:2] - rows, away_pair)
        scatter_add(relation_sum, entries[3:4], split(query_grad * head))

        ends = (i == steps - 1) | (plan[jnp.minimum(i + 1, steps - 1)] != here)

        @pl.when(ends)
        def _():
            negative_out[here] = split(negative_grad[...])

        @pl.when(ends & ~swapped)
        def _():
            add_negatives(away_other, negative_ids[here] - rows, negative_out[here])

        return carry

    lax.fori_loop(0, steps, one_block, 0)


def scatter_kernel(row, first, plan, ids, negative_ids, grads, negative_grads, *sums):
    most = ids.shape[0]
    for piece in sums:
        piece[...] = jnp.zeros_like(piece)

    def one_block(i, carry):
        scatter_add(sums, ids[i][row : row + 1], grads[i])
        return carry

    lax.fori_loop(0, plan[2 * most], one_block, 0)
    for k in range(first, first + negative_ids.shape[0] // 2):

        @pl.when(plan[2 * most + 1 + k] != 0)
        def _(k=k):
            add_negatives(sums, negative_ids[k], negative_grads[k])


def entity_kernel(n, table, state, returned, *refs):
    parts, (new_table, new_state) = refs[:n], refs[n:]
    grad = returned[...]
    for part in parts:
        grad = grad + part[...]
    lanes = 128
    before = jnp.broadcast_to(state[...], (lanes, table.shape[0])).T[:, :1]
    after = before + jnp.mean(grad * grad, axis=-1, keepdims=True)
    new_table[...] = table[...] - learn_rate * grad / jnp.sqrt(after)
    new_state[...] = jnp.broadcast_to(after, (table.shape[0], lanes)).T[:1]


def relation_kernel(chunk, codes, relations, state, mine, theirs, out, grad, column):
    chunks = mine.shape[0] // chunk
    for k in range(2 * chunks):
        part = (mine, theirs)[k // chunks]
        start = (k % chunks) * chunk
        grad[pl.ds(pl.multiple_of(codes[2] ^ (k * chunk), chunk), chunk), :] = part[start : start + chunk, :]
    count = relations.shape[0]
    column[...] = jnp.ones_like(column)
    column[:, :count] = jnp.broadcast_to(state[...], (column.shape[0], count))
    g = grad[:count, :]
    total = column[...].T[:count, :1] + jnp.mean(g * g, axis=-1, keepdims=True)
    out[...] = relations[...] - learn_rate * g / jnp.sqrt(total)


def exchange(x, axis, mask):
    return lax.ppermute(x, axis, [(i, i ^ mask) for i in range(lax.axis_size(axis))])


def on_device(
    entity_table,
    entity_state,
    relations,
    relation_state,
    head_rows,
    tail_rows,
    relation_ids,
    negative_rows,
    edge_counts,
):
    n = lax.axis_size("sub")
    n_dom = lax.axis_size("dom")
    me_sub = lax.axis_index("sub")
    me_dom = lax.axis_index("dom")
    pair = n_dom // 2
    team = 2 * n
    rows, dims = entity_table.shape
    slots = head_rows.shape[2]
    count = negative_rows.shape[2]
    width = count
    most = slots // width
    rel_rows = -(-relations.shape[0] // 256) * 256
    chips = 2 * n
    chunk = rel_rows // (2 * chips)
    me = lax.shift_right_logical(me_dom, pair.bit_length() - 1) * n + me_sub
    chunk_code = (me_dom & 1) * chips + ((me_dom >> 1) & 1) * n + me_sub
    codes = jnp.stack([me, me_sub * rows, chunk_code * chunk]).astype(i32)

    in_vmem = pl.BlockSpec(memory_space=pltpu.VMEM)
    in_smem = pl.BlockSpec(memory_space=pltpu.SMEM)

    def call(kernel, name, outs, scratch, unit, scalars, arrays, held=True):
        place = (lambda x, t: pltpu.VMEM(x, t)) if held else jax.ShapeDtypeStruct
        return pl.pallas_call(
            kernel,
            in_specs=[in_smem] * len(scalars) + [in_vmem] * len(arrays),
            out_specs=[in_vmem] * len(outs),
            out_shape=[place(x, t) for x, t in outs],
            scratch_shapes=scratch,
            compiler_params=params,
            cost_estimate=pl.CostEstimate(flops=slots * dims * unit, bytes_accessed=slots * dims, transcendentals=0),
            name=name,
        )(*scalars, *(pltpu.with_memory_space_constraint(x, pltpu.VMEM) for x in arrays))

    halves = 2
    *local, ids = call(
        prep_kernel,
        "prep_kernel",
        [((dims, rows // halves), bf16)] * halves + [((most + 1, 3, width), jnp.int16)],
        [],
        1,
        (edge_counts,),
        (
            entity_table,
            head_rows.reshape(1, slots),
            tail_rows.reshape(1, slots),
            relation_ids.reshape(1, slots),
            negative_rows.reshape(1, count),
        ),
    )

    def along_sub(x):
        return [x] + [exchange(x, "sub", k) for k in range(1, n)]

    def in_order(pieces):
        return [piece[k] for k in range(n) for piece in pieces]

    all_ids = along_sub(ids) + along_sub(exchange(ids, "dom", pair))
    away_slab = in_order([along_sub(exchange(x, "dom", pair)) for x in local])
    near_slab = in_order([along_sub(x) for x in local])
    parts = n * halves

    plan, step_ids, negative_ids = pl.pallas_call(
        functools.partial(plan_kernel, n),
        in_specs=[in_smem] + [in_vmem] * team,
        out_specs=[in_smem, in_vmem, in_vmem],
        out_shape=[
            jax.ShapeDtypeStruct((2 * most + 1 + team,), i32),
            pltpu.VMEM((most, 4, width), i32),
            pltpu.VMEM((team, 1, width), i32),
        ],
        compiler_params=params,
        name="plan_kernel",
    )(codes, *(pltpu.with_memory_space_constraint(x, pltpu.VMEM) for x in all_ids))

    near_rows, operator = call(
        near_kernel,
        "near_kernel",
        [((most, dims, width), bf16), ((most, dims, width), f32)],
        [pltpu.VMEM((rel_rows, dims), f32), pltpu.VMEM((2 * dims, rel_rows), bf16)],
        n * rows + 2 * rel_rows,
        (plan,),
        (step_ids, relations, *near_slab),
    )
    sums = ((rows, dims), f32)
    pair_out = ((most, 2 * dims, width), bf16)
    near_grad, away_grad, negative_grad, *found = call(
        functools.partial(edge_kernel, n, parts),
        "edge_kernel",
        [pair_out, pair_out, ((team, 2 * count, dims), bf16)]
        + [sums] * (n - 1)
        + [((chunk, dims), f32)] * chips
        + [((chips * chunk, dims), f32)],
        [pltpu.VMEM((count, dims), bf16), pltpu.VMEM((dims, count), bf16), pltpu.VMEM((count, dims), f32)],
        (2 * n - 1) * rows + 3 * count + 2 * rel_rows,
        (plan,),
        (step_ids, negative_ids, near_rows, operator, *near_slab, *away_slab),
    )
    away_other, relation_part = found[: n - 1], found[n - 1 :]
    (away_total,) = call(
        functools.partial(scatter_kernel, 1, 0),
        "away_kernel",
        [sums],
        [],
        2 * rows,
        (plan,),
        (step_ids, negative_ids, away_grad, negative_grad),
    )
    for k in range(1, n):
        away_total = away_total + exchange(away_other[k - 1], "sub", k)

    def to_chip(x, mask):
        pairs = []
        for d in range(n_dom):
            for s in range(n):
                pairs.append((d * n + s, (d ^ (mask // n * 2)) * n + (s ^ (mask % n))))
        return lax.ppermute(x, ("dom", "sub"), pairs)

    other_core = exchange(relation_part[chips], "dom", 1)
    partial = [relation_part[k] + other_core[k * chunk : (k + 1) * chunk] for k in range(chips)]
    chunk_total = partial[0]
    for k in range(1, chips):
        chunk_total = chunk_total + to_chip(partial[k], k)
    mask = 4
    while mask < n_dom:
        chunk_total = chunk_total + exchange(chunk_total, "dom", mask)
        mask *= 2

    plan, away_total, chunk_total = lax.optimization_barrier((plan, away_total, chunk_total))
    returned = exchange(away_total, "dom", pair)
    mine = jnp.concatenate([chunk_total] + [to_chip(chunk_total, k) for k in range(1, chips)], axis=0)
    theirs = exchange(mine, "dom", 1)
    near_sum = call(
        functools.partial(scatter_kernel, 0, n),
        "own_kernel",
        [sums] * n,
        [],
        2 * n * rows,
        (plan,),
        (step_ids, negative_ids, near_grad, negative_grad),
    )
    near_sum = [near_sum[0]] + [exchange(near_sum[k], "sub", k) for k in range(1, n)]
    (new_relations,) = call(
        functools.partial(relation_kernel, chunk),
        "relation_kernel",
        [(relations.shape, f32)],
        [pltpu.VMEM((rel_rows, dims), f32), pltpu.VMEM((128, rel_rows), f32)],
        1,
        (codes,),
        (relations, relation_state.reshape(1, -1), mine, theirs),
        held=False,
    )
    new_table, new_state = call(
        functools.partial(entity_kernel, n),
        "entity_kernel",
        [((rows, dims), f32), ((1, rows), f32)],
        [],
        1,
        (),
        (entity_table, entity_state.reshape(1, rows), returned, *near_sum),
        held=False,
    )
    return (new_table, new_state.reshape(rows), new_relations)


def solution(mesh):
    in_specs = (
        P(("dom", "sub"), None),
        P(("dom", "sub")),
        P(),
        P(),
        P("dom", "sub", None),
        P("dom", "sub", None),
        P("dom", "sub", None),
        P("dom", "sub", None),
        P("dom", "sub"),
    )
    out_specs = (P(("dom", "sub"), None), P(("dom", "sub")), P())
    return jax.shard_map(
        on_device, mesh=mesh, in_specs=in_specs, out_specs=out_specs, check_vma=False
    )
```

time: 149 us -> 111 us (0.74)
  Pallas kernels: 59.8 us -> 30.5 us
  waiting for transfers between devices: 44.9 us -> 37.1 us
  other arithmetic: 1.85 us -> 0.21 us
    pallas_call x8 -> x7, Pallas kernels: 57.3 us -> 28.5 us  [call(): pl.pallas_call(kernel, in_specs=[in_smem] * len(scalars) + [in_vmem] * le...]
    ppermute x13 -> x16, waiting for transfers between devices: 41.2 us -> 34.9 us  [exchange(): lax.ppermute(x, axis, [(i, i ^ mask) for i in range(lax.axis_size(axis))])]
    ppermute x13 -> x16, starting transfers between devices: 25 us -> 28 us  [exchange(): lax.ppermute(x, axis, [(i, i ^ mask) for i in range(lax.axis_size(axis))])]
    ppermute x6, starting transfers between devices: 10.3 us -> 8.11 us  [to_chip(): return lax.ppermute(x, ('dom', 'sub'), pairs)]
    ppermute x6, waiting for transfers between devices: 3.73 us -> 2.21 us  [to_chip(): return lax.ppermute(x, ('dom', 'sub'), pairs)]
    unnamed x30 -> x23, local copies, waits for them, and re-layouts: 3.73 us -> 5.03 us
  transfers between devices with their start and end apart: 19 -> 22, of which waited for: 8 -> 10; matrix products, arithmetic and copies ran while one was open for 2% -> 0% of each run, Pallas kernels for 26% -> 14%
where the time goes in v4:
time: 111 us; the launch traced here: 110 us
  waiting for transfers between devices  37.1 us (33%)
  starting transfers between devices  36.1 us (33%)
  Pallas kernels  30.5 us (27%)
  local copies, waits for them, and re-layouts  5.04 us (5%)
  between operations  1.48 us (1%)
    ppermute x16, waiting for transfers between devices, exchange(): lax.ppermute(x, axis, [(i, i ^ mask) for i in range(lax.axis_size(axis))])  34.9 us
    pallas_call x7, Pallas kernels, call(): pl.pallas_call(kernel, in_specs=[in_smem] * len(scalars) + [in_vmem] * le...  28.5 us
    ppermute x16, starting transfers between devices, exchange(): lax.ppermute(x, axis, [(i, i ^ mask) for i in range(lax.axis_size(axis))])  28 us
    ppermute x6, starting transfers between devices, to_chip(): return lax.ppermute(x, ('dom', 'sub'), pairs)  8.11 us
    unnamed x23, local copies, waits for them, and re-layouts  5.03 us
  transfers between devices with their start and end apart: 22, of which 10 were waited for; matrix products, arithmetic and copies ran while one was open for 0% of the time, Pallas kernels for 14%

profile of v4, /device:TPU:0, one launch (start us, length us, event | category | flops | bytes accessed | tf_op | source)
XLA Modules:
  0.0 110.5 jit_solution(16292972146153135446)
XLA Ops:
  1.3 0.0 copy-start
  1.3 1.0 copy-done
  2.3 0.8 copy-done.4
  3.1 0.8 copy-done.5
  3.8 0.8 copy-done.6
  4.6 0.7 copy-done.7
  5.3 0.1 prep_kernel.1
  5.4 4.1 %collective-permute-start.1 = (s16[17,3,512]{2,1,0:T(4,128)(2,1)S(1)}, s16[17,3,512]{2,1,0:T(4,128)(2,1)S(1)}, u32[]{:S(2)}, u32[]{:S(2)}) collective-permute-start(s16[17,3,512]{2,1,0:T(4,128)(2,1)S(1)} %get-tuple-element.27.refs_0_), channel_id=1, source_target_pairs={{0,16},{2,18},{4,20},{6,22},{8,24},{10,26},{12,28},{14,30},{16,0},... | collective-permute-start | bytes 156680 | tf_op jit(solution)/shard_map/ppermute | solution.py:246
  9.5 1.5 %collective-permute-start = (s16[17,3,512]{2,1,0:T(4,128)(2,1)S(1)}, s16[17,3,512]{2,1,0:T(4,128)(2,1)S(1)}, u32[]{:S(2)}, u32[]{:S(2)}) collective-permute-start(s16[17,3,512]{2,1,0:T(4,128)(2,1)S(1)} %get-tuple-element.27.refs_0_), channel_id=1, source_target_pairs={{0,1},{1,0},{2,3},{3,2},{4,5},{5,4},{6,7},{7,6},{8,9},{9,8},{10,11... | collective-permute-start | bytes 156680 | tf_op jit(solution)/shard_map/ppermute | solution.py:246
  11.0 0.3 collective-permute-start.5
  11.4 2.6 %collective-permute-start.6 = (bf16[256,256]{1,0:T(8,128)(2,1)S(1)}, bf16[256,256]{1,0:T(8,128)(2,1)S(1)}, u32[]{:S(2)}, u32[]{:S(2)}) collective-permute-start(bf16[256,256]{1,0:T(8,128)(2,1)S(1)} %get-tuple-element.32.refs_1_), channel_id=1, source_target_pairs={{0,16},{2,18},{4,20},{6,22},{8,24},{10,26},{12,28},{14,30},{16,0},... | collective-permute-start | bytes 393224 | tf_op jit(solution)/shard_map/ppermute | solution.py:246
  14.0 0.5 collective-permute-start.3
  14.5 0.0 collective-permute-done.1.refs_2_
  14.5 1.5 %collective-permute-start.4 = (bf16[256,256]{1,0:T(8,128)(2,1)S(1)}, bf16[256,256]{1,0:T(8,128)(2,1)S(1)}, u32[]{:S(2)}, u32[]{:S(2)}) collective-permute-start(bf16[256,256]{1,0:T(8,128)(2,1)S(1)} %get-tuple-element.32.refs_1_), channel_id=1, source_target_pairs={{0,1},{1,0},{2,3},{3,2},{4,5},{5,4},{6,7},{7,6},{8,9},{9,8},{10,11... | collective-permute-start | bytes 393224 | tf_op jit(solution)/shard_map/ppermute | solution.py:246
  16.0 0.0 collective-permute-done.refs_1_
  16.0 0.5 collective-permute-start.2
  16.5 0.1 pad_add_fusion.codes
  16.6 5.8 %collective-permute-done.2.refs_3_ = s16[17,3,512]{2,1,0:T(4,128)(2,1)S(1)} collective-permute-done((s16[17,3,512]{2,1,0:T(4,128)(2,1)S(1)}, s16[17,3,512]{2,1,0:T(4,128)(2,1)S(1)}, u32[]{:S(2)}, u32[]{:S(2)}) %collective-permute-start.2) | collective-permute-done | bytes 52256 | tf_op jit(solution)/shard_map/ppermute | solution.py:246
  22.4 2.0 %plan_kernel.1 = (s32[37]{0:T(128)S(1)}, s32[16,4,512]{2,1,0:T(4,128)S(1)}, s32[4,1,512]{2,1,0:T(1,128)S(1)}) custom-call(s32[3]{0:T(128)S(1)} %pad_add_fusion.codes, s16[17,3,512]{2,1,0:T(4,128)(2,1)S(1)} %get-tuple-element.27.refs_0_, s16[17,3,512]{2,1,0:T(4,128)(2,1)S(1)} %collective-permute-done.refs_1_, ...), custom_call_target="tpu_custom_call" | custom-call | tf_op jit(solution)/shard_map/plan_kernel/pallas_call | solution.py:322
  24.4 0.0 collective-permute-done.5.refs_4_
  24.4 0.6 collective-permute-start.7
  25.0 0.1 collective-permute-done.6.refs_5_
  25.1 1.4 %collective-permute-start.8 = (bf16[256,256]{1,0:T(8,128)(2,1)S(1)}, bf16[256,256]{1,0:T(8,128)(2,1)S(1)}, u32[]{:S(2)}, u32[]{:S(2)}) collective-permute-start(bf16[256,256]{1,0:T(8,128)(2,1)S(1)} %collective-permute-done.6.refs_5_), channel_id=1, source_target_pairs={{0,1},{1,0},{2,3},{3,2},{4,5},{5,4},{6,7},{7,6},{8,9},{9,8},{10,11... | collective-permute-start | bytes 393224 | tf_op jit(solution)/shard_map/ppermute | solution.py:246
  26.5 0.0 collective-permute-done.3.refs_2_
  26.5 0.0 collective-permute-done.4.refs_3_
  26.5 1.0 copy-done.2
  27.5 4.3 %near_kernel.1 = (bf16[16,256,512]{2,1,0:T(8,128)(2,1)S(1)}, f32[16,256,512]{2,1,0:T(8,128)S(1)}) custom-call(s32[37]{0:T(128)S(1)} %get-tuple-element.44.plan, s32[16,4,512]{2,1,0:T(4,128)S(1)} %get-tuple-element.29.ids, f32[400,256]{1,0:T(8,128)S(1)} %copy-done.2, bf16[256,256]{1,0:T(8,128)(2,1)S(1)} %get-tuple-element.31.refs_0_, ...), custom_call_target="tpu_custom_call" | custom-call | flops 4294967296 | bytes 2097152 | tf_op jit(solution)/shard_map/near_kernel/pallas_call | solution.py:283
  31.8 0.0 collective-permute-done.7.refs_6_
  31.8 0.0 collective-permute-done.8.refs_7_
  31.8 13.5 %edge_kernel.1 = (bf16[16,512,512]{2,1,0:T(8,128)(2,1)S(1)}, bf16[16,512,512]{2,1,0:T(8,128)(2,1)S(1)}, bf16[4,1024,256]{2,1,0:T(8,128)(2,1)S(1)}, f32[512,256]{...) custom-call(s32[37]{0:T(128)S(1)} %get-tuple-element.44.plan, ...), custom_call_target="tpu_custom_call" | custom-call | flops 8589934592 | bytes 2097152 | tf_op jit(solution)/shard_map/edge_kernel/pallas_call | solution.py:283
  45.4 9.5 %collective-permute-start.10 = (f32[256,256]{1,0:T(8,128)S(1)}, f32[256,256]{1,0:T(8,128)S(1)}, u32[]{:S(2)}, u32[]{:S(2)}) collective-permute-start(f32[256,256]{1,0:T(8,128)S(1)} %get-tuple-element.39), channel_id=1, source_target_pairs={{0,2},{2,0},{4,6},{6,4},{8,10},{10,8},{12,14},{14,12},{16,18},{18,... | collective-permute-start | bytes 786440 | tf_op jit(solution)/shard_map/ppermute | solution.py:246
  54.9 1.2 %collective-permute-done.10 = f32[256,256]{1,0:T(8,128)S(1)} collective-permute-done((f32[256,256]{1,0:T(8,128)S(1)}, f32[256,256]{1,0:T(8,128)S(1)}, u32[]{:S(2)}, u32[]{:S(2)}) %collective-permute-start.10) | collective-permute-done | bytes 262176 | tf_op jit(solution)/shard_map/ppermute | solution.py:246
  56.1 3.0 %collective-permute-start.11 = (f32[64,256]{1,0:T(8,128)S(1)}, f32[64,256]{1,0:T(8,128)S(1)}, u32[]{:S(2)}, u32[]{:S(2)}) collective-permute-start(f32[64,256]{1,0:T(8,128)S(1)} %get-tuple-element.51), channel_id=1, source_target_pairs={{0,1},{1,0},{2,3},{3,2},{4,5},{5,4},{6,7},{7,6},{8,9},{9,8},{10,11... | collective-permute-start | bytes 196616 | tf_op jit(solution)/shard_map/ppermute | solution.py:376
  59.1 0.0 collective-permute-start.13
  59.1 1.5 %collective-permute-start.12 = (f32[64,256]{1,0:T(8,128)S(1)}, f32[64,256]{1,0:T(8,128)S(1)}, u32[]{:S(2)}, u32[]{:S(2)}) collective-permute-start(f32[64,256]{1,0:T(8,128)S(1)} %get-tuple-element.53), channel_id=1, source_target_pairs={{0,4},{1,5},{2,6},{3,7},{4,0},{5,1},{6,2},{7,3},{8,12},{9,13},{10,... | collective-permute-start | bytes 196616 | tf_op jit(solution)/shard_map/ppermute | solution.py:376
  60.6 1.9 %collective-permute-start.9 = (f32[512,256]{1,0:T(8,128)S(1)}, f32[512,256]{1,0:T(8,128)S(1)}, u32[]{:S(2)}, u32[]{:S(2)}) collective-permute-start(f32[512,256]{1,0:T(8,128)S(1)} %get-tuple-element.37), channel_id=1, source_target_pairs={{0,1},{1,0},{2,3},{3,2},{4,5},{5,4},{6,7},{7,6},{8,9},{9,8},{10,11... | collective-permute-start | bytes 1572872 | tf_op jit(solution)/shard_map/ppermute | solution.py:246
  62.6 0.0 collective-permute-done.11
  62.6 2.2 %collective-permute-done.13 = f32[64,256]{1,0:T(8,128)S(1)} collective-permute-done((f32[64,256]{1,0:T(8,128)S(1)}, f32[64,256]{1,0:T(8,128)S(1)}, u32[]{:S(2)}, u32[]{:S(2)}) %collective-permute-start.13) | collective-permute-done | bytes 65568 | tf_op jit(solution)/shard_map/ppermute | solution.py:376
  64.8 0.0 collective-permute-done.12
  64.8 0.1 collective-permute-start.14
  64.9 4.3 %collective-permute-done.14 = f32[64,256]{1,0:T(8,128)S(1)} collective-permute-done((f32[64,256]{1,0:T(8,128)S(1)}, f32[64,256]{1,0:T(8,128)S(1)}, u32[]{:S(2)}, u32[]{:S(2)}) %collective-permute-start.14) | collective-permute-done | bytes 65568 | tf_op jit(solution)/shard_map/ppermute | solution.py:246
  69.2 0.1 collective-permute-start.15
  69.2 3.4 %away_kernel.1 = f32[512,256]{1,0:T(8,128)S(1)} custom-call(s32[37]{0:T(128)S(1)} %get-tuple-element.44.plan, s32[16,4,512]{2,1,0:T(4,128)S(1)} %get-tuple-element.29.ids, s32[4,1,512]{2,1,0:T(1,128)S(1)} %get-tuple-element.30.negative_ids, bf16[16,512,512]{2,1,0:T(8,128)(2,1)S(1)} %get-tuple-element.35.grads, ...), custom_call_target="tpu_custom_call" | custom-call | flops 2147483648 | bytes 2097152 | tf_op jit(solution)/shard_map/away_kernel/pallas_call | solution.py:283
  72.6 1.9 %collective-permute-done.15 = f32[64,256]{1,0:T(8,128)S(1)} collective-permute-done((f32[64,256]{1,0:T(8,128)S(1)}, f32[64,256]{1,0:T(8,128)S(1)}, u32[]{:S(2)}, u32[]{:S(2)}) %collective-permute-start.15) | collective-permute-done | bytes 65568 | tf_op jit(solution)/shard_map/ppermute | solution.py:246
  74.6 0.8 collective-permute-done.9
  75.3 0.1 add.42
  75.4 0.0 copy-start.3
  75.4 0.0 copy-start.8
  75.4 0.8 collective-permute-start.20
  76.2 1.5 %collective-permute-start.19 = (f32[64,256]{1,0:T(8,128)S(1)}, f32[64,256]{1,0:T(8,128)S(1)}, u32[]{:S(2)}, u32[]{:S(2)}) collective-permute-start(f32[64,256]{1,0:T(8,128)S(1)} %add.51), channel_id=1, source_target_pairs={{0,4},{1,5},{2,6},{3,7},{4,0},{5,1},{6,2},{7,3},{8,12},{9,13},{10,... | collective-permute-start | bytes 196616 | tf_op jit(solution)/shard_map/ppermute | solution.py:376
  77.7 1.2 %collective-permute-start.18 = (f32[64,256]{1,0:T(8,128)S(1)}, f32[64,256]{1,0:T(8,128)S(1)}, u32[]{:S(2)}, u32[]{:S(2)}) collective-permute-start(f32[64,256]{1,0:T(8,128)S(1)} %add.51), channel_id=1, source_target_pairs={{0,1},{1,0},{2,3},{3,2},{4,5},{5,4},{6,7},{7,6},{8,9},{9,8},{10,11... | collective-permute-start | bytes 196616 | tf_op jit(solution)/shard_map/ppermute | solution.py:376
  79.0 4.3 %own_kernel.1 = (f32[512,256]{1,0:T(8,128)S(1)}, f32[512,256]{1,0:T(8,128)S(1)}) custom-call(s32[37]{0:T(128)S(1)} %get-tuple-element.44.plan, s32[16,4,512]{2,1,0:T(4,128)S(1)} %get-tuple-element.29.ids, s32[4,1,512]{2,1,0:T(1,128)S(1)} %get-tuple-element.30.negative_ids, bf16[16,512,512]{2,1,0:T(8,128)(2,1)S(1)} %get-tuple-element.45.grads, ...), custom_call_target="tpu_custom_call" | custom-call | flops 4294967296 | bytes 2097152 | tf_op jit(solution)/shard_map/own_kernel/pallas_call | solution.py:283
  83.3 0.9 collective-permute-start.17
  84.1 2.4 %collective-permute-start.16 = (f32[512,256]{1,0:T(8,128)S(1)}, f32[512,256]{1,0:T(8,128)S(1)}, u32[]{:S(2)}, u32[]{:S(2)}) collective-permute-start(f32[512,256]{1,0:T(8,128)S(1)} %add.42), channel_id=1, source_target_pairs={{0,16},{2,18},{4,20},{6,22},{8,24},{10,26},{12,28},{14,30},{16,0},... | collective-permute-start | bytes 1572872 | tf_op jit(solution)/shard_map/ppermute | solution.py:246
  86.5 0.0 collective-permute-done.18
  86.6 0.0 collective-permute-done.19
  86.6 0.0 collective-permute-done.20
  86.6 0.1 collective-permute-start.21
  86.7 1.5 %collective-permute-done.21.theirs = f32[256,256]{1,0:T(8,128)S(1)} collective-permute-done((f32[256,256]{1,0:T(8,128)S(1)}, f32[256,256]{1,0:T(8,128)S(1)}, u32[]{:S(2)}, u32[]{:S(2)}) %collective-permute-start.21) | collective-permute-done | bytes 262176 | tf_op jit(solution)/shard_map/ppermute | solution.py:246
  88.2 1.6 %relation_kernel.1 = f32[400,256]{1,0:T(8,128)} custom-call(s32[3]{0:T(128)S(1)} %pad_add_fusion.codes, f32[400,256]{1,0:T(8,128)S(1)} %copy-done.3, f32[1,400]{1,0:T(1,128)S(1)} %bitcast.14, f32[256,256]{1,0:T(8,128)S(1)} %constant_dynamic-update-slice_fusion.mine, f32[256,256]{1,0:T(8,128)S(1)} %collective-permute-done.21.theirs), custom_call_target="tpu_custom_call" | custom-call | flops 2097152 | bytes 2097152 | tf_op jit(solution)/shard_map/relation_kernel/pallas_call | solution.py:283
  89.9 8.3 %collective-permute-done.17.refs_1_ = f32[512,256]{1,0:T(8,128)S(1)} collective-permute-done((f32[512,256]{1,0:T(8,128)S(1)}, f32[512,256]{1,0:T(8,128)S(1)}, u32[]{:S(2)}, u32[]{:S(2)}) %collective-permute-start.17) | collective-permute-done | bytes 524320 | tf_op jit(solution)/shard_map/ppermute | solution.py:246
  98.2 11.1 %collective-permute-done.16.returned = f32[512,256]{1,0:T(8,128)S(1)} collective-permute-done((f32[512,256]{1,0:T(8,128)S(1)}, f32[512,256]{1,0:T(8,128)S(1)}, u32[]{:S(2)}, u32[]{:S(2)}) %collective-permute-start.16) | collective-permute-done | bytes 524320 | tf_op jit(solution)/shard_map/ppermute | solution.py:246
  109.3 0.0 copy-done.1
  109.3 1.2 %entity_kernel.1 = (f32[512,256]{1,0:T(8,128)}, f32[1,512]{1,0:T(1,128)}) custom-call(f32[512,256]{1,0:T(8,128)S(1)} %copy-done.1, f32[1,512]{1,0:T(1,128)S(1)} %bitcast.15, f32[512,256]{1,0:T(8,128)S(1)} %collective-permute-done.16.returned, f32[512,256]{1,0:T(8,128)S(1)} %get-tuple-element.46.refs_0_, f32[512,256]{1,0:T(8,128)S(1)} %collective-permute-done.17.refs_1_), custom_call_target="tpu_custom_call" | custom-call | flops 2097152 | bytes 2097152 | tf_op jit(solution)/shard_map/entity_kernel/pallas_call | solution.py:283
  (18 shorter events, 0.1 us)
Async XLA Ops:
  1.3 1.0 copy-start
  2.3 0.8 copy-start.4
  3.1 0.8 copy-start.5
  3.8 0.8 copy-start.6
  4.6 0.7 copy-start.7
  5.4 9.1 %collective-permute-start.1 = (s16[17,3,512]{2,1,0:T(4,128)(2,1)S(1)}, s16[17,3,512]{2,1,0:T(4,128)(2,1)S(1)}, u32[]{:S(2)}, u32[]{:S(2)}) collective-permute-start(s16[17,3,512]{2,1,0:T(4,128)(2,1)S(1)} %get-tuple-element.27.refs_0_), channel_id=1, source_target_pairs={{0,16},{2,18},{4,20},{6,22},{8,24},{10,26},{12,28},{14,30},{16,0},... | collective-permute-start | bytes 156680 | tf_op jit(solution)/shard_map/ppermute | solution.py:246
  9.5 6.5 %collective-permute-start = (s16[17,3,512]{2,1,0:T(4,128)(2,1)S(1)}, s16[17,3,512]{2,1,0:T(4,128)(2,1)S(1)}, u32[]{:S(2)}, u32[]{:S(2)}) collective-permute-start(s16[17,3,512]{2,1,0:T(4,128)(2,1)S(1)} %get-tuple-element.27.refs_0_), channel_id=1, source_target_pairs={{0,1},{1,0},{2,3},{3,2},{4,5},{5,4},{6,7},{7,6},{8,9},{9,8},{10,11... | collective-permute-start | bytes 156680 | tf_op jit(solution)/shard_map/ppermute | solution.py:246
  11.0 13.3 %collective-permute-start.5 = (bf16[256,256]{1,0:T(8,128)(2,1)S(1)}, bf16[256,256]{1,0:T(8,128)(2,1)S(1)}, u32[]{:S(2)}, u32[]{:S(2)}) collective-permute-start(bf16[256,256]{1,0:T(8,128)(2,1)S(1)} %get-tuple-element.31.refs_0_), channel_id=1, source_target_pairs={{0,16},{2,18},{4,20},{6,22},{8,24},{10,26},{12,28},{14,30},{16,0},... | collective-permute-start | bytes 393224 | tf_op jit(solution)/shard_map/ppermute | solution.py:246
  11.4 13.7 %collective-permute-start.6 = (bf16[256,256]{1,0:T(8,128)(2,1)S(1)}, bf16[256,256]{1,0:T(8,128)(2,1)S(1)}, u32[]{:S(2)}, u32[]{:S(2)}) collective-permute-start(bf16[256,256]{1,0:T(8,128)(2,1)S(1)} %get-tuple-element.32.refs_1_), channel_id=1, source_target_pairs={{0,16},{2,18},{4,20},{6,22},{8,24},{10,26},{12,28},{14,30},{16,0},... | collective-permute-start | bytes 393224 | tf_op jit(solution)/shard_map/ppermute | solution.py:246
  14.0 12.5 %collective-permute-start.3 = (bf16[256,256]{1,0:T(8,128)(2,1)S(1)}, bf16[256,256]{1,0:T(8,128)(2,1)S(1)}, u32[]{:S(2)}, u32[]{:S(2)}) collective-permute-start(bf16[256,256]{1,0:T(8,128)(2,1)S(1)} %get-tuple-element.31.refs_0_), channel_id=1, source_target_pairs={{0,1},{1,0},{2,3},{3,2},{4,5},{5,4},{6,7},{7,6},{8,9},{9,8},{10,11... | collective-permute-start | bytes 393224 | tf_op jit(solution)/shard_map/ppermute | solution.py:246
  14.5 12.0 %collective-permute-start.4 = (bf16[256,256]{1,0:T(8,128)(2,1)S(1)}, bf16[256,256]{1,0:T(8,128)(2,1)S(1)}, u32[]{:S(2)}, u32[]{:S(2)}) collective-permute-start(bf16[256,256]{1,0:T(8,128)(2,1)S(1)} %get-tuple-element.32.refs_1_), channel_id=1, source_target_pairs={{0,1},{1,0},{2,3},{3,2},{4,5},{5,4},{6,7},{7,6},{8,9},{9,8},{10,11... | collective-permute-start | bytes 393224 | tf_op jit(solution)/shard_map/ppermute | solution.py:246
  16.0 6.4 %collective-permute-start.2 = (s16[17,3,512]{2,1,0:T(4,128)(2,1)S(1)}, s16[17,3,512]{2,1,0:T(4,128)(2,1)S(1)}, u32[]{:S(2)}, u32[]{:S(2)}) collective-permute-start(s16[17,3,512]{2,1,0:T(4,128)(2,1)S(1)} %collective-permute-done.1.refs_2_), channel_id=1, source_target_pairs={{0,1},{1,0},{2,3},{3,2},{4,5},{5,4},{6,7},{7,6},{8,9},{9,8},{10,11... | collective-permute-start | bytes 156680 | tf_op jit(solution)/shard_map/ppermute | solution.py:246
  24.4 7.4 %collective-permute-start.7 = (bf16[256,256]{1,0:T(8,128)(2,1)S(1)}, bf16[256,256]{1,0:T(8,128)(2,1)S(1)}, u32[]{:S(2)}, u32[]{:S(2)}) collective-permute-start(bf16[256,256]{1,0:T(8,128)(2,1)S(1)} %collective-permute-done.5.refs_4_), channel_id=1, source_target_pairs={{0,1},{1,0},{2,3},{3,2},{4,5},{5,4},{6,7},{7,6},{8,9},{9,8},{10,11... | collective-permute-start | bytes 393224 | tf_op jit(solution)/shard_map/ppermute | solution.py:246
  25.1 6.8 %collective-permute-start.8 = (bf16[256,256]{1,0:T(8,128)(2,1)S(1)}, bf16[256,256]{1,0:T(8,128)(2,1)S(1)}, u32[]{:S(2)}, u32[]{:S(2)}) collective-permute-start(bf16[256,256]{1,0:T(8,128)(2,1)S(1)} %collective-permute-done.6.refs_5_), channel_id=1, source_target_pairs={{0,1},{1,0},{2,3},{3,2},{4,5},{5,4},{6,7},{7,6},{8,9},{9,8},{10,11... | collective-permute-start | bytes 393224 | tf_op jit(solution)/shard_map/ppermute | solution.py:246
  26.5 1.0 copy-start.2
  45.4 10.7 %collective-permute-start.10 = (f32[256,256]{1,0:T(8,128)S(1)}, f32[256,256]{1,0:T(8,128)S(1)}, u32[]{:S(2)}, u32[]{:S(2)}) collective-permute-start(f32[256,256]{1,0:T(8,128)S(1)} %get-tuple-element.39), channel_id=1, source_target_pairs={{0,2},{2,0},{4,6},{6,4},{8,10},{10,8},{12,14},{14,12},{16,18},{18,... | collective-permute-start | bytes 786440 | tf_op jit(solution)/shard_map/ppermute | solution.py:246
  56.1 6.5 %collective-permute-start.11 = (f32[64,256]{1,0:T(8,128)S(1)}, f32[64,256]{1,0:T(8,128)S(1)}, u32[]{:S(2)}, u32[]{:S(2)}) collective-permute-start(f32[64,256]{1,0:T(8,128)S(1)} %get-tuple-element.51), channel_id=1, source_target_pairs={{0,1},{1,0},{2,3},{3,2},{4,5},{5,4},{6,7},{7,6},{8,9},{9,8},{10,11... | collective-permute-start | bytes 196616 | tf_op jit(solution)/shard_map/ppermute | solution.py:376
  59.1 5.7 %collective-permute-start.13 = (f32[64,256]{1,0:T(8,128)S(1)}, f32[64,256]{1,0:T(8,128)S(1)}, u32[]{:S(2)}, u32[]{:S(2)}) collective-permute-start(f32[64,256]{1,0:T(8,128)S(1)} %get-tuple-element.52), channel_id=1, source_target_pairs={{0,5},{1,4},{2,7},{3,6},{4,1},{5,0},{6,3},{7,2},{8,13},{9,12},{10,... | collective-permute-start | bytes 196616 | tf_op jit(solution)/shard_map/ppermute | solution.py:376
  59.1 5.7 %collective-permute-start.12 = (f32[64,256]{1,0:T(8,128)S(1)}, f32[64,256]{1,0:T(8,128)S(1)}, u32[]{:S(2)}, u32[]{:S(2)}) collective-permute-start(f32[64,256]{1,0:T(8,128)S(1)} %get-tuple-element.53), channel_id=1, source_target_pairs={{0,4},{1,5},{2,6},{3,7},{4,0},{5,1},{6,2},{7,3},{8,12},{9,13},{10,... | collective-permute-start | bytes 196616 | tf_op jit(solution)/shard_map/ppermute | solution.py:376
  60.6 14.7 %collective-permute-start.9 = (f32[512,256]{1,0:T(8,128)S(1)}, f32[512,256]{1,0:T(8,128)S(1)}, u32[]{:S(2)}, u32[]{:S(2)}) collective-permute-start(f32[512,256]{1,0:T(8,128)S(1)} %get-tuple-element.37), channel_id=1, source_target_pairs={{0,1},{1,0},{2,3},{3,2},{4,5},{5,4},{6,7},{7,6},{8,9},{9,8},{10,11... | collective-permute-start | bytes 1572872 | tf_op jit(solution)/shard_map/ppermute | solution.py:246
  64.8 4.3 %collective-permute-start.14 = (f32[64,256]{1,0:T(8,128)S(1)}, f32[64,256]{1,0:T(8,128)S(1)}, u32[]{:S(2)}, u32[]{:S(2)}) collective-permute-start(f32[64,256]{1,0:T(8,128)S(1)} %fusion.2), channel_id=1, source_target_pairs={{0,8},{2,10},{4,12},{6,14},{8,0},{10,2},{12,4},{14,6},{16,24},{18,... | collective-permute-start | bytes 196616 | tf_op jit(solution)/shard_map/ppermute | solution.py:246
  69.2 5.4 %collective-permute-start.15 = (f32[64,256]{1,0:T(8,128)S(1)}, f32[64,256]{1,0:T(8,128)S(1)}, u32[]{:S(2)}, u32[]{:S(2)}) collective-permute-start(f32[64,256]{1,0:T(8,128)S(1)} %add.50), channel_id=1, source_target_pairs={{0,16},{2,18},{4,20},{6,22},{8,24},{10,26},{12,28},{14,30},{16,0},... | collective-permute-start | bytes 196616 | tf_op jit(solution)/shard_map/ppermute | solution.py:246
  75.4 12.8 %copy-start.3 = (f32[400,256]{1,0:T(8,128)S(1)}, f32[400,256]{1,0:T(8,128)}, u32[]{:S(2)}) copy-start(f32[400,256]{1,0:T(8,128)} %relations.3) | copy-start | bytes 1228804
  75.4 12.8 %copy-start.8 = (f32[400]{0:T(512)S(1)}, f32[400]{0:T(512)}, u32[]{:S(2)}) copy-start(f32[400]{0:T(512)} %param.12) | copy-start | bytes 4804
  75.4 11.2 %collective-permute-start.20 = (f32[64,256]{1,0:T(8,128)S(1)}, f32[64,256]{1,0:T(8,128)S(1)}, u32[]{:S(2)}, u32[]{:S(2)}) collective-permute-start(f32[64,256]{1,0:T(8,128)S(1)} %add.51), channel_id=1, source_target_pairs={{0,5},{1,4},{2,7},{3,6},{4,1},{5,0},{6,3},{7,2},{8,13},{9,12},{10,... | collective-permute-start | bytes 196616 | tf_op jit(solution)/shard_map/ppermute | solution.py:376
  76.2 10.3 %collective-permute-start.19 = (f32[64,256]{1,0:T(8,128)S(1)}, f32[64,256]{1,0:T(8,128)S(1)}, u32[]{:S(2)}, u32[]{:S(2)}) collective-permute-start(f32[64,256]{1,0:T(8,128)S(1)} %add.51), channel_id=1, source_target_pairs={{0,4},{1,5},{2,6},{3,7},{4,0},{5,1},{6,2},{7,3},{8,12},{9,13},{10,... | collective-permute-start | bytes 196616 | tf_op jit(solution)/shard_map/ppermute | solution.py:376
  77.7 8.8 %collective-permute-start.18 = (f32[64,256]{1,0:T(8,128)S(1)}, f32[64,256]{1,0:T(8,128)S(1)}, u32[]{:S(2)}, u32[]{:S(2)}) collective-permute-start(f32[64,256]{1,0:T(8,128)S(1)} %add.51), channel_id=1, source_target_pairs={{0,1},{1,0},{2,3},{3,2},{4,5},{5,4},{6,7},{7,6},{8,9},{9,8},{10,11... | collective-permute-start | bytes 196616 | tf_op jit(solution)/shard_map/ppermute | solution.py:376
  79.0 30.3 %copy-start.1 = (f32[512,256]{1,0:T(8,128)S(1)}, f32[512,256]{1,0:T(8,128)}, u32[]{:S(2)}) copy-start(f32[512,256]{1,0:T(8,128)} %table.3) | copy-start | bytes 1572868
  79.0 30.3 %copy-start.9 = (f32[512]{0:T(512)S(1)}, f32[512]{0:T(512)}, u32[]{:S(2)}) copy-start(f32[512]{0:T(512)} %param.10) | copy-start | bytes 6148
  83.3 14.9 %collective-permute-start.17 = (f32[512,256]{1,0:T(8,128)S(1)}, f32[512,256]{1,0:T(8,128)S(1)}, u32[]{:S(2)}, u32[]{:S(2)}) collective-permute-start(f32[512,256]{1,0:T(8,128)S(1)} %get-tuple-element.47), channel_id=1, source_target_pairs={{0,1},{1,0},{2,3},{3,2},{4,5},{5,4},{6,7},{7,6},{8,9},{9,8},{10,11... | collective-permute-start | bytes 1572872 | tf_op jit(solution)/shard_map/ppermute | solution.py:246
  84.1 25.1 %collective-permute-start.16 = (f32[512,256]{1,0:T(8,128)S(1)}, f32[512,256]{1,0:T(8,128)S(1)}, u32[]{:S(2)}, u32[]{:S(2)}) collective-permute-start(f32[512,256]{1,0:T(8,128)S(1)} %add.42), channel_id=1, source_target_pairs={{0,16},{2,18},{4,20},{6,22},{8,24},{10,26},{12,28},{14,30},{16,0},... | collective-permute-start | bytes 1572872 | tf_op jit(solution)/shard_map/ppermute | solution.py:246
  86.6 1.6 %collective-permute-start.21 = (f32[256,256]{1,0:T(8,128)S(1)}, f32[256,256]{1,0:T(8,128)S(1)}, u32[]{:S(2)}, u32[]{:S(2)}) collective-permute-start(f32[256,256]{1,0:T(8,128)S(1)} %constant_dynamic-update-slice_fusion.mine), channel_id=1, source_target_pairs={{0,2},{2,0},{4,6},{6,4},{8,10},{10,8},{12,14},{14,12},{16,18},{18,... | collective-permute-start | bytes 786440 | tf_op jit(solution)/shard_map/ppermute | solution.py:246

commit v5 on v4

--- a/solution.py
+++ b/solution.py
@@ -61,11 +61,11 @@
         start += piece.shape[0]
 
 
-def prep_kernel(count, table, heads, tails, kinds, negatives, *refs):
-    rows_out, ids_out = refs[:-1], refs[-1]
-    each = rows_out[0].shape[1]
-    for k, out in enumerate(rows_out):
-        out[...] = table[k * each : (k + 1) * each, :].T.astype(bf16)
+def rows_kernel(table, out):
+    out[...] = table[...].T.astype(bf16)
+
+
+def ids_kernel(count, heads, tails, kinds, negatives, ids_out):
     blocks, _, width = ids_out.shape
     for j in range(blocks - 1):
         at = slice(j * width, (j + 1) * width)
@@ -115,7 +115,7 @@
 
         return carry
 
-    lax.fori_loop(0, most, one_step, 0)
+    lax.fori_loop(0, high - low, one_step, 0)
 
 
 def near_kernel(plan, ids, relations, *refs):
@@ -135,17 +135,17 @@
     lax.fori_loop(0, plan[2 * ids.shape[0]], one_block, 0)
 
 
-def edge_kernel(n, parts, plan, ids, negative_ids, near_in, operator_in, *refs):
-    near, away = refs[:parts], refs[parts : 2 * parts]
-    near_grad, away_grad, negative_out = refs[2 * parts : 2 * parts + 3]
-    away_other = refs[2 * parts + 3 : 2 * parts + 2 + n]
-    relation_sum, (table, table_t, negative_grad) = refs[2 * parts + 2 + n : -3], refs[-3:]
+def edge_kernel(n, plan, ids, negative_ids, near_in, operator_in, *refs):
+    near, away = refs[:n], refs[n : 2 * n]
+    near_grad, away_grad, negative_out = refs[2 * n : 2 * n + 3]
+    away_other = refs[2 * n + 3 : 3 * n + 2]
+    relation_sum, (table, table_t, negative_grad) = refs[3 * n + 2 : -3], refs[-3:]
     most, _, width = ids.shape
     steps = plan[2 * most]
     count = table.shape[0]
     for piece in (*away_other, *relation_sum):
         piece[...] = jnp.zeros_like(piece)
-    rows = sum(piece.shape[1] for piece in away) // n
+    rows = away[0].shape[1]
 
     def one_block(i, carry):
         here = plan[i]
@@ -199,13 +199,13 @@
     lax.fori_loop(0, steps, one_block, 0)
 
 
-def scatter_kernel(row, first, plan, ids, negative_ids, grads, negative_grads, *sums):
+def scatter_kernel(row, start, first, plan, ids, negative_ids, grads, negative_grads, *sums):
     most = ids.shape[0]
     for piece in sums:
         piece[...] = jnp.zeros_like(piece)
 
     def one_block(i, carry):
-        scatter_add(sums, ids[i][row : row + 1], grads[i])
+        scatter_add(sums, ids[i][row : row + 1] - start, grads[i])
         return carry
 
     lax.fori_loop(0, plan[2 * most], one_block, 0)
@@ -213,7 +213,7 @@
 
         @pl.when(plan[2 * most + 1 + k] != 0)
         def _(k=k):
-            add_negatives(sums, negative_ids[k], negative_grads[k])
+            add_negatives(sums, negative_ids[k] - start, negative_grads[k])
 
 
 def entity_kernel(n, table, state, returned, *refs):
@@ -278,7 +278,7 @@
     in_vmem = pl.BlockSpec(memory_space=pltpu.VMEM)
     in_smem = pl.BlockSpec(memory_space=pltpu.SMEM)
 
-    def call(kernel, name, outs, scratch, unit, scalars, arrays, held=True):
+    def call(kernel, name, outs, scratch, unit, scalars, arrays, held=True, fetch=False):
         place = (lambda x, t: pltpu.VMEM(x, t)) if held else jax.ShapeDtypeStruct
         return pl.pallas_call(
             kernel,
@@ -289,35 +289,36 @@
             compiler_params=params,
             cost_estimate=pl.CostEstimate(flops=slots * dims * unit, bytes_accessed=slots * dims, transcendentals=0),
             name=name,
-        )(*scalars, *(pltpu.with_memory_space_constraint(x, pltpu.VMEM) for x in arrays))
-
-    halves = 2
-    *local, ids = call(
-        prep_kernel,
-        "prep_kernel",
-        [((dims, rows // halves), bf16)] * halves + [((most + 1, 3, width), jnp.int16)],
+        )(*scalars, *(pltpu.with_memory_space_constraint(x, pltpu.HBM if fetch else pltpu.VMEM) for x in arrays))
+
+    (ids,) = call(
+        ids_kernel,
+        "ids_kernel",
+        [((most + 1, 3, width), jnp.int16)],
         [],
         1,
         (edge_counts,),
         (
-            entity_table,
             head_rows.reshape(1, slots),
             tail_rows.reshape(1, slots),
             relation_ids.reshape(1, slots),
             negative_rows.reshape(1, count),
         ),
-    )
+        fetch=True,
+    )
+    ids, table = lax.optimization_barrier((ids, entity_table))
+    (local,) = call(rows_kernel, "rows_kernel", [((dims, rows), bf16)], [], 1, (), (table,), fetch=True)
+
+    def to_peer(x, across, aside):
+        pairs = [(d * n + s, (d ^ across) * n + (s ^ aside)) for d in range(n_dom) for s in range(n)]
+        return lax.ppermute(x, ("dom", "sub"), pairs)
 
     def along_sub(x):
         return [x] + [exchange(x, "sub", k) for k in range(1, n)]
 
-    def in_order(pieces):
-        return [piece[k] for k in range(n) for piece in pieces]
-
     all_ids = along_sub(ids) + along_sub(exchange(ids, "dom", pair))
-    away_slab = in_order([along_sub(exchange(x, "dom", pair)) for x in local])
-    near_slab = in_order([along_sub(x) for x in local])
-    parts = n * halves
+    near_slab = along_sub(local)
+    away_first = exchange(local, "dom", pair)
 
     plan, step_ids, negative_ids = pl.pallas_call(
         functools.partial(plan_kernel, n),
@@ -329,22 +330,25 @@
             pltpu.VMEM((team, 1, width), i32),
         ],
         compiler_params=params,
+        cost_estimate=pl.CostEstimate(flops=32 * slots * dims * rows, bytes_accessed=slots * dims, transcendentals=0),
         name="plan_kernel",
     )(codes, *(pltpu.with_memory_space_constraint(x, pltpu.VMEM) for x in all_ids))
 
+    near_plan, away_first = lax.optimization_barrier((plan, away_first))
+    away_slab = along_sub(away_first)
     near_rows, operator = call(
         near_kernel,
         "near_kernel",
         [((most, dims, width), bf16), ((most, dims, width), f32)],
         [pltpu.VMEM((rel_rows, dims), f32), pltpu.VMEM((2 * dims, rel_rows), bf16)],
         n * rows + 2 * rel_rows,
-        (plan,),
+        (near_plan,),
         (step_ids, relations, *near_slab),
     )
     sums = ((rows, dims), f32)
     pair_out = ((most, 2 * dims, width), bf16)
     near_grad, away_grad, negative_grad, *found = call(
-        functools.partial(edge_kernel, n, parts),
+        functools.partial(edge_kernel, n),
         "edge_kernel",
         [pair_out, pair_out, ((team, 2 * count, dims), bf16)]
         + [sums] * (n - 1)
@@ -356,49 +360,43 @@
         (step_ids, negative_ids, near_rows, operator, *near_slab, *away_slab),
     )
     away_other, relation_part = found[: n - 1], found[n - 1 :]
-    (away_total,) = call(
-        functools.partial(scatter_kernel, 1, 0),
-        "away_kernel",
-        [sums],
-        [],
-        2 * rows,
-        (plan,),
-        (step_ids, negative_ids, away_grad, negative_grad),
-    )
-    for k in range(1, n):
-        away_total = away_total + exchange(away_other[k - 1], "sub", k)
-
-    def to_chip(x, mask):
-        pairs = []
-        for d in range(n_dom):
-            for s in range(n):
-                pairs.append((d * n + s, (d ^ (mask // n * 2)) * n + (s ^ (mask % n))))
-        return lax.ppermute(x, ("dom", "sub"), pairs)
+
+    def scatter(name, row, start, parts, first, plan, grads):
+        return call(
+            functools.partial(scatter_kernel, row, start, first),
+            name,
+            [sums] * parts,
+            [],
+            2 * parts * rows,
+            (plan,),
+            (step_ids, negative_ids, grads, negative_grad),
+        )
+
+    def to_chip(x, k):
+        return to_peer(x, k // n * 2, k % n)
 
     other_core = exchange(relation_part[chips], "dom", 1)
     partial = [relation_part[k] + other_core[k * chunk : (k + 1) * chunk] for k in range(chips)]
+    *partial, plan = lax.optimization_barrier((*partial, plan))
     chunk_total = partial[0]
     for k in range(1, chips):
         chunk_total = chunk_total + to_chip(partial[k], k)
+    (away_total,) = scatter("away_kernel", 1, 0, 1, 0, plan, away_grad)
+    chunk_total, away_total, plan, *away_other = lax.optimization_barrier((chunk_total, away_total, plan, *away_other))
+    away_received = [exchange(away_other[k - 1], "sub", k) for k in range(1, n)]
     mask = 4
     while mask < n_dom:
         chunk_total = chunk_total + exchange(chunk_total, "dom", mask)
         mask *= 2
-
-    plan, away_total, chunk_total = lax.optimization_barrier((plan, away_total, chunk_total))
+    near_other = scatter("own_other_kernel", 0, rows, n - 1, n, plan, near_grad)
+    for x in away_received:
+        away_total = away_total + x
+    plan, away_total, chunk_total, *near_other = lax.optimization_barrier((plan, away_total, chunk_total, *near_other))
     returned = exchange(away_total, "dom", pair)
     mine = jnp.concatenate([chunk_total] + [to_chip(chunk_total, k) for k in range(1, chips)], axis=0)
     theirs = exchange(mine, "dom", 1)
-    near_sum = call(
-        functools.partial(scatter_kernel, 0, n),
-        "own_kernel",
-        [sums] * n,
-        [],
-        2 * n * rows,
-        (plan,),
-        (step_ids, negative_ids, near_grad, negative_grad),
-    )
-    near_sum = [near_sum[0]] + [exchange(near_sum[k], "sub", k) for k in range(1, n)]
+    near_sum = [exchange(near_other[k - 1], "sub", k) for k in range(1, n)]
+    near_sum += scatter("own_kernel", 0, 0, 1, n, plan, near_grad)
     (new_relations,) = call(
         functools.partial(relation_kernel, chunk),
         "relation_kernel",

time: 111 us -> 102 us (0.919)
  starting transfers between devices: 36.1 us -> 27.2 us
  local copies, waits for them, and re-layouts: 5.04 us -> 0.05 us
  Pallas kernels: 30.5 us -> 33.7 us
  waiting for transfers between devices: 37.1 us -> 38.8 us
    ppermute x16 -> x13, starting transfers between devices: 28 us -> 18.2 us  [exchange(): lax.ppermute(x, axis, [(i, i ^ mask) for i in range(lax.axis_size(axis))])]
    unnamed x23 -> x11, local copies, waits for them, and re-layouts: 5.03 us -> 0.04 us
    pallas_call x7 -> x9, Pallas kernels: 28.5 us -> 32.1 us  [call(): pl.pallas_call(kernel, in_specs=[in_smem] * len(scalars) + [in_vmem] * le...]
    ppermute x6, waiting for transfers between devices: 2.21 us -> 3.33 us  [to_peer(): return lax.ppermute(x, ('dom', 'sub'), pairs)]
    ppermute x16 -> x13, waiting for transfers between devices: 34.9 us -> 35.4 us  [exchange(): lax.ppermute(x, axis, [(i, i ^ mask) for i in range(lax.axis_size(axis))])]
  transfers between devices with their start and end apart: 22 -> 19, of which waited for: 10 -> 11; matrix products, arithmetic and copies ran while one was open for 0% -> 0% of each run, Pallas kernels for 14% -> 18%
where the time goes in v5:
time: 102 us; the launch traced here: 101 us
  waiting for transfers between devices  38.8 us (38%)
  Pallas kernels  33.7 us (33%)
  starting transfers between devices  27.2 us (27%)
  between operations  1.47 us (1%)
    ppermute x13, waiting for transfers between devices, exchange(): lax.ppermute(x, axis, [(i, i ^ mask) for i in range(lax.axis_size(axis))])  35.4 us
    pallas_call x9, Pallas kernels, call(): pl.pallas_call(kernel, in_specs=[in_smem] * len(scalars) + [in_vmem] * le...  32.1 us
    ppermute x13, starting transfers between devices, exchange(): lax.ppermute(x, axis, [(i, i ^ mask) for i in range(lax.axis_size(axis))])  18.2 us
    ppermute x6, starting transfers between devices, to_peer(): return lax.ppermute(x, ('dom', 'sub'), pairs)  8.97 us
    ppermute x6, waiting for transfers between devices, to_peer(): return lax.ppermute(x, ('dom', 'sub'), pairs)  3.33 us
  transfers between devices with their start and end apart: 19, of which 11 were waited for; matrix products, arithmetic and copies ran while one was open for 0% of the time, Pallas kernels for 18%

profile of v5, /device:TPU:0, one launch (start us, length us, event | category | flops | bytes accessed | tf_op | source)
XLA Modules:
  0.0 101.4 jit_solution(6729088671296254470)
XLA Ops:
  1.3 0.8 ids_kernel.1.refs_0_
  2.1 4.1 %collective-permute-start.1 = (s16[17,3,512]{2,1,0:T(4,128)(2,1)S(1)}, s16[17,3,512]{2,1,0:T(4,128)(2,1)S(1)}, u32[]{:S(2)}, u32[]{:S(2)}) collective-permute-start(s16[17,3,512]{2,1,0:T(4,128)(2,1)S(1)} %ids_kernel.1.refs_0_), channel_id=1, source_target_pairs={{0,16},{2,18},{4,20},{6,22},{8,24},{10,26},{12,28},{14,30},{16,0},... | collective-permute-start | bytes 156680 | tf_op jit(solution)/shard_map/ppermute | solution.py:246
  6.2 1.5 %collective-permute-start = (s16[17,3,512]{2,1,0:T(4,128)(2,1)S(1)}, s16[17,3,512]{2,1,0:T(4,128)(2,1)S(1)}, u32[]{:S(2)}, u32[]{:S(2)}) collective-permute-start(s16[17,3,512]{2,1,0:T(4,128)(2,1)S(1)} %ids_kernel.1.refs_0_), channel_id=1, source_target_pairs={{0,1},{1,0},{2,3},{3,2},{4,5},{5,4},{6,7},{7,6},{8,9},{9,8},{10,11... | collective-permute-start | bytes 156680 | tf_op jit(solution)/shard_map/ppermute | solution.py:246
  7.7 1.2 %rows_kernel.1.refs_0_ = bf16[256,512]{1,0:T(8,128)(2,1)S(1)} custom-call(f32[512,256]{1,0:T(8,128)} %table.2), custom_call_target="tpu_custom_call" | custom-call | flops 2097152 | bytes 2097152 | tf_op jit(solution)/shard_map/rows_kernel/pallas_call | solution.py:283
  8.9 0.6 collective-permute-start.4
  9.5 0.1 collective-permute-start.3
  9.6 0.4 collective-permute-done.1.refs_2_
  10.0 1.7 %collective-permute-start.2 = (s16[17,3,512]{2,1,0:T(4,128)(2,1)S(1)}, s16[17,3,512]{2,1,0:T(4,128)(2,1)S(1)}, u32[]{:S(2)}, u32[]{:S(2)}) collective-permute-start(s16[17,3,512]{2,1,0:T(4,128)(2,1)S(1)} %collective-permute-done.1.refs_2_), channel_id=1, source_target_pairs={{0,1},{1,0},{2,3},{3,2},{4,5},{5,4},{6,7},{7,6},{8,9},{9,8},{10,11... | collective-permute-start | bytes 156680 | tf_op jit(solution)/shard_map/ppermute | solution.py:246
  11.7 0.1 pad_add_fusion.codes
  11.8 0.0 copy-start.1
  11.8 0.0 collective-permute-done.refs_1_
  11.8 6.2 %collective-permute-done.2.refs_3_ = s16[17,3,512]{2,1,0:T(4,128)(2,1)S(1)} collective-permute-done((s16[17,3,512]{2,1,0:T(4,128)(2,1)S(1)}, s16[17,3,512]{2,1,0:T(4,128)(2,1)S(1)}, u32[]{:S(2)}, u32[]{:S(2)}) %collective-permute-start.2) | collective-permute-done | bytes 52256 | tf_op jit(solution)/shard_map/ppermute | solution.py:246
  18.0 1.6 %plan_kernel.1 = (s32[37]{0:T(128)S(1)}, s32[16,4,512]{2,1,0:T(4,128)S(1)}, s32[4,1,512]{2,1,0:T(1,128)S(1)}) custom-call(s32[3]{0:T(128)S(1)} %pad_add_fusion.codes, s16[17,3,512]{2,1,0:T(4,128)(2,1)S(1)} %ids_kernel.1.refs_0_, s16[17,3,512]{2,1,0:T(4,128)(2,1)S(1)} %collective-permute-done.refs_1_, s16[17,3,512]{2,1,0:T(4,128)(2,1)S(1)} %collective-permute-done.1.refs_2_, ...), custom_call_target="tpu_custom_call" | custom-call | flops 34359738368 | bytes 2097152 | tf_op jit(solution)/shard_map/plan_kernel/pallas_call | solution.py:323
  19.5 3.7 %collective-permute-done.3.refs_2_ = bf16[256,512]{1,0:T(8,128)(2,1)S(1)} collective-permute-done((bf16[256,512]{1,0:T(8,128)(2,1)S(1)}, bf16[256,512]{1,0:T(8,128)(2,1)S(1)}, u32[]{:S(2)}, u32[]{:S(2)}) %collective-permute-start.3) | collective-permute-done | bytes 262176 | tf_op jit(solution)/shard_map/ppermute | solution.py:246
  23.2 1.5 %collective-permute-start.5 = (bf16[256,512]{1,0:T(8,128)(2,1)S(1)}, bf16[256,512]{1,0:T(8,128)(2,1)S(1)}, u32[]{:S(2)}, u32[]{:S(2)}) collective-permute-start(bf16[256,512]{1,0:T(8,128)(2,1)S(1)} %collective-permute-done.3.refs_2_), channel_id=1, source_target_pairs={{0,1},{1,0},{2,3},{3,2},{4,5},{5,4},{6,7},{7,6},{8,9},{9,8},{10,11... | collective-permute-start | bytes 786440 | tf_op jit(solution)/shard_map/ppermute | solution.py:246
  24.7 0.0 collective-permute-done.4.refs_1_
  24.7 0.0 copy-done.1
  24.7 4.3 %near_kernel.1 = (bf16[16,256,512]{2,1,0:T(8,128)(2,1)S(1)}, f32[16,256,512]{2,1,0:T(8,128)S(1)}) custom-call(s32[37]{0:T(128)S(1)} %get-tuple-element.65.plan, s32[16,4,512]{2,1,0:T(4,128)S(1)} %get-tuple-element.38.ids, f32[400,256]{1,0:T(8,128)S(1)} %copy-done.1, bf16[256,512]{1,0:T(8,128)(2,1)S(1)} %rows_kernel.1.refs_0_, ...), custom_call_target="tpu_custom_call" | custom-call | flops 4294967296 | bytes 2097152 | tf_op jit(solution)/shard_map/near_kernel/pallas_call | solution.py:283
  29.1 1.3 %collective-permute-done.5.refs_3_ = bf16[256,512]{1,0:T(8,128)(2,1)S(1)} collective-permute-done((bf16[256,512]{1,0:T(8,128)(2,1)S(1)}, bf16[256,512]{1,0:T(8,128)(2,1)S(1)}, u32[]{:S(2)}, u32[]{:S(2)}) %collective-permute-start.5) | collective-permute-done | bytes 262176 | tf_op jit(solution)/shard_map/ppermute | solution.py:246
  30.4 13.7 %edge_kernel.1 = (bf16[16,512,512]{2,1,0:T(8,128)(2,1)S(1)}, bf16[16,512,512]{2,1,0:T(8,128)(2,1)S(1)}, bf16[4,1024,256]{2,1,0:T(8,128)(2,1)S(1)}, f32[512,256]{...) custom-call(s32[37]{0:T(128)S(1)} %get-tuple-element.65.plan, ...), custom_call_target="tpu_custom_call" | custom-call | flops 8589934592 | bytes 2097152 | tf_op jit(solution)/shard_map/edge_kernel/pallas_call | solution.py:283
  44.0 4.7 %collective-permute-start.6 = (f32[256,256]{1,0:T(8,128)S(1)}, f32[256,256]{1,0:T(8,128)S(1)}, u32[]{:S(2)}, u32[]{:S(2)}) collective-permute-start(f32[256,256]{1,0:T(8,128)S(1)} %get-tuple-element.46), channel_id=1, source_target_pairs={{0,2},{2,0},{4,6},{6,4},{8,10},{10,8},{12,14},{14,12},{16,18},{18,... | collective-permute-start | bytes 786440 | tf_op jit(solution)/shard_map/ppermute | solution.py:246
  48.7 1.2 %collective-permute-done.6 = f32[256,256]{1,0:T(8,128)S(1)} collective-permute-done((f32[256,256]{1,0:T(8,128)S(1)}, f32[256,256]{1,0:T(8,128)S(1)}, u32[]{:S(2)}, u32[]{:S(2)}) %collective-permute-start.6) | collective-permute-done | bytes 262176 | tf_op jit(solution)/shard_map/ppermute | solution.py:246
  49.9 3.9 %collective-permute-start.7 = (f32[64,256]{1,0:T(8,128)S(1)}, f32[64,256]{1,0:T(8,128)S(1)}, u32[]{:S(2)}, u32[]{:S(2)}) collective-permute-start(f32[64,256]{1,0:T(8,128)S(1)} %get-tuple-element.51), channel_id=1, source_target_pairs={{0,1},{1,0},{2,3},{3,2},{4,5},{5,4},{6,7},{7,6},{8,9},{9,8},{10,11... | collective-permute-start | bytes 196616 | tf_op jit(solution)/shard_map/ppermute | solution.py:314
  53.8 0.0 collective-permute-start.8
  53.8 1.5 %collective-permute-start.9 = (f32[64,256]{1,0:T(8,128)S(1)}, f32[64,256]{1,0:T(8,128)S(1)}, u32[]{:S(2)}, u32[]{:S(2)}) collective-permute-start(f32[64,256]{1,0:T(8,128)S(1)} %get-tuple-element.53), channel_id=1, source_target_pairs={{0,5},{1,4},{2,7},{3,6},{4,1},{5,0},{6,3},{7,2},{8,13},{9,12},{10,... | collective-permute-start | bytes 196616 | tf_op jit(solution)/shard_map/ppermute | solution.py:314
  55.3 3.4 %away_kernel.1 = f32[512,256]{1,0:T(8,128)S(1)} custom-call(s32[37]{0:T(128)S(1)} %get-tuple-element.65.plan, s32[16,4,512]{2,1,0:T(4,128)S(1)} %get-tuple-element.38.ids, s32[4,1,512]{2,1,0:T(1,128)S(1)} %get-tuple-element.39.negative_ids, bf16[16,512,512]{2,1,0:T(8,128)(2,1)S(1)} %get-tuple-element.55.grads, ...), custom_call_target="tpu_custom_call" | custom-call | flops 2147483648 | bytes 2097152 | tf_op jit(solution)/shard_map/away_kernel/pallas_call | solution.py:283
  58.7 0.0 collective-permute-done.7
  58.7 0.0 collective-permute-done.8
  58.7 0.3 collective-permute-done.9
  59.1 2.2 %collective-permute-start.10 = (f32[512,256]{1,0:T(8,128)S(1)}, f32[512,256]{1,0:T(8,128)S(1)}, u32[]{:S(2)}, u32[]{:S(2)}) collective-permute-start(f32[512,256]{1,0:T(8,128)S(1)} %get-tuple-element.60), channel_id=1, source_target_pairs={{0,1},{1,0},{2,3},{3,2},{4,5},{5,4},{6,7},{7,6},{8,9},{9,8},{10,11... | collective-permute-start | bytes 1572872 | tf_op jit(solution)/shard_map/ppermute | solution.py:246
  61.3 0.0 collective-permute-start.11
  61.3 4.3 %collective-permute-done.11 = f32[64,256]{1,0:T(8,128)S(1)} collective-permute-done((f32[64,256]{1,0:T(8,128)S(1)}, f32[64,256]{1,0:T(8,128)S(1)}, u32[]{:S(2)}, u32[]{:S(2)}) %collective-permute-start.11) | collective-permute-done | bytes 65568 | tf_op jit(solution)/shard_map/ppermute | solution.py:246
  65.5 0.1 collective-permute-start.12
  65.6 2.9 %own_other_kernel.1 = f32[512,256]{1,0:T(8,128)S(1)} custom-call(s32[37]{0:T(128)S(1)} %get-tuple-element.65.plan, s32[16,4,512]{2,1,0:T(4,128)S(1)} %get-tuple-element.38.ids, s32[4,1,512]{2,1,0:T(1,128)S(1)} %get-tuple-element.39.negative_ids, bf16[16,512,512]{2,1,0:T(8,128)(2,1)S(1)} %get-tuple-element.62.grads, ...), custom_call_target="tpu_custom_call" | custom-call | flops 2147483648 | bytes 2097152 | tf_op jit(solution)/shard_map/own_other_kernel/pallas_call | solution.py:283
  68.6 0.0 copy-start.2
  68.6 0.0 copy-start
  68.6 0.0 copy-start.3
  68.6 2.6 %collective-permute-done.12 = f32[64,256]{1,0:T(8,128)S(1)} collective-permute-done((f32[64,256]{1,0:T(8,128)S(1)}, f32[64,256]{1,0:T(8,128)S(1)}, u32[]{:S(2)}, u32[]{:S(2)}) %collective-permute-start.12) | collective-permute-done | bytes 65568 | tf_op jit(solution)/shard_map/ppermute | solution.py:246
  71.2 2.6 %collective-permute-done.10 = f32[512,256]{1,0:T(8,128)S(1)} collective-permute-done((f32[512,256]{1,0:T(8,128)S(1)}, f32[512,256]{1,0:T(8,128)S(1)}, u32[]{:S(2)}, u32[]{:S(2)}) %collective-permute-start.10) | collective-permute-done | bytes 524320 | tf_op jit(solution)/shard_map/ppermute | solution.py:246
  73.8 0.1 add.49
  73.9 1.5 %collective-permute-start.17 = (f32[64,256]{1,0:T(8,128)S(1)}, f32[64,256]{1,0:T(8,128)S(1)}, u32[]{:S(2)}, u32[]{:S(2)}) collective-permute-start(f32[64,256]{1,0:T(8,128)S(1)} %add.51), channel_id=1, source_target_pairs={{0,5},{1,4},{2,7},{3,6},{4,1},{5,0},{6,3},{7,2},{8,13},{9,12},{10,... | collective-permute-start | bytes 196616 | tf_op jit(solution)/shard_map/ppermute | solution.py:314
  75.4 1.8 %collective-permute-start.16 = (f32[64,256]{1,0:T(8,128)S(1)}, f32[64,256]{1,0:T(8,128)S(1)}, u32[]{:S(2)}, u32[]{:S(2)}) collective-permute-start(f32[64,256]{1,0:T(8,128)S(1)} %add.51), channel_id=1, source_target_pairs={{0,4},{1,5},{2,6},{3,7},{4,0},{5,1},{6,2},{7,3},{8,12},{9,13},{10,... | collective-permute-start | bytes 196616 | tf_op jit(solution)/shard_map/ppermute | solution.py:314
  77.2 0.3 collective-permute-start.15
  77.5 0.0 collective-permute-start.13
  77.5 1.7 %collective-permute-start.14 = (f32[512,256]{1,0:T(8,128)S(1)}, f32[512,256]{1,0:T(8,128)S(1)}, u32[]{:S(2)}, u32[]{:S(2)}) collective-permute-start(f32[512,256]{1,0:T(8,128)S(1)} %own_other_kernel.1), channel_id=1, source_target_pairs={{0,1},{1,0},{2,3},{3,2},{4,5},{5,4},{6,7},{7,6},{8,9},{9,8},{10,11... | collective-permute-start | bytes 1572872 | tf_op jit(solution)/shard_map/ppermute | solution.py:246
  79.2 3.0 %collective-permute-done.15 = f32[64,256]{1,0:T(8,128)S(1)} collective-permute-done((f32[64,256]{1,0:T(8,128)S(1)}, f32[64,256]{1,0:T(8,128)S(1)}, u32[]{:S(2)}, u32[]{:S(2)}) %collective-permute-start.15) | collective-permute-done | bytes 65568 | tf_op jit(solution)/shard_map/ppermute | solution.py:314
  82.2 0.0 collective-permute-done.16
  82.2 0.0 collective-permute-done.17
  82.2 0.1 collective-permute-start.18
  82.3 2.9 %own_kernel.1.refs_1_ = f32[512,256]{1,0:T(8,128)S(1)} custom-call(s32[37]{0:T(128)S(1)} %get-tuple-element.65.plan, s32[16,4,512]{2,1,0:T(4,128)S(1)} %get-tuple-element.38.ids, s32[4,1,512]{2,1,0:T(1,128)S(1)} %get-tuple-element.39.negative_ids, bf16[16,512,512]{2,1,0:T(8,128)(2,1)S(1)} %get-tuple-element.62.grads, ...), custom_call_target="tpu_custom_call" | custom-call | flops 2147483648 | bytes 2097152 | tf_op jit(solution)/shard_map/own_kernel/pallas_call | solution.py:283
  85.3 0.0 collective-permute-done.18.theirs
  85.3 0.0 copy-done.2
  85.3 1.6 %relation_kernel.1 = f32[400,256]{1,0:T(8,128)} custom-call(s32[3]{0:T(128)S(1)} %pad_add_fusion.codes, f32[400,256]{1,0:T(8,128)S(1)} %copy-done.1, f32[1,400]{1,0:T(1,128)S(1)} %bitcast.10, f32[256,256]{1,0:T(8,128)S(1)} %constant_dynamic-update-slice_fusion.mine, f32[256,256]{1,0:T(8,128)S(1)} %collective-permute-done.18.theirs), custom_call_target="tpu_custom_call" | custom-call | flops 2097152 | bytes 2097152 | tf_op jit(solution)/shard_map/relation_kernel/pallas_call | solution.py:283
  86.9 13.2 %collective-permute-done.13.returned = f32[512,256]{1,0:T(8,128)S(1)} collective-permute-done((f32[512,256]{1,0:T(8,128)S(1)}, f32[512,256]{1,0:T(8,128)S(1)}, u32[]{:S(2)}, u32[]{:S(2)}) %collective-permute-start.13) | collective-permute-done | bytes 524320 | tf_op jit(solution)/shard_map/ppermute | solution.py:246
  100.1 0.0 collective-permute-done.14.refs_0_
  100.1 0.0 copy-done
  100.1 0.0 copy-done.3
  100.1 1.2 %entity_kernel.1 = (f32[512,256]{1,0:T(8,128)}, f32[1,512]{1,0:T(1,128)}) custom-call(f32[512,256]{1,0:T(8,128)S(1)} %copy-done, f32[1,512]{1,0:T(1,128)S(1)} %bitcast.11, f32[512,256]{1,0:T(8,128)S(1)} %collective-permute-done.13.returned, f32[512,256]{1,0:T(8,128)S(1)} %collective-permute-done.14.refs_0_, f32[512,256]{1,0:T(8,128)S(1)} %own_kernel.1.refs_1_), custom_call_target="tpu_custom_call" | custom-call | flops 2097152 | bytes 2097152 | tf_op jit(solution)/shard_map/entity_kernel/pallas_call | solution.py:283
  (8 shorter events, 0.1 us)
Async XLA Ops:
  2.1 7.9 %collective-permute-start.1 = (s16[17,3,512]{2,1,0:T(4,128)(2,1)S(1)}, s16[17,3,512]{2,1,0:T(4,128)(2,1)S(1)}, u32[]{:S(2)}, u32[]{:S(2)}) collective-permute-start(s16[17,3,512]{2,1,0:T(4,128)(2,1)S(1)} %ids_kernel.1.refs_0_), channel_id=1, source_target_pairs={{0,16},{2,18},{4,20},{6,22},{8,24},{10,26},{12,28},{14,30},{16,0},... | collective-permute-start | bytes 156680 | tf_op jit(solution)/shard_map/ppermute | solution.py:246
  6.2 5.6 %collective-permute-start = (s16[17,3,512]{2,1,0:T(4,128)(2,1)S(1)}, s16[17,3,512]{2,1,0:T(4,128)(2,1)S(1)}, u32[]{:S(2)}, u32[]{:S(2)}) collective-permute-start(s16[17,3,512]{2,1,0:T(4,128)(2,1)S(1)} %ids_kernel.1.refs_0_), channel_id=1, source_target_pairs={{0,1},{1,0},{2,3},{3,2},{4,5},{5,4},{6,7},{7,6},{8,9},{9,8},{10,11... | collective-permute-start | bytes 156680 | tf_op jit(solution)/shard_map/ppermute | solution.py:246
  8.9 15.8 %collective-permute-start.4 = (bf16[256,512]{1,0:T(8,128)(2,1)S(1)}, bf16[256,512]{1,0:T(8,128)(2,1)S(1)}, u32[]{:S(2)}, u32[]{:S(2)}) collective-permute-start(bf16[256,512]{1,0:T(8,128)(2,1)S(1)} %rows_kernel.1.refs_0_), channel_id=1, source_target_pairs={{0,1},{1,0},{2,3},{3,2},{4,5},{5,4},{6,7},{7,6},{8,9},{9,8},{10,11... | collective-permute-start | bytes 786440 | tf_op jit(solution)/shard_map/ppermute | solution.py:246
  9.5 13.7 %collective-permute-start.3 = (bf16[256,512]{1,0:T(8,128)(2,1)S(1)}, bf16[256,512]{1,0:T(8,128)(2,1)S(1)}, u32[]{:S(2)}, u32[]{:S(2)}) collective-permute-start(bf16[256,512]{1,0:T(8,128)(2,1)S(1)} %rows_kernel.1.refs_0_), channel_id=1, source_target_pairs={{0,16},{2,18},{4,20},{6,22},{8,24},{10,26},{12,28},{14,30},{16,0},... | collective-permute-start | bytes 786440 | tf_op jit(solution)/shard_map/ppermute | solution.py:246
  10.0 8.0 %collective-permute-start.2 = (s16[17,3,512]{2,1,0:T(4,128)(2,1)S(1)}, s16[17,3,512]{2,1,0:T(4,128)(2,1)S(1)}, u32[]{:S(2)}, u32[]{:S(2)}) collective-permute-start(s16[17,3,512]{2,1,0:T(4,128)(2,1)S(1)} %collective-permute-done.1.refs_2_), channel_id=1, source_target_pairs={{0,1},{1,0},{2,3},{3,2},{4,5},{5,4},{6,7},{7,6},{8,9},{9,8},{10,11... | collective-permute-start | bytes 156680 | tf_op jit(solution)/shard_map/ppermute | solution.py:246
  11.8 12.9 %copy-start.1 = (f32[400,256]{1,0:T(8,128)S(1)}, f32[400,256]{1,0:T(8,128)}, u32[]{:S(2)}) copy-start(f32[400,256]{1,0:T(8,128)} %relations.3) | copy-start | bytes 1228804
  23.2 7.1 %collective-permute-start.5 = (bf16[256,512]{1,0:T(8,128)(2,1)S(1)}, bf16[256,512]{1,0:T(8,128)(2,1)S(1)}, u32[]{:S(2)}, u32[]{:S(2)}) collective-permute-start(bf16[256,512]{1,0:T(8,128)(2,1)S(1)} %collective-permute-done.3.refs_2_), channel_id=1, source_target_pairs={{0,1},{1,0},{2,3},{3,2},{4,5},{5,4},{6,7},{7,6},{8,9},{9,8},{10,11... | collective-permute-start | bytes 786440 | tf_op jit(solution)/shard_map/ppermute | solution.py:246
  44.0 5.9 %collective-permute-start.6 = (f32[256,256]{1,0:T(8,128)S(1)}, f32[256,256]{1,0:T(8,128)S(1)}, u32[]{:S(2)}, u32[]{:S(2)}) collective-permute-start(f32[256,256]{1,0:T(8,128)S(1)} %get-tuple-element.46), channel_id=1, source_target_pairs={{0,2},{2,0},{4,6},{6,4},{8,10},{10,8},{12,14},{14,12},{16,18},{18,... | collective-permute-start | bytes 786440 | tf_op jit(solution)/shard_map/ppermute | solution.py:246
  49.9 8.8 %collective-permute-start.7 = (f32[64,256]{1,0:T(8,128)S(1)}, f32[64,256]{1,0:T(8,128)S(1)}, u32[]{:S(2)}, u32[]{:S(2)}) collective-permute-start(f32[64,256]{1,0:T(8,128)S(1)} %get-tuple-element.51), channel_id=1, source_target_pairs={{0,1},{1,0},{2,3},{3,2},{4,5},{5,4},{6,7},{7,6},{8,9},{9,8},{10,11... | collective-permute-start | bytes 196616 | tf_op jit(solution)/shard_map/ppermute | solution.py:314
  53.8 4.9 %collective-permute-start.8 = (f32[64,256]{1,0:T(8,128)S(1)}, f32[64,256]{1,0:T(8,128)S(1)}, u32[]{:S(2)}, u32[]{:S(2)}) collective-permute-start(f32[64,256]{1,0:T(8,128)S(1)} %get-tuple-element.52), channel_id=1, source_target_pairs={{0,4},{1,5},{2,6},{3,7},{4,0},{5,1},{6,2},{7,3},{8,12},{9,13},{10,... | collective-permute-start | bytes 196616 | tf_op jit(solution)/shard_map/ppermute | solution.py:314
  53.8 5.3 %collective-permute-start.9 = (f32[64,256]{1,0:T(8,128)S(1)}, f32[64,256]{1,0:T(8,128)S(1)}, u32[]{:S(2)}, u32[]{:S(2)}) collective-permute-start(f32[64,256]{1,0:T(8,128)S(1)} %get-tuple-element.53), channel_id=1, source_target_pairs={{0,5},{1,4},{2,7},{3,6},{4,1},{5,0},{6,3},{7,2},{8,13},{9,12},{10,... | collective-permute-start | bytes 196616 | tf_op jit(solution)/shard_map/ppermute | solution.py:314
  59.1 14.8 %collective-permute-start.10 = (f32[512,256]{1,0:T(8,128)S(1)}, f32[512,256]{1,0:T(8,128)S(1)}, u32[]{:S(2)}, u32[]{:S(2)}) collective-permute-start(f32[512,256]{1,0:T(8,128)S(1)} %get-tuple-element.60), channel_id=1, source_target_pairs={{0,1},{1,0},{2,3},{3,2},{4,5},{5,4},{6,7},{7,6},{8,9},{9,8},{10,11... | collective-permute-start | bytes 1572872 | tf_op jit(solution)/shard_map/ppermute | solution.py:246
  61.3 4.3 %collective-permute-start.11 = (f32[64,256]{1,0:T(8,128)S(1)}, f32[64,256]{1,0:T(8,128)S(1)}, u32[]{:S(2)}, u32[]{:S(2)}) collective-permute-start(f32[64,256]{1,0:T(8,128)S(1)} %add_add_fusion), channel_id=1, source_target_pairs={{0,8},{2,10},{4,12},{6,14},{8,0},{10,2},{12,4},{14,6},{16,24},{18,... | collective-permute-start | bytes 196616 | tf_op jit(solution)/shard_map/ppermute | solution.py:246
  65.5 5.7 %collective-permute-start.12 = (f32[64,256]{1,0:T(8,128)S(1)}, f32[64,256]{1,0:T(8,128)S(1)}, u32[]{:S(2)}, u32[]{:S(2)}) collective-permute-start(f32[64,256]{1,0:T(8,128)S(1)} %add.50), channel_id=1, source_target_pairs={{0,16},{2,18},{4,20},{6,22},{8,24},{10,26},{12,28},{14,30},{16,0},... | collective-permute-start | bytes 196616 | tf_op jit(solution)/shard_map/ppermute | solution.py:246
  68.6 16.7 %copy-start.2 = (f32[400]{0:T(512)S(1)}, f32[400]{0:T(512)}, u32[]{:S(2)}) copy-start(f32[400]{0:T(512)} %param.12) | copy-start | bytes 4804
  68.6 31.5 %copy-start = (f32[512,256]{1,0:T(8,128)S(1)}, f32[512,256]{1,0:T(8,128)}, u32[]{:S(2)}) copy-start(f32[512,256]{1,0:T(8,128)} %table.2) | copy-start | bytes 1572868
  68.6 31.5 %copy-start.3 = (f32[512]{0:T(512)S(1)}, f32[512]{0:T(512)}, u32[]{:S(2)}) copy-start(f32[512]{0:T(512)} %param.10) | copy-start | bytes 6148
  73.9 8.3 %collective-permute-start.17 = (f32[64,256]{1,0:T(8,128)S(1)}, f32[64,256]{1,0:T(8,128)S(1)}, u32[]{:S(2)}, u32[]{:S(2)}) collective-permute-start(f32[64,256]{1,0:T(8,128)S(1)} %add.51), channel_id=1, source_target_pairs={{0,5},{1,4},{2,7},{3,6},{4,1},{5,0},{6,3},{7,2},{8,13},{9,12},{10,... | collective-permute-start | bytes 196616 | tf_op jit(solution)/shard_map/ppermute | solution.py:314
  75.4 6.8 %collective-permute-start.16 = (f32[64,256]{1,0:T(8,128)S(1)}, f32[64,256]{1,0:T(8,128)S(1)}, u32[]{:S(2)}, u32[]{:S(2)}) collective-permute-start(f32[64,256]{1,0:T(8,128)S(1)} %add.51), channel_id=1, source_target_pairs={{0,4},{1,5},{2,6},{3,7},{4,0},{5,1},{6,2},{7,3},{8,12},{9,13},{10,... | collective-permute-start | bytes 196616 | tf_op jit(solution)/shard_map/ppermute | solution.py:314
  77.2 5.0 %collective-permute-start.15 = (f32[64,256]{1,0:T(8,128)S(1)}, f32[64,256]{1,0:T(8,128)S(1)}, u32[]{:S(2)}, u32[]{:S(2)}) collective-permute-start(f32[64,256]{1,0:T(8,128)S(1)} %add.51), channel_id=1, source_target_pairs={{0,1},{1,0},{2,3},{3,2},{4,5},{5,4},{6,7},{7,6},{8,9},{9,8},{10,11... | collective-permute-start | bytes 196616 | tf_op jit(solution)/shard_map/ppermute | solution.py:314
  77.5 22.7 %collective-permute-start.13 = (f32[512,256]{1,0:T(8,128)S(1)}, f32[512,256]{1,0:T(8,128)S(1)}, u32[]{:S(2)}, u32[]{:S(2)}) collective-permute-start(f32[512,256]{1,0:T(8,128)S(1)} %add.49), channel_id=1, source_target_pairs={{0,16},{2,18},{4,20},{6,22},{8,24},{10,26},{12,28},{14,30},{16,0},... | collective-permute-start | bytes 1572872 | tf_op jit(solution)/shard_map/ppermute | solution.py:246
  77.5 22.7 %collective-permute-start.14 = (f32[512,256]{1,0:T(8,128)S(1)}, f32[512,256]{1,0:T(8,128)S(1)}, u32[]{:S(2)}, u32[]{:S(2)}) collective-permute-start(f32[512,256]{1,0:T(8,128)S(1)} %own_other_kernel.1), channel_id=1, source_target_pairs={{0,1},{1,0},{2,3},{3,2},{4,5},{5,4},{6,7},{7,6},{8,9},{9,8},{10,11... | collective-permute-start | bytes 1572872 | tf_op jit(solution)/shard_map/ppermute | solution.py:246
  82.2 3.0 %collective-permute-start.18 = (f32[256,256]{1,0:T(8,128)S(1)}, f32[256,256]{1,0:T(8,128)S(1)}, u32[]{:S(2)}, u32[]{:S(2)}) collective-permute-start(f32[256,256]{1,0:T(8,128)S(1)} %constant_dynamic-update-slice_fusion.mine), channel_id=1, source_target_pairs={{0,2},{2,0},{4,6},{6,4},{8,10},{10,8},{12,14},{14,12},{16,18},{18,... | collective-permute-start | bytes 786440 | tf_op jit(solution)/shard_map/ppermute | solution.py:246

commit v6 on v5

--- a/solution.py
+++ b/solution.py
@@ -138,8 +138,8 @@
 def edge_kernel(n, plan, ids, negative_ids, near_in, operator_in, *refs):
     near, away = refs[:n], refs[n : 2 * n]
     near_grad, away_grad, negative_out = refs[2 * n : 2 * n + 3]
-    away_other = refs[2 * n + 3 : 3 * n + 2]
-    relation_sum, (table, table_t, negative_grad) = refs[3 * n + 2 : -3], refs[-3:]
+    away_out, away_other = refs[2 * n + 3 : 3 * n + 2], refs[1 - n :]
+    relation_sum, (table, table_t, negative_grad) = refs[3 * n + 2 : -2 - n], refs[-2 - n : 1 - n]
     most, _, width = ids.shape
     steps = plan[2 * most]
     count = table.shape[0]
@@ -197,6 +197,8 @@
         return carry
 
     lax.fori_loop(0, steps, one_block, 0)
+    for total, out in zip(away_other, away_out, strict=True):
+        out[...] = total[...].astype(bf16)
 
 
 def scatter_kernel(row, start, first, plan, ids, negative_ids, grads, negative_grads, *sums):
@@ -218,7 +220,7 @@
 
 def entity_kernel(n, table, state, returned, *refs):
     parts, (new_table, new_state) = refs[:n], refs[n:]
-    grad = returned[...]
+    grad = returned[...].astype(f32)
     for part in parts:
         grad = grad + part[...]
     lanes = 128
@@ -351,10 +353,11 @@
         functools.partial(edge_kernel, n),
         "edge_kernel",
         [pair_out, pair_out, ((team, 2 * count, dims), bf16)]
-        + [sums] * (n - 1)
+        + [((rows, dims), bf16)] * (n - 1)
         + [((chunk, dims), f32)] * chips
         + [((chips * chunk, dims), f32)],
-        [pltpu.VMEM((count, dims), bf16), pltpu.VMEM((dims, count), bf16), pltpu.VMEM((count, dims), f32)],
+        [pltpu.VMEM((count, dims), bf16), pltpu.VMEM((dims, count), bf16), pltpu.VMEM((count, dims), f32)]
+        + [pltpu.VMEM((rows, dims), f32)] * (n - 1),
         (2 * n - 1) * rows + 3 * count + 2 * rel_rows,
         (plan,),
         (step_ids, negative_ids, near_rows, operator, *near_slab, *away_slab),
@@ -381,16 +384,17 @@
     chunk_total = partial[0]
     for k in range(1, chips):
         chunk_total = chunk_total + to_chip(partial[k], k)
+    away_received = [exchange(away_other[k - 1], "sub", k) for k in range(1, n)]
     (away_total,) = scatter("away_kernel", 1, 0, 1, 0, plan, away_grad)
-    chunk_total, away_total, plan, *away_other = lax.optimization_barrier((chunk_total, away_total, plan, *away_other))
-    away_received = [exchange(away_other[k - 1], "sub", k) for k in range(1, n)]
+    chunk_total, away_total, plan = lax.optimization_barrier((chunk_total, away_total, plan))
     mask = 4
     while mask < n_dom:
         chunk_total = chunk_total + exchange(chunk_total, "dom", mask)
         mask *= 2
     near_other = scatter("own_other_kernel", 0, rows, n - 1, n, plan, near_grad)
     for x in away_received:
-        away_total = away_total + x
+        away_total = away_total + x.astype(f32)
+    away_total = away_total.astype(bf16)
     plan, away_total, chunk_total, *near_other = lax.optimization_barrier((plan, away_total, chunk_total, *near_other))
     returned = exchange(away_total, "dom", pair)
     mine = jnp.concatenate([chunk_total] + [to_chip(chunk_total, k) for k in range(1, chips)], axis=0)

time: 102 us -> 97.3 us (0.954)
  waiting for transfers between devices: 38.8 us -> 29 us
  starting transfers between devices: 27.2 us -> 33.2 us
    ppermute x13, waiting for transfers between devices: 35.4 us -> 23.1 us  [exchange(): lax.ppermute(x, axis, [(i, i ^ mask) for i in range(lax.axis_size(axis))])]
    ppermute x13, starting transfers between devices: 18.2 us -> 25.9 us  [exchange(): lax.ppermute(x, axis, [(i, i ^ mask) for i in range(lax.axis_size(axis))])]
    ppermute x6, waiting for transfers between devices: 3.33 us -> 5.95 us  [to_peer(): return lax.ppermute(x, ('dom', 'sub'), pairs)]
    ppermute x6, starting transfers between devices: 8.97 us -> 7.29 us  [to_peer(): return lax.ppermute(x, ('dom', 'sub'), pairs)]
  transfers between devices with their start and end apart: 19 -> 19, of which waited for: 11 -> 9; matrix products, arithmetic and copies ran while one was open for 0% -> 0% of each run, Pallas kernels for 18% -> 18%
where the time goes in v6:
time: 97.3 us; the launch traced here: 97.5 us
  Pallas kernels  33.6 us (35%)
  starting transfers between devices  33.2 us (34%)
  waiting for transfers between devices  29 us (30%)
  between operations  1.47 us (2%)
    pallas_call x9, Pallas kernels, call(): pl.pallas_call(kernel, in_specs=[in_smem] * len(scalars) + [in_vmem] * le...  32 us
    ppermute x13, starting transfers between devices, exchange(): lax.ppermute(x, axis, [(i, i ^ mask) for i in range(lax.axis_size(axis))])  25.9 us
    ppermute x13, waiting for transfers between devices, exchange(): lax.ppermute(x, axis, [(i, i ^ mask) for i in range(lax.axis_size(axis))])  23.1 us
    ppermute x6, starting transfers between devices, to_peer(): return lax.ppermute(x, ('dom', 'sub'), pairs)  7.29 us
    ppermute x6, waiting for transfers between devices, to_peer(): return lax.ppermute(x, ('dom', 'sub'), pairs)  5.95 us
  transfers between devices with their start and end apart: 19, of which 9 were waited for; matrix products, arithmetic and copies ran while one was open for 0% of the time, Pallas kernels for 18%

profile of v6, /device:TPU:0, one launch (start us, length us, event | category | flops | bytes accessed | tf_op | source)
XLA Modules:
  0.0 97.5 jit_solution(8081048152040425216)
XLA Ops:
  1.3 0.8 ids_kernel.1.refs_0_
  2.1 4.1 %collective-permute-start.1 = (s16[17,3,512]{2,1,0:T(4,128)(2,1)S(1)}, s16[17,3,512]{2,1,0:T(4,128)(2,1)S(1)}, u32[]{:S(2)}, u32[]{:S(2)}) collective-permute-start(s16[17,3,512]{2,1,0:T(4,128)(2,1)S(1)} %ids_kernel.1.refs_0_), channel_id=1, source_target_pairs={{0,16},{2,18},{4,20},{6,22},{8,24},{10,26},{12,28},{14,30},{16,0},... | collective-permute-start | bytes 156680 | tf_op jit(solution)/shard_map/ppermute | solution.py:248
  6.2 1.5 %collective-permute-start = (s16[17,3,512]{2,1,0:T(4,128)(2,1)S(1)}, s16[17,3,512]{2,1,0:T(4,128)(2,1)S(1)}, u32[]{:S(2)}, u32[]{:S(2)}) collective-permute-start(s16[17,3,512]{2,1,0:T(4,128)(2,1)S(1)} %ids_kernel.1.refs_0_), channel_id=1, source_target_pairs={{0,1},{1,0},{2,3},{3,2},{4,5},{5,4},{6,7},{7,6},{8,9},{9,8},{10,11... | collective-permute-start | bytes 156680 | tf_op jit(solution)/shard_map/ppermute | solution.py:248
  7.7 1.2 %rows_kernel.1.refs_0_ = bf16[256,512]{1,0:T(8,128)(2,1)S(1)} custom-call(f32[512,256]{1,0:T(8,128)} %table.2), custom_call_target="tpu_custom_call" | custom-call | flops 2097152 | bytes 2097152 | tf_op jit(solution)/shard_map/rows_kernel/pallas_call | solution.py:285
  8.9 0.6 collective-permute-start.4
  9.5 0.1 collective-permute-start.3
  9.6 0.4 collective-permute-done.1.refs_2_
  10.0 1.7 %collective-permute-start.2 = (s16[17,3,512]{2,1,0:T(4,128)(2,1)S(1)}, s16[17,3,512]{2,1,0:T(4,128)(2,1)S(1)}, u32[]{:S(2)}, u32[]{:S(2)}) collective-permute-start(s16[17,3,512]{2,1,0:T(4,128)(2,1)S(1)} %collective-permute-done.1.refs_2_), channel_id=1, source_target_pairs={{0,1},{1,0},{2,3},{3,2},{4,5},{5,4},{6,7},{7,6},{8,9},{9,8},{10,11... | collective-permute-start | bytes 156680 | tf_op jit(solution)/shard_map/ppermute | solution.py:248
  11.7 0.1 pad_add_fusion.codes
  11.8 0.0 copy-start.1
  11.8 0.0 collective-permute-done.refs_1_
  11.8 6.2 %collective-permute-done.2.refs_3_ = s16[17,3,512]{2,1,0:T(4,128)(2,1)S(1)} collective-permute-done((s16[17,3,512]{2,1,0:T(4,128)(2,1)S(1)}, s16[17,3,512]{2,1,0:T(4,128)(2,1)S(1)}, u32[]{:S(2)}, u32[]{:S(2)}) %collective-permute-start.2) | collective-permute-done | bytes 52256 | tf_op jit(solution)/shard_map/ppermute | solution.py:248
  18.0 1.6 %plan_kernel.1 = (s32[37]{0:T(128)S(1)}, s32[16,4,512]{2,1,0:T(4,128)S(1)}, s32[4,1,512]{2,1,0:T(1,128)S(1)}) custom-call(s32[3]{0:T(128)S(1)} %pad_add_fusion.codes, s16[17,3,512]{2,1,0:T(4,128)(2,1)S(1)} %ids_kernel.1.refs_0_, s16[17,3,512]{2,1,0:T(4,128)(2,1)S(1)} %collective-permute-done.refs_1_, s16[17,3,512]{2,1,0:T(4,128)(2,1)S(1)} %collective-permute-done.1.refs_2_, ...), custom_call_target="tpu_custom_call" | custom-call | flops 34359738368 | bytes 2097152 | tf_op jit(solution)/shard_map/plan_kernel/pallas_call | solution.py:325
  19.5 3.7 %collective-permute-done.3.refs_2_ = bf16[256,512]{1,0:T(8,128)(2,1)S(1)} collective-permute-done((bf16[256,512]{1,0:T(8,128)(2,1)S(1)}, bf16[256,512]{1,0:T(8,128)(2,1)S(1)}, u32[]{:S(2)}, u32[]{:S(2)}) %collective-permute-start.3) | collective-permute-done | bytes 262176 | tf_op jit(solution)/shard_map/ppermute | solution.py:248
  23.2 1.5 %collective-permute-start.5 = (bf16[256,512]{1,0:T(8,128)(2,1)S(1)}, bf16[256,512]{1,0:T(8,128)(2,1)S(1)}, u32[]{:S(2)}, u32[]{:S(2)}) collective-permute-start(bf16[256,512]{1,0:T(8,128)(2,1)S(1)} %collective-permute-done.3.refs_2_), channel_id=1, source_target_pairs={{0,1},{1,0},{2,3},{3,2},{4,5},{5,4},{6,7},{7,6},{8,9},{9,8},{10,11... | collective-permute-start | bytes 786440 | tf_op jit(solution)/shard_map/ppermute | solution.py:248
  24.7 0.0 collective-permute-done.4.refs_1_
  24.7 0.0 copy-done.1
  24.7 4.3 %near_kernel.1 = (bf16[16,256,512]{2,1,0:T(8,128)(2,1)S(1)}, f32[16,256,512]{2,1,0:T(8,128)S(1)}) custom-call(s32[37]{0:T(128)S(1)} %get-tuple-element.63.plan, s32[16,4,512]{2,1,0:T(4,128)S(1)} %get-tuple-element.37.ids, f32[400,256]{1,0:T(8,128)S(1)} %copy-done.1, bf16[256,512]{1,0:T(8,128)(2,1)S(1)} %rows_kernel.1.refs_0_, ...), custom_call_target="tpu_custom_call" | custom-call | flops 4294967296 | bytes 2097152 | tf_op jit(solution)/shard_map/near_kernel/pallas_call | solution.py:285
  29.1 1.3 %collective-permute-done.5.refs_3_ = bf16[256,512]{1,0:T(8,128)(2,1)S(1)} collective-permute-done((bf16[256,512]{1,0:T(8,128)(2,1)S(1)}, bf16[256,512]{1,0:T(8,128)(2,1)S(1)}, u32[]{:S(2)}, u32[]{:S(2)}) %collective-permute-start.5) | collective-permute-done | bytes 262176 | tf_op jit(solution)/shard_map/ppermute | solution.py:248
  30.4 13.6 %edge_kernel.1 = (bf16[16,512,512]{2,1,0:T(8,128)(2,1)S(1)}, bf16[16,512,512]{2,1,0:T(8,128)(2,1)S(1)}, bf16[4,1024,256]{2,1,0:T(8,128)(2,1)S(1)}, bf16[512,256]...) custom-call(s32[37]{0:T(128)S(1)} %get-tuple-element.63.plan, ...), custom_call_target="tpu_custom_call" | custom-call | flops 8589934592 | bytes 2097152 | tf_op jit(solution)/shard_map/edge_kernel/pallas_call | solution.py:285
  44.0 1.6 %collective-permute-start.6 = (f32[256,256]{1,0:T(8,128)S(1)}, f32[256,256]{1,0:T(8,128)S(1)}, u32[]{:S(2)}, u32[]{:S(2)}) collective-permute-start(f32[256,256]{1,0:T(8,128)S(1)} %get-tuple-element.45), channel_id=1, source_target_pairs={{0,2},{2,0},{4,6},{6,4},{8,10},{10,8},{12,14},{14,12},{16,18},{18,... | collective-permute-start | bytes 786440 | tf_op jit(solution)/shard_map/ppermute | solution.py:248
  45.6 0.7 collective-permute-start.10
  46.3 0.5 collective-permute-done.6
  46.8 1.1 %collective-permute-start.7 = (f32[64,256]{1,0:T(8,128)S(1)}, f32[64,256]{1,0:T(8,128)S(1)}, u32[]{:S(2)}, u32[]{:S(2)}) collective-permute-start(f32[64,256]{1,0:T(8,128)S(1)} %get-tuple-element.50), channel_id=1, source_target_pairs={{0,1},{1,0},{2,3},{3,2},{4,5},{5,4},{6,7},{7,6},{8,9},{9,8},{10,11... | collective-permute-start | bytes 196616 | tf_op jit(solution)/shard_map/ppermute | solution.py:316
  47.8 1.9 %collective-permute-start.8 = (f32[64,256]{1,0:T(8,128)S(1)}, f32[64,256]{1,0:T(8,128)S(1)}, u32[]{:S(2)}, u32[]{:S(2)}) collective-permute-start(f32[64,256]{1,0:T(8,128)S(1)} %get-tuple-element.51), channel_id=1, source_target_pairs={{0,4},{1,5},{2,6},{3,7},{4,0},{5,1},{6,2},{7,3},{8,12},{9,13},{10,... | collective-permute-start | bytes 196616 | tf_op jit(solution)/shard_map/ppermute | solution.py:316
  49.8 0.6 collective-permute-start.9
  50.4 3.4 %away_kernel.1 = f32[512,256]{1,0:T(8,128)S(1)} custom-call(s32[37]{0:T(128)S(1)} %get-tuple-element.63.plan, s32[16,4,512]{2,1,0:T(4,128)S(1)} %get-tuple-element.37.ids, s32[4,1,512]{2,1,0:T(1,128)S(1)} %get-tuple-element.38.negative_ids, bf16[16,512,512]{2,1,0:T(8,128)(2,1)S(1)} %get-tuple-element.54.grads, ...), custom_call_target="tpu_custom_call" | custom-call | flops 2147483648 | bytes 2097152 | tf_op jit(solution)/shard_map/away_kernel/pallas_call | solution.py:285
  53.7 2.9 %collective-permute-done.7 = f32[64,256]{1,0:T(8,128)S(1)} collective-permute-done((f32[64,256]{1,0:T(8,128)S(1)}, f32[64,256]{1,0:T(8,128)S(1)}, u32[]{:S(2)}, u32[]{:S(2)}) %collective-permute-start.7) | collective-permute-done | bytes 65568 | tf_op jit(solution)/shard_map/ppermute | solution.py:316
  56.7 0.0 collective-permute-done.8
  56.7 0.0 collective-permute-done.9
  56.7 6.0 %collective-permute-start.11 = (f32[64,256]{1,0:T(8,128)S(1)}, f32[64,256]{1,0:T(8,128)S(1)}, u32[]{:S(2)}, u32[]{:S(2)}) collective-permute-start(f32[64,256]{1,0:T(8,128)S(1)} %add_add_fusion), channel_id=1, source_target_pairs={{0,8},{2,10},{4,12},{6,14},{8,0},{10,2},{12,4},{14,6},{16,24},{18,... | collective-permute-start | bytes 196616 | tf_op jit(solution)/shard_map/ppermute | solution.py:248
  62.7 0.0 collective-permute-done.10
  62.7 0.1 add_convert_fusion
  62.8 2.2 %collective-permute-done.11 = f32[64,256]{1,0:T(8,128)S(1)} collective-permute-done((f32[64,256]{1,0:T(8,128)S(1)}, f32[64,256]{1,0:T(8,128)S(1)}, u32[]{:S(2)}, u32[]{:S(2)}) %collective-permute-start.11) | collective-permute-done | bytes 65568 | tf_op jit(solution)/shard_map/ppermute | solution.py:248
  65.0 4.2 %collective-permute-start.12 = (f32[64,256]{1,0:T(8,128)S(1)}, f32[64,256]{1,0:T(8,128)S(1)}, u32[]{:S(2)}, u32[]{:S(2)}) collective-permute-start(f32[64,256]{1,0:T(8,128)S(1)} %add.50), channel_id=1, source_target_pairs={{0,16},{2,18},{4,20},{6,22},{8,24},{10,26},{12,28},{14,30},{16,0},... | collective-permute-start | bytes 196616 | tf_op jit(solution)/shard_map/ppermute | solution.py:248
  69.2 2.9 %own_other_kernel.1 = f32[512,256]{1,0:T(8,128)S(1)} custom-call(s32[37]{0:T(128)S(1)} %get-tuple-element.63.plan, s32[16,4,512]{2,1,0:T(4,128)S(1)} %get-tuple-element.37.ids, s32[4,1,512]{2,1,0:T(1,128)S(1)} %get-tuple-element.38.negative_ids, bf16[16,512,512]{2,1,0:T(8,128)(2,1)S(1)} %get-tuple-element.60.grads, ...), custom_call_target="tpu_custom_call" | custom-call | flops 2147483648 | bytes 2097152 | tf_op jit(solution)/shard_map/own_other_kernel/pallas_call | solution.py:285
  72.1 0.0 copy-start.2
  72.2 0.0 copy-start
  72.2 0.0 copy-start.3
  72.2 0.0 collective-permute-done.12
  72.2 0.1 collective-permute-start.17
  72.3 3.6 %collective-permute-start.16 = (f32[64,256]{1,0:T(8,128)S(1)}, f32[64,256]{1,0:T(8,128)S(1)}, u32[]{:S(2)}, u32[]{:S(2)}) collective-permute-start(f32[64,256]{1,0:T(8,128)S(1)} %add.51), channel_id=1, source_target_pairs={{0,4},{1,5},{2,6},{3,7},{4,0},{5,1},{6,2},{7,3},{8,12},{9,13},{10,... | collective-permute-start | bytes 196616 | tf_op jit(solution)/shard_map/ppermute | solution.py:316
  75.9 0.0 collective-permute-start.15
  75.9 2.0 %collective-permute-start.14 = (f32[512,256]{1,0:T(8,128)S(1)}, f32[512,256]{1,0:T(8,128)S(1)}, u32[]{:S(2)}, u32[]{:S(2)}) collective-permute-start(f32[512,256]{1,0:T(8,128)S(1)} %own_other_kernel.1), channel_id=1, source_target_pairs={{0,1},{1,0},{2,3},{3,2},{4,5},{5,4},{6,7},{7,6},{8,9},{9,8},{10,11... | collective-permute-start | bytes 1572872 | tf_op jit(solution)/shard_map/ppermute | solution.py:248
  78.0 3.0 %collective-permute-done.15 = f32[64,256]{1,0:T(8,128)S(1)} collective-permute-done((f32[64,256]{1,0:T(8,128)S(1)}, f32[64,256]{1,0:T(8,128)S(1)}, u32[]{:S(2)}, u32[]{:S(2)}) %collective-permute-start.15) | collective-permute-done | bytes 65568 | tf_op jit(solution)/shard_map/ppermute | solution.py:316
  81.0 0.0 collective-permute-done.16
  81.0 0.0 collective-permute-done.17
  81.0 0.1 collective-permute-start.18
  81.1 1.8 %collective-permute-start.13 = (bf16[512,256]{1,0:T(8,128)(2,1)S(1)}, bf16[512,256]{1,0:T(8,128)(2,1)S(1)}, u32[]{:S(2)}, u32[]{:S(2)}) collective-permute-start(bf16[512,256]{1,0:T(8,128)(2,1)S(1)} %add_convert_fusion), channel_id=1, source_target_pairs={{0,16},{2,18},{4,20},{6,22},{8,24},{10,26},{12,28},{14,30},{16,0},... | collective-permute-start | bytes 786440 | tf_op jit(solution)/shard_map/ppermute | solution.py:248
  82.9 2.9 %own_kernel.1.refs_1_ = f32[512,256]{1,0:T(8,128)S(1)} custom-call(s32[37]{0:T(128)S(1)} %get-tuple-element.63.plan, s32[16,4,512]{2,1,0:T(4,128)S(1)} %get-tuple-element.37.ids, s32[4,1,512]{2,1,0:T(1,128)S(1)} %get-tuple-element.38.negative_ids, bf16[16,512,512]{2,1,0:T(8,128)(2,1)S(1)} %get-tuple-element.60.grads, ...), custom_call_target="tpu_custom_call" | custom-call | flops 2147483648 | bytes 2097152 | tf_op jit(solution)/shard_map/own_kernel/pallas_call | solution.py:285
  85.8 0.0 collective-permute-done.18.theirs
  85.9 0.0 copy-done.2
  85.9 1.6 %relation_kernel.1 = f32[400,256]{1,0:T(8,128)} custom-call(s32[3]{0:T(128)S(1)} %pad_add_fusion.codes, f32[400,256]{1,0:T(8,128)S(1)} %copy-done.1, f32[1,400]{1,0:T(1,128)S(1)} %bitcast.10, f32[256,256]{1,0:T(8,128)S(1)} %constant_dynamic-update-slice_fusion.mine, f32[256,256]{1,0:T(8,128)S(1)} %collective-permute-done.18.theirs), custom_call_target="tpu_custom_call" | custom-call | flops 2097152 | bytes 2097152 | tf_op jit(solution)/shard_map/relation_kernel/pallas_call | solution.py:285
  87.5 8.8 %collective-permute-done.13.returned = bf16[512,256]{1,0:T(8,128)(2,1)S(1)} collective-permute-done((bf16[512,256]{1,0:T(8,128)(2,1)S(1)}, bf16[512,256]{1,0:T(8,128)(2,1)S(1)}, u32[]{:S(2)}, u32[]{:S(2)}) %collective-permute-start.13) | collective-permute-done | bytes 262176 | tf_op jit(solution)/shard_map/ppermute | solution.py:248
  96.3 0.0 collective-permute-done.14.refs_0_
  96.3 0.0 copy-done
  96.3 0.0 copy-done.3
  96.3 1.2 %entity_kernel.1 = (f32[512,256]{1,0:T(8,128)}, f32[1,512]{1,0:T(1,128)}) custom-call(f32[512,256]{1,0:T(8,128)S(1)} %copy-done, f32[1,512]{1,0:T(1,128)S(1)} %bitcast.11, bf16[512,256]{1,0:T(8,128)(2,1)S(1)} %collective-permute-done.13.returned, f32[512,256]{1,0:T(8,128)S(1)} %collective-permute-done.14.refs_0_, f32[512,256]{1,0:T(8,128)S(1)} %own_kernel.1.refs_1_), custom_call_target="tpu_custom_call" | custom-call | flops 2097152 | bytes 2097152 | tf_op jit(solution)/shard_map/entity_kernel/pallas_call | solution.py:285
  (8 shorter events, 0.1 us)
Async XLA Ops:
  2.1 7.9 %collective-permute-start.1 = (s16[17,3,512]{2,1,0:T(4,128)(2,1)S(1)}, s16[17,3,512]{2,1,0:T(4,128)(2,1)S(1)}, u32[]{:S(2)}, u32[]{:S(2)}) collective-permute-start(s16[17,3,512]{2,1,0:T(4,128)(2,1)S(1)} %ids_kernel.1.refs_0_), channel_id=1, source_target_pairs={{0,16},{2,18},{4,20},{6,22},{8,24},{10,26},{12,28},{14,30},{16,0},... | collective-permute-start | bytes 156680 | tf_op jit(solution)/shard_map/ppermute | solution.py:248
  6.2 5.6 %collective-permute-start = (s16[17,3,512]{2,1,0:T(4,128)(2,1)S(1)}, s16[17,3,512]{2,1,0:T(4,128)(2,1)S(1)}, u32[]{:S(2)}, u32[]{:S(2)}) collective-permute-start(s16[17,3,512]{2,1,0:T(4,128)(2,1)S(1)} %ids_kernel.1.refs_0_), channel_id=1, source_target_pairs={{0,1},{1,0},{2,3},{3,2},{4,5},{5,4},{6,7},{7,6},{8,9},{9,8},{10,11... | collective-permute-start | bytes 156680 | tf_op jit(solution)/shard_map/ppermute | solution.py:248
  8.9 15.8 %collective-permute-start.4 = (bf16[256,512]{1,0:T(8,128)(2,1)S(1)}, bf16[256,512]{1,0:T(8,128)(2,1)S(1)}, u32[]{:S(2)}, u32[]{:S(2)}) collective-permute-start(bf16[256,512]{1,0:T(8,128)(2,1)S(1)} %rows_kernel.1.refs_0_), channel_id=1, source_target_pairs={{0,1},{1,0},{2,3},{3,2},{4,5},{5,4},{6,7},{7,6},{8,9},{9,8},{10,11... | collective-permute-start | bytes 786440 | tf_op jit(solution)/shard_map/ppermute | solution.py:248
  9.5 13.7 %collective-permute-start.3 = (bf16[256,512]{1,0:T(8,128)(2,1)S(1)}, bf16[256,512]{1,0:T(8,128)(2,1)S(1)}, u32[]{:S(2)}, u32[]{:S(2)}) collective-permute-start(bf16[256,512]{1,0:T(8,128)(2,1)S(1)} %rows_kernel.1.refs_0_), channel_id=1, source_target_pairs={{0,16},{2,18},{4,20},{6,22},{8,24},{10,26},{12,28},{14,30},{16,0},... | collective-permute-start | bytes 786440 | tf_op jit(solution)/shard_map/ppermute | solution.py:248
  10.0 8.0 %collective-permute-start.2 = (s16[17,3,512]{2,1,0:T(4,128)(2,1)S(1)}, s16[17,3,512]{2,1,0:T(4,128)(2,1)S(1)}, u32[]{:S(2)}, u32[]{:S(2)}) collective-permute-start(s16[17,3,512]{2,1,0:T(4,128)(2,1)S(1)} %collective-permute-done.1.refs_2_), channel_id=1, source_target_pairs={{0,1},{1,0},{2,3},{3,2},{4,5},{5,4},{6,7},{7,6},{8,9},{9,8},{10,11... | collective-permute-start | bytes 156680 | tf_op jit(solution)/shard_map/ppermute | solution.py:248
  11.8 12.9 %copy-start.1 = (f32[400,256]{1,0:T(8,128)S(1)}, f32[400,256]{1,0:T(8,128)}, u32[]{:S(2)}) copy-start(f32[400,256]{1,0:T(8,128)} %relations.3) | copy-start | bytes 1228804
  23.2 7.1 %collective-permute-start.5 = (bf16[256,512]{1,0:T(8,128)(2,1)S(1)}, bf16[256,512]{1,0:T(8,128)(2,1)S(1)}, u32[]{:S(2)}, u32[]{:S(2)}) collective-permute-start(bf16[256,512]{1,0:T(8,128)(2,1)S(1)} %collective-permute-done.3.refs_2_), channel_id=1, source_target_pairs={{0,1},{1,0},{2,3},{3,2},{4,5},{5,4},{6,7},{7,6},{8,9},{9,8},{10,11... | collective-permute-start | bytes 786440 | tf_op jit(solution)/shard_map/ppermute | solution.py:248
  44.0 2.7 %collective-permute-start.6 = (f32[256,256]{1,0:T(8,128)S(1)}, f32[256,256]{1,0:T(8,128)S(1)}, u32[]{:S(2)}, u32[]{:S(2)}) collective-permute-start(f32[256,256]{1,0:T(8,128)S(1)} %get-tuple-element.45), channel_id=1, source_target_pairs={{0,2},{2,0},{4,6},{6,4},{8,10},{10,8},{12,14},{14,12},{16,18},{18,... | collective-permute-start | bytes 786440 | tf_op jit(solution)/shard_map/ppermute | solution.py:248
  45.6 17.1 %collective-permute-start.10 = (bf16[512,256]{1,0:T(8,128)(2,1)S(1)}, bf16[512,256]{1,0:T(8,128)(2,1)S(1)}, u32[]{:S(2)}, u32[]{:S(2)}) collective-permute-start(bf16[512,256]{1,0:T(8,128)(2,1)S(1)} %get-tuple-element.58), channel_id=1, source_target_pairs={{0,1},{1,0},{2,3},{3,2},{4,5},{5,4},{6,7},{7,6},{8,9},{9,8},{10,11... | collective-permute-start | bytes 786440 | tf_op jit(solution)/shard_map/ppermute | solution.py:248
  46.8 9.9 %collective-permute-start.7 = (f32[64,256]{1,0:T(8,128)S(1)}, f32[64,256]{1,0:T(8,128)S(1)}, u32[]{:S(2)}, u32[]{:S(2)}) collective-permute-start(f32[64,256]{1,0:T(8,128)S(1)} %get-tuple-element.50), channel_id=1, source_target_pairs={{0,1},{1,0},{2,3},{3,2},{4,5},{5,4},{6,7},{7,6},{8,9},{9,8},{10,11... | collective-permute-start | bytes 196616 | tf_op jit(solution)/shard_map/ppermute | solution.py:316
  47.8 8.9 %collective-permute-start.8 = (f32[64,256]{1,0:T(8,128)S(1)}, f32[64,256]{1,0:T(8,128)S(1)}, u32[]{:S(2)}, u32[]{:S(2)}) collective-permute-start(f32[64,256]{1,0:T(8,128)S(1)} %get-tuple-element.51), channel_id=1, source_target_pairs={{0,4},{1,5},{2,6},{3,7},{4,0},{5,1},{6,2},{7,3},{8,12},{9,13},{10,... | collective-permute-start | bytes 196616 | tf_op jit(solution)/shard_map/ppermute | solution.py:316
  49.8 6.9 %collective-permute-start.9 = (f32[64,256]{1,0:T(8,128)S(1)}, f32[64,256]{1,0:T(8,128)S(1)}, u32[]{:S(2)}, u32[]{:S(2)}) collective-permute-start(f32[64,256]{1,0:T(8,128)S(1)} %get-tuple-element.52), channel_id=1, source_target_pairs={{0,5},{1,4},{2,7},{3,6},{4,1},{5,0},{6,3},{7,2},{8,13},{9,12},{10,... | collective-permute-start | bytes 196616 | tf_op jit(solution)/shard_map/ppermute | solution.py:316
  56.7 8.2 %collective-permute-start.11 = (f32[64,256]{1,0:T(8,128)S(1)}, f32[64,256]{1,0:T(8,128)S(1)}, u32[]{:S(2)}, u32[]{:S(2)}) collective-permute-start(f32[64,256]{1,0:T(8,128)S(1)} %add_add_fusion), channel_id=1, source_target_pairs={{0,8},{2,10},{4,12},{6,14},{8,0},{10,2},{12,4},{14,6},{16,24},{18,... | collective-permute-start | bytes 196616 | tf_op jit(solution)/shard_map/ppermute | solution.py:248
  65.0 7.2 %collective-permute-start.12 = (f32[64,256]{1,0:T(8,128)S(1)}, f32[64,256]{1,0:T(8,128)S(1)}, u32[]{:S(2)}, u32[]{:S(2)}) collective-permute-start(f32[64,256]{1,0:T(8,128)S(1)} %add.50), channel_id=1, source_target_pairs={{0,16},{2,18},{4,20},{6,22},{8,24},{10,26},{12,28},{14,30},{16,0},... | collective-permute-start | bytes 196616 | tf_op jit(solution)/shard_map/ppermute | solution.py:248
  72.1 13.7 %copy-start.2 = (f32[400]{0:T(512)S(1)}, f32[400]{0:T(512)}, u32[]{:S(2)}) copy-start(f32[400]{0:T(512)} %param.12) | copy-start | bytes 4804
  72.2 24.2 %copy-start = (f32[512,256]{1,0:T(8,128)S(1)}, f32[512,256]{1,0:T(8,128)}, u32[]{:S(2)}) copy-start(f32[512,256]{1,0:T(8,128)} %table.2) | copy-start | bytes 1572868
  72.2 24.2 %copy-start.3 = (f32[512]{0:T(512)S(1)}, f32[512]{0:T(512)}, u32[]{:S(2)}) copy-start(f32[512]{0:T(512)} %param.10) | copy-start | bytes 6148
  72.2 8.8 %collective-permute-start.17 = (f32[64,256]{1,0:T(8,128)S(1)}, f32[64,256]{1,0:T(8,128)S(1)}, u32[]{:S(2)}, u32[]{:S(2)}) collective-permute-start(f32[64,256]{1,0:T(8,128)S(1)} %add.51), channel_id=1, source_target_pairs={{0,5},{1,4},{2,7},{3,6},{4,1},{5,0},{6,3},{7,2},{8,13},{9,12},{10,... | collective-permute-start | bytes 196616 | tf_op jit(solution)/shard_map/ppermute | solution.py:316
  72.3 8.7 %collective-permute-start.16 = (f32[64,256]{1,0:T(8,128)S(1)}, f32[64,256]{1,0:T(8,128)S(1)}, u32[]{:S(2)}, u32[]{:S(2)}) collective-permute-start(f32[64,256]{1,0:T(8,128)S(1)} %add.51), channel_id=1, source_target_pairs={{0,4},{1,5},{2,6},{3,7},{4,0},{5,1},{6,2},{7,3},{8,12},{9,13},{10,... | collective-permute-start | bytes 196616 | tf_op jit(solution)/shard_map/ppermute | solution.py:316
  75.9 5.0 %collective-permute-start.15 = (f32[64,256]{1,0:T(8,128)S(1)}, f32[64,256]{1,0:T(8,128)S(1)}, u32[]{:S(2)}, u32[]{:S(2)}) collective-permute-start(f32[64,256]{1,0:T(8,128)S(1)} %add.51), channel_id=1, source_target_pairs={{0,1},{1,0},{2,3},{3,2},{4,5},{5,4},{6,7},{7,6},{8,9},{9,8},{10,11... | collective-permute-start | bytes 196616 | tf_op jit(solution)/shard_map/ppermute | solution.py:316
  75.9 20.4 %collective-permute-start.14 = (f32[512,256]{1,0:T(8,128)S(1)}, f32[512,256]{1,0:T(8,128)S(1)}, u32[]{:S(2)}, u32[]{:S(2)}) collective-permute-start(f32[512,256]{1,0:T(8,128)S(1)} %own_other_kernel.1), channel_id=1, source_target_pairs={{0,1},{1,0},{2,3},{3,2},{4,5},{5,4},{6,7},{7,6},{8,9},{9,8},{10,11... | collective-permute-start | bytes 1572872 | tf_op jit(solution)/shard_map/ppermute | solution.py:248
  81.0 4.8 %collective-permute-start.18 = (f32[256,256]{1,0:T(8,128)S(1)}, f32[256,256]{1,0:T(8,128)S(1)}, u32[]{:S(2)}, u32[]{:S(2)}) collective-permute-start(f32[256,256]{1,0:T(8,128)S(1)} %constant_dynamic-update-slice_fusion.mine), channel_id=1, source_target_pairs={{0,2},{2,0},{4,6},{6,4},{8,10},{10,8},{12,14},{14,12},{16,18},{18,... | collective-permute-start | bytes 786440 | tf_op jit(solution)/shard_map/ppermute | solution.py:248
  81.1 15.2 %collective-permute-start.13 = (bf16[512,256]{1,0:T(8,128)(2,1)S(1)}, bf16[512,256]{1,0:T(8,128)(2,1)S(1)}, u32[]{:S(2)}, u32[]{:S(2)}) collective-permute-start(bf16[512,256]{1,0:T(8,128)(2,1)S(1)} %add_convert_fusion), channel_id=1, source_target_pairs={{0,16},{2,18},{4,20},{6,22},{8,24},{10,26},{12,28},{14,30},{16,0},... | collective-permute-start | bytes 786440 | tf_op jit(solution)/shard_map/ppermute | solution.py:248
